TPU v7x, 256 devices: a whole 4x4x8 slice. The times are simulated.
256 devices in a mesh: expert: 64 (over z, x, core), zero: 4 (over y).
Axes of the slice: x: 4, y: 4, z: 8, core: 2. Of those that a mesh axis runs over, the one named last changes fastest.
Arguments:
- cotangent: bfloat16 [32768, 2048], P(('expert', 'zero')), may hold values from -0.59765625 to 0.59765625
- gates: float32 [32768, 8], P(('expert', 'zero')), may hold values from 0.05 to 1
- expert_ids: int32 [32768, 8], P(('expert', 'zero')), may hold values from 0 to 127, all different within a row; in each aligned block of 128 rows (0 to 127, 128 to 255, ...) at most 16 rows name the same one
- hidden: bfloat16 [128, 4096, 768], P('expert', 'zero'), may hold values from -6 to 6
- momentum_left: float32 [128, 768, 32], P('expert', 'zero'), may hold values from -6 to 6
- momentum_right: float32 [128, 32, 2048], P('expert', None, 'zero'), may hold values from -1 to 1
- sketch: float32 [128, 2048, 32], P('expert'), may hold values from -6 to 6
Outputs:
- basis: float32 [128, 768, 32], P('expert', 'zero')
- coefficients: float32 [128, 32, 2048], P('expert', None, 'zero')
Inputs may be any that keep to these rules, and one draw needn't show every extreme that they name: `expert_ids`: among the 128 tokens of one device (an aligned block of rows) no expert is named more than 16 times, a bound that some block reaches; the 8 experts of a token differ.
All inputs are finite; a program needn't handle non-finite values.
Results may differ from a plain program's by a relative error of at most 0.0035.
Values may be sent and summed in bfloat16 or wider, within the bound.
No kernel may reach another device: no remote copies, remote signals or barrier semaphores. Data moves between devices by JAX's collectives and lax.ppermute only.
A program may use at most 128 MiB of HBM per device.

v0:
```python
import functools

import jax
import jax.numpy as jnp
from jax import lax
from jax.experimental import pallas as pl
from jax.experimental.pallas import tpu as pltpu
from jax.sharding import PartitionSpec as P

NX, NC = 4, 2
CAP = 16
MOMENTUM_DECAY = 0.9

WIDE, NARROW = 20 << 20, 12 << 20

BF, F32 = jnp.bfloat16, jnp.float32
HIGHEST = lax.Precision.HIGHEST
VMEM = pl.BlockSpec(memory_space=pltpu.VMEM)
ANY = pl.BlockSpec(memory_space=pl.ANY)
HBM = pl.BlockSpec(memory_space=pltpu.HBM)
SMEM = pl.BlockSpec(memory_space=pltpu.SMEM)
NT = (((1,), (1,)), ((), ()))
NN = (((1,), (0,)), ((), ()))


def dot(a, b, dims=NN, precision=None):
    return lax.dot_general(a, b, dims, precision=precision, preferred_element_type=F32)


def split(v):
    hi = v.astype(BF)
    return hi, (v - hi.astype(F32)).astype(BF)


def stacked(v):
    return jnp.concatenate(split(v), axis=0)


def folded(v):
    half = v.shape[0] // 2
    return v[:half] + v[half:]


def call(kernel, outs, args, specs=None, scratch=(), limit=WIDE, flops=0, spaces=None):
    return pl.pallas_call(
        kernel,
        out_shape=outs,
        in_specs=specs or [VMEM] * len(args),
        out_specs=spaces or jax.tree.map(lambda _: VMEM, outs),
        scratch_shapes=list(scratch),
        compiler_params=pltpu.CompilerParams(vmem_limit_bytes=limit),
        cost_estimate=pl.CostEstimate(flops=flops, bytes_accessed=flops // 500, transcendentals=0),
    )(*args)


def after(values, *needs):
    def kernel(*refs):
        for n in range(len(values)):
            refs[len(values) + len(needs) + n][...] = refs[n][...]

    outs = [jax.ShapeDtypeStruct(v.shape, v.dtype) for v in values]
    return call(kernel, outs, (*values, *needs), limit=NARROW)


def pack_kernel(cot_ref, gates_ref, ids_ref, out_ref, g_scr, i_scr, e_scr, sems):
    tokens, width = cot_ref.shape
    main = pltpu.make_async_copy(cot_ref, out_ref.at[:, 0:width], sems.at[0])
    first = pltpu.make_async_copy(gates_ref, g_scr, sems.at[1])
    second = pltpu.make_async_copy(ids_ref, i_scr, sems.at[2])
    main.start()
    first.start()
    second.start()
    first.wait()
    second.wait()
    g = g_scr[...]
    hi = g.astype(BF).astype(F32)
    mid = (g - hi).astype(BF).astype(F32)
    low = g - hi - mid
    ids = i_scr[...].astype(F32)
    rest = jnp.zeros((tokens - 4 * g.shape[0], tokens), F32)
    e_scr[...] = jnp.concatenate([ids, hi, mid, low, rest], axis=0).astype(BF)
    last = pltpu.make_async_copy(e_scr, out_ref.at[:, width : width + tokens], sems.at[3])
    last.start()
    main.wait()
    last.wait()


def sketch_kernel(st_ref, out_ref):
    hi, low = split(st_ref[...])
    out_ref[0] = hi
    out_ref[1] = low


def momentum_kernel(meta_ref, st_ref, r_ref, *refs):
    lefts, (full_ref, mom_ref, rows) = refs[:-3], refs[-3:]
    ny, y = len(lefts), meta_ref[3]
    for d in range(ny):
        rows[lax.rem(y - d + ny, ny)] = lefts[d][...]
    local = lefts[0].shape[-1]
    cols = r_ref.shape[-1]
    for i in range(r_ref.shape[0]):
        part = st_ref[i, :, pl.ds(pl.multiple_of(y * cols, 128), cols)]
        inner = dot(part, r_ref[i], NT, HIGHEST) * MOMENTUM_DECAY
        for a in range(ny):
            block = rows[a, i]
            full_ref[i, :, a * local : (a + 1) * local] = block
            mom_ref[i, :, a * local : (a + 1) * local] = dot(inner, block, NN, HIGHEST)


def forward_kernel(meta_ref, right_ref, left_ref, out_ref, token_ref):
    out_ref[...] = jnp.where(meta_ref[2] == 0, right_ref[...], left_ref[...])
    token_ref[...] = jnp.zeros_like(token_ref)


def one_hot(place, line):
    return jnp.where(place == line.astype(BF), jnp.ones((), BF), jnp.zeros((), BF))


def project_kernel(places, nz, ng, carried, whole, meta_ref, *refs):
    nb = len(places)
    pieces, refs = refs[:nb], refs[nb:]
    fed = 1 if whole else ng
    sketches, earlier, refs = refs[:fed], refs[fed : fed + carried], refs[fed + carried :]
    outs, (pos_ref, y_scr) = refs[:-2], refs[-2:]
    all_s = sketches[0] if whole else outs[-1]
    outs = outs if whole else outs[:-1]
    _, rank, slots = outs[0].shape
    count = len(outs) * outs[0].shape[0]
    local = count // ng
    rows = count * rank
    gates = nb * count
    tokens = pieces[0].shape[0]
    width = all_s.shape[1]
    if not whole:
        per = rows // ng
        for d in range(ng):
            for k in range(2):
                at = k * rows + d * per
                all_s[at : at + per] = sketches[d][k]
    which = lax.broadcasted_iota(jnp.int32, (count, tokens), 0)
    before = (
        lax.broadcasted_iota(jnp.int32, (tokens, tokens), 0)
        < lax.broadcasted_iota(jnp.int32, (tokens, tokens), 1)
    ).astype(F32).astype(BF)
    z, x, c = meta_ref[0], meta_ref[1], meta_ref[2]
    experts = [
        (((z * NX + lax.rem(x + q // local, ng)) * NC + c) * local + q % local).astype(F32)
        for q in range(count)
    ]
    named, weights = [], []
    for b in range(nb):
        extra = pieces[b][0:32, width:].astype(F32)
        ids = extra[0:8]
        g = extra[8:16] + extra[16:24] + extra[24:32]
        member = jnp.zeros((count, tokens), F32)
        gate = jnp.zeros((count, tokens), F32)
        for q in range(count):
            hit = ids == experts[q]
            m = jnp.sum(jnp.where(hit, 1.0, 0.0), axis=0, keepdims=True)
            w = jnp.sum(jnp.where(hit, g, 0.0), axis=0, keepdims=True)
            member = jnp.where(which == q, m, member)
            gate = jnp.where(which == q, w, gate)
        named.append(member)
        weights.append(gate)
    member = jnp.concatenate(named, axis=0)
    slot = dot(member.astype(BF), before)
    for b, (k, same) in enumerate(places):
        here = slice(b * count, (b + 1) * count)
        source = c if same else NC - 1 - c
        base = ((lax.rem(z - (1 - 2 * c) * k + nz, nz) * NC + source) * CAP).astype(F32)
        pos_ref[here] = jnp.where(member[here] > 0.5, slot[here] + base, -1.0)
        pos_ref[gates + b * count : gates + (b + 1) * count] = weights[b]
    for b in range(0, nb, 2):
        pair = slice(b * tokens, (b + 2) * tokens)
        x2 = jnp.concatenate([ref[:, :width] for ref in pieces[b : b + 2]], axis=0)
        y_scr[:, pair] = folded(dot(all_s[...], x2, NT))
    place = lax.broadcasted_iota(jnp.int32, (slots, nb * tokens), 0).astype(F32).astype(BF)
    for q in range(count):
        line = lambda at: jnp.concatenate(
            [pos_ref[at + b * count + q : at + b * count + q + 1] for b in range(nb)], axis=1
        )
        v = y_scr[q * rank : (q + 1) * rank] * line(gates)
        r = folded(dot(stacked(v), one_hot(place, line(0)), NT))
        per = count // len(outs)
        outs[q // per][q % per] = r + earlier[0][q] if carried else r


def sum_kernel(nd, meta_ref, *refs):
    parts, (h_ref, mom_ref, out_ref) = refs[:nd], refs[nd:]
    for i in range(out_ref.shape[0]):
        total = mom_ref[i]
        for d in range(nd):
            h = h_ref[i, :, lax.rem(meta_ref[1] - d + nd, nd)]
            h = h.reshape(-1, h.shape[-1])
            total = total + folded(dot(stacked(parts[d][i]), h))
        out_ref[i] = total


def basis_kernel(ny, nd, meta_ref, *refs):
    parts, (h_ref, basis_ref), zs = refs[:ny], refs[ny : ny + 2], refs[ny + 2 :]
    count, rank, ff = basis_ref.shape
    row = lax.broadcasted_iota(jnp.int32, (rank, 2 * rank), 0)
    lane = lax.broadcasted_iota(jnp.int32, (rank, 2 * rank), 1)
    sk, work = [], []
    for i in range(count):
        s = parts[0][i]
        for d in range(1, ny):
            s = s + parts[d][i]
        sk.append(s)
        both = jnp.concatenate([jnp.zeros_like(s), s], axis=0)
        a = dot(s, both, NT, HIGHEST) / ff
        work.append(jnp.where(lane == row, 1.0, a))
    for j in range(rank):
        for i in range(count):
            a = work[i]
            pivot = a[j : j + 1, rank + j : rank + j + 1]
            factor = a[:, rank + j : rank + j + 1] / pivot
            work[i] = a - jnp.where(row > j, factor, 0.0) * a[j : j + 1]
    for i in range(count):
        diag = jnp.sum(jnp.where(lane == row + rank, work[i], 0.0), axis=1, keepdims=True)
        inverse = (work[i] / jnp.sqrt(diag))[:, :rank]
        basis = dot(inverse, sk[i], NN, HIGHEST)
        basis_ref[i] = basis
        b = stacked(basis / ff)
        for d in range(nd):
            h = h_ref[i, :, lax.rem(meta_ref[1] + d, nd)]
            h = h.reshape(-1, h.shape[-1])
            zs[d][i] = folded(dot(b, h, NT))


def own_kernel(meta_ref, basis_ref, left_ref, r_ref, out_ref, mom_ref):
    count, rank, ff = basis_ref.shape
    local = out_ref.shape[-1]
    y = meta_ref[3]
    for i in range(count):
        b = basis_ref[i]
        own = b[:, :local]
        for a in range(1, ff // local):
            own = jnp.where(y == a, b[:, a * local : (a + 1) * local], own)
        out_ref[i] = own
        inner = dot(b, left_ref[i], NT, HIGHEST) * (MOMENTUM_DECAY / ff)
        mom_ref[i] = dot(inner, r_ref[i], NN, HIGHEST)


def coefficient_kernel(counts, nd, unread, *refs):
    nb = sum(counts)
    pieces, refs = refs[:nb], refs[nb:]
    zs, refs = refs[:nd], refs[nd:]
    poss, refs = refs[: len(counts)], refs[len(counts) + unread :]
    outs, w_scr = refs[:nd], refs[nd]
    local, rank, slots = zs[0].shape
    count = nd * local
    tokens = poss[0].shape[1]
    rows = count * rank
    width = outs[0].shape[-1]
    place = lax.broadcasted_iota(jnp.int32, (slots, nb * tokens), 0).astype(F32).astype(BF)
    for q in range(count):
        line = lambda gate: jnp.concatenate(
            [
                r[(gate * n + b) * count + q : (gate * n + b) * count + q + 1]
                for r, n in zip(poss, counts)
                for b in range(n)
            ],
            axis=1,
        )
        w = folded(dot(stacked(zs[q // local][q % local]), one_hot(place, line(0)))) * line(1)
        hi, low = split(w)
        w_scr[q * rank : (q + 1) * rank] = hi
        w_scr[rows + q * rank : rows + (q + 1) * rank] = low
    step = 256

    @pl.loop(0, width // step)
    def _(n):
        cols = pl.ds(pl.multiple_of(n * step, step), step)
        x = jnp.concatenate([ref[:, cols] for ref in pieces], axis=0)
        total = folded(dot(w_scr[...], x))
        for q in range(count):
            ref = outs[q // local]
            ref[q % local, :, cols] = total[q * rank : (q + 1) * rank].astype(ref.dtype)


def body(cotangent, gates, expert_ids, hidden, momentum_left, momentum_right, sketch):
    nx, nc = NX, NC
    ne, ny = lax.axis_size("expert"), lax.axis_size("zero")
    nz = ne // (nx * nc)
    local, _, ff = hidden.shape
    tokens, width = cotangent.shape
    rank = sketch.shape[2]
    me, y = lax.axis_index("expert"), lax.axis_index("zero")
    z, x, c = me // (nx * nc), me // nc % nx, me % nc
    meta = jnp.stack([z, x, c, y]).astype(jnp.int32)

    def shift(v, dz=0, dx=0, dc=0):
        pairs = []
        for e in range(ne):
            a, b, k = e // (nx * nc), e // nc % nx, e % nc
            to = ((a + dz) % nz * nx + (b + dx) % nx) * nc + (k + dc) % nc
            pairs.append((e, to))
        return lax.ppermute(v, "expert", pairs)

    def shift_y(v, dy):
        return lax.ppermute(v, "zero", [(a, (a + dy) % ny) for a in range(ny)])

    def shaped(s, t=F32):
        return jax.ShapeDtypeStruct(s, t)

    mine = call(
        pack_kernel,
        shaped((tokens, width + tokens), BF),
        (cotangent, gates.T, expert_ids.T),
        specs=[ANY] * 3,
        scratch=[
            pltpu.VMEM((gates.shape[1], tokens), F32),
            pltpu.VMEM((gates.shape[1], tokens), jnp.int32),
            pltpu.VMEM((tokens, tokens), BF),
            pltpu.SemaphoreType.DMA((4,)),
        ],
    )

    st = jnp.swapaxes(sketch, 1, 2)
    rows = local * rank
    two = call(sketch_kernel, shaped((2, rows, width), BF), (st.reshape(rows, width),))
    lt = jnp.swapaxes(momentum_left, 1, 2)
    slots = nz * nc * CAP
    count = nx * local
    half = nz // 2

    def along(v, axis="z"):
        pairs = []
        for e in range(ne):
            a, b, k = e // (nx * nc), e // nc % nx, e % nc
            if axis == "z":
                pairs.append((e, ((a + 1 - 2 * k) % nz * nx + b) * nc + k))
            else:
                pairs.append((e, (a * nx + (b - 1 + 2 * k) % nx) * nc + k))
        return lax.ppermute(v, "expert", pairs)

    def swap(v):
        return shift(v, dc=1)

    def project(named, sketches, earlier, parts=1):
        places, blocks = zip(*named)
        nb = len(blocks)
        whole = len(sketches) == 1
        outs = [shaped((count // parts, rank, slots))] * parts
        products = call(
            functools.partial(project_kernel, places, nz, nx, len(earlier), whole),
            outs
            + ([] if whole else [shaped((2 * count * rank, width), BF)])
            + [shaped((2 * nb * count, tokens))],
            (meta, *blocks, *sketches, *earlier),
            specs=[SMEM] + [VMEM] * (nb + len(sketches) + len(earlier)),
            scratch=[pltpu.VMEM((count * rank, nb * tokens), F32)],
            flops=2 * 2 * count * rank * nb * tokens * width,
        )
        return nb, blocks, products[:parts], products[-1], products[-2]

    def ring(k, p, q):
        return [((k, 1), p), ((k, 0), q), ((-k, 0), swap(p)), ((-k, 1), swap(q))]

    p = along(mine)
    sibling = swap(mine)
    q = along(sibling)
    near = [shift(two, dx=-1), shift(two, dx=1)]
    first = [((0, 1), mine), ((0, 0), sibling)] + ring(1, p, q)
    farther, token = call(
        forward_kernel,
        [shaped((2, rows, width), BF), shaped((8, 128))],
        (meta, *near),
        specs=[SMEM, VMEM, VMEM],
    )
    far = along(farther, "x")
    lefts = [lt] + [shift_y(lt, d) for d in range(1, ny)]
    left_full, mom = call(
        momentum_kernel,
        [shaped((local, rank, ff))] * 2,
        (meta, st, momentum_right, *lefts),
        specs=[SMEM] + [VMEM] * (2 + ny),
        scratch=[pltpu.VMEM((ny, local, rank, ff // ny), F32)],
    )
    p, q = after([along(p), along(q)], token)
    second = ring(2, p, q)
    a = project(first, [two, near[0], far, near[1]], [])
    all_s = [a[4]]
    p, q = after([along(p), along(q)], a[3], mom)
    third = ring(3, p, q)
    b = project(second, all_s, a[2])
    [p] = after([along(p)], b[3])
    fourth = [((4, 1), p), ((4, 0), swap(p))]
    e = project(third, all_s, b[2])
    f = project(fourth, all_s, e[2], nx)
    steps = [a, b, e, f]
    counts = [v[0] for v in steps]
    pieces = [block for v in steps for block in v[1]]
    products = [f[2][0]] + [shift(f[2][d], dx=d) for d in range(1, nx)]

    h = hidden.reshape(local, nz, nx, nc * CAP, ff)
    part = call(
        functools.partial(sum_kernel, nx),
        shaped((local, rank, ff)),
        (meta, *products, h, mom),
        specs=[SMEM] + [VMEM] * (nx + 2),
        limit=NARROW,
    )
    parts = [part] + [shift_y(part, d) for d in range(1, ny)]
    basis, *coded = call(
        functools.partial(basis_kernel, ny, nx),
        [shaped((local, rank, ff))] + [shaped((local, rank, slots))] * nx,
        (meta, *parts, h),
        specs=[SMEM] + [VMEM] * (ny + 1),
        limit=NARROW,
    )
    coded = [coded[0]] + [shift(coded[d], dx=d) for d in range(1, nx)]
    coded = [coded[-d % nx] for d in range(nx)]
    own_basis, own_mom = call(
        own_kernel,
        [shaped((local, rank, ff // ny)), shaped(momentum_right.shape)],
        (meta, basis, left_full, momentum_right),
        specs=[SMEM] + [VMEM] * 3,
        limit=NARROW,
    )
    coeff = call(
        functools.partial(coefficient_kernel, counts, nx, 1),
        [shaped((local, rank, width))] + [shaped((local, rank, width), BF)] * (nx - 1),
        (*pieces, *coded, *[v[3] for v in steps], own_mom),
        specs=[VMEM] * (len(pieces) + nx + len(steps) + 1),
        limit=WIDE,
        scratch=[
            pltpu.VMEM((2 * count * rank, sum(counts) * tokens), BF),
        ],
        flops=2 * 2 * count * rank * sum(counts) * tokens * width,
    )
    total = coeff[0]
    for d in range(1, nx):
        total = total + shift(coeff[d], dx=d).astype(F32)
    cols = width // ny

    def columns(d):
        return lax.dynamic_slice_in_dim(total, lax.rem(y + d, ny) * cols, cols, axis=2)

    out = columns(0) + own_mom
    for d in range(1, ny):
        out = out + shift_y(columns(d), d)
    return jnp.swapaxes(own_basis, 1, 2), out


def solution(mesh):
    return jax.shard_map(
        body,
        mesh=mesh,
        in_specs=(
            P(("expert", "zero"), None),
            P(("expert", "zero"), None),
            P(("expert", "zero"), None),
            P("expert", "zero", None),
            P("expert", "zero", None),
            P("expert", None, "zero"),
            P("expert", None, None),
        ),
        out_specs=(P("expert", "zero", None), P("expert", None, "zero")),
        check_vma=False,
    )
```

profile of v0, /device:TPU:6, one launch (start us, length us, event | category | flops | bytes accessed | tf_op | source)
XLA Modules:
  0.0 139.3 jit_solution(14121436285129211619)
XLA Ops:
  9.3 2.4 %collective-permute-start.6 = (bf16[2,64,2048]{2,1,0:T(8,128)(2,1)S(1)}, bf16[2,64,2048]{2,1,0:T(8,128)(2,1)}, u32[]{:S(2)}, u32[]{:S(2)}) collective-permute-start(bf16[2,64,2048]{2,1,0:T(8,128)(2,1)S(1)} %shard_map.87.refs_6_), channel_id=1, source_target_pairs={{0,8},{4,12},{8,16},{12,20},{16,24},{20,28},{24,0},{28,4},{32,40},... | collective-permute-start | bytes 1572872 | tf_op jit(solution)/shard_map/ppermute | solution.py:299
  11.7 5.2 %collective-permute-done.refs_2_ = bf16[128,2176]{1,0:T(8,128)(2,1)} collective-permute-done((bf16[128,2176]{1,0:T(8,128)(2,1)S(1)}, bf16[128,2176]{1,0:T(8,128)(2,1)}, u32[]{:S(2)}, u32[]{:S(2)}) %collective-permute-start) | collective-permute-done | bytes 557088 | tf_op jit(solution)/shard_map/ppermute | solution.py:336
  16.9 6.0 %collective-permute-done.3.refs_3_ = bf16[128,2176]{1,0:T(8,128)(2,1)} collective-permute-done((bf16[128,2176]{1,0:T(8,128)(2,1)S(1)}, bf16[128,2176]{1,0:T(8,128)(2,1)}, u32[]{:S(2)}, u32[]{:S(2)}) %collective-permute-start.3) | collective-permute-done | bytes 557088 | tf_op jit(solution)/shard_map/ppermute | solution.py:336
  24.4 2.1 %collective-permute-start.9 = (bf16[128,2176]{1,0:T(8,128)(2,1)}, bf16[128,2176]{1,0:T(8,128)(2,1)S(1)}, u32[]{:S(2)}, u32[]{:S(2)}) collective-permute-start(bf16[128,2176]{1,0:T(8,128)(2,1)} %collective-permute-done.refs_2_), channel_id=1, source_target_pairs={{0,4},{4,0},{8,12},{12,8},{16,20},{20,16},{24,28},{28,24},{32,36},... | collective-permute-start | bytes 1671176 | tf_op jit(solution)/shard_map/ppermute | solution.py:299
  29.4 2.5 %collective-permute-start.13 = (f32[2,32,192]{2,1,0:T(8,128)S(1)}, f32[2,32,192]{2,1,0:T(8,128)S(1)}, u32[]{:S(2)}, u32[]{:S(2)}) collective-permute-start(f32[2,32,192]{2,1,0:T(8,128)S(1)} %bitcast.17), channel_id=1, source_target_pairs={{0,2},{1,3},{2,0},{3,1},{4,6},{5,7},{6,4},{7,5},{8,10},{9,11},{10,... | collective-permute-start | bytes 147464 | tf_op jit(solution)/shard_map/ppermute | solution.py:302
  31.9 2.8 %collective-permute-done.4.refs_1_ = bf16[128,2176]{1,0:T(8,128)(2,1)S(1)} collective-permute-done((bf16[128,2176]{1,0:T(8,128)(2,1)}, bf16[128,2176]{1,0:T(8,128)(2,1)S(1)}, u32[]{:S(2)}, u32[]{:S(2)}) %collective-permute-start.4) | collective-permute-done | bytes 557088 | tf_op jit(solution)/shard_map/ppermute | solution.py:336
  34.7 3.0 %collective-permute-start.14 = (f32[2,32,192]{2,1,0:T(8,128)S(1)}, f32[2,32,192]{2,1,0:T(8,128)S(1)}, u32[]{:S(2)}, u32[]{:S(2)}) collective-permute-start(f32[2,32,192]{2,1,0:T(8,128)S(1)} %bitcast.18), channel_id=1, source_target_pairs={{0,3},{1,0},{2,1},{3,2},{4,7},{5,4},{6,5},{7,6},{8,11},{9,8},{10,9... | collective-permute-start | bytes 147464 | tf_op jit(solution)/shard_map/ppermute | solution.py:302
  41.2 2.1 %collective-permute-start.16 = (bf16[128,2176]{1,0:T(8,128)(2,1)S(1)}, bf16[128,2176]{1,0:T(8,128)(2,1)S(1)}, u32[]{:S(2)}, u32[]{:S(2)}) collective-permute-start(bf16[128,2176]{1,0:T(8,128)(2,1)S(1)} %get-tuple-element.34.refs_0_.refs_6_), channel_id=1, source_target_pairs={{0,4},{4,0},{8,12},{12,8},{16,20},{20,16},{24,28},{28,24},{32,36},... | collective-permute-start | bytes 1671176 | tf_op jit(solution)/shard_map/ppermute | solution.py:299
  44.6 5.1 %shard_map.90 = (f32[8,32,256]{2,1,0:T(8,128)S(1)}, bf16[512,2048]{1,0:T(8,128)(2,1)S(1)}, f32[96,128]{1,0:T(8,128)S(1)}) custom-call(s32[4]{0:T(128)S(1)} %pad_add_fusion.meta_ref, bf16[128,2176]{1,0:T(8,128)(2,1)S(1)} %shard_map.86.refs_0_, bf16[128,2176]{1,0:T(8,128)(2,1)S(1)} %copy-done.9, bf16[128,2176]{1,0:T(8,128)(2,1)} %collective-permute-done.refs_2_, ...), custom_call_target="tpu_custom_call" | custom-call | flops 1610612736 | bytes 3221225 | tf_op jit(solution)/shard_map/pallas_call | solution.py:45
  49.8 4.8 %collective-permute-done.8.refs_1_ = bf16[128,2176]{1,0:T(8,128)(2,1)S(1)} collective-permute-done((bf16[128,2176]{1,0:T(8,128)(2,1)S(1)}, bf16[128,2176]{1,0:T(8,128)(2,1)S(1)}, u32[]{:S(2)}, u32[]{:S(2)}) %collective-permute-start.8) | collective-permute-done | bytes 557088 | tf_op jit(solution)/shard_map/ppermute | solution.py:336
  55.8 2.4 %shard_map.93 = (f32[8,32,256]{2,1,0:T(8,128)S(1)}, f32[64,128]{1,0:T(8,128)S(1)}) custom-call(s32[4]{0:T(128)S(1)} %pad_add_fusion.meta_ref, bf16[128,2176]{1,0:T(8,128)(2,1)S(1)} %get-tuple-element.34.refs_0_.refs_6_, bf16[128,2176]{1,0:T(8,128)(2,1)S(1)} %get-tuple-element.35.refs_1_.refs_7_, ...), custom_call_target="tpu_custom_call" | custom-call | flops 1073741824 | bytes 2147483 | tf_op jit(solution)/shard_map/pallas_call | solution.py:45
  58.3 7.2 %collective-permute-done.15.refs_0_ = bf16[128,2176]{1,0:T(8,128)(2,1)S(1)} collective-permute-done((bf16[128,2176]{1,0:T(8,128)(2,1)S(1)}, bf16[128,2176]{1,0:T(8,128)(2,1)S(1)}, u32[]{:S(2)}, u32[]{:S(2)}) %collective-permute-start.15) | collective-permute-done | bytes 557088 | tf_op jit(solution)/shard_map/ppermute | solution.py:336
  65.7 2.4 %shard_map.95 = (f32[8,32,256]{2,1,0:T(8,128)S(1)}, f32[64,128]{1,0:T(8,128)S(1)}) custom-call(s32[4]{0:T(128)S(1)} %pad_add_fusion.meta_ref, bf16[128,2176]{1,0:T(8,128)(2,1)S(1)} %get-tuple-element.39.refs_0_.refs_10_, bf16[128,2176]{1,0:T(8,128)(2,1)S(1)} %get-tuple-element.43.refs_1_.refs_11_, ...), custom_call_target="tpu_custom_call" | custom-call | flops 1073741824 | bytes 2147483 | tf_op jit(solution)/shard_map/pallas_call | solution.py:45
  70.7 2.4 %collective-permute-start.22 = (f32[2,32,256]{2,1,0:T(8,128)S(1)}, f32[2,32,256]{2,1,0:T(8,128)S(1)}, u32[]{:S(2)}, u32[]{:S(2)}) collective-permute-start(f32[2,32,256]{2,1,0:T(8,128)S(1)} %get-tuple-element.48), channel_id=1, source_target_pairs={{0,16},{4,20},{8,24},{12,28},{16,0},{20,4},{24,8},{28,12},{32,48},... | collective-permute-start | bytes 196616 | tf_op jit(solution)/shard_map/ppermute | solution.py:299
  76.5 2.1 %collective-permute-done.23.refs_3_ = f32[2,32,256]{2,1,0:T(8,128)S(1)} collective-permute-done((f32[2,32,256]{2,1,0:T(8,128)S(1)}, f32[2,32,256]{2,1,0:T(8,128)S(1)}, u32[]{:S(2)}, u32[]{:S(2)}) %collective-permute-start.23) | collective-permute-done | bytes 65568 | tf_op jit(solution)/shard_map/ppermute | solution.py:299
  79.9 2.2 %collective-permute-start.25 = (f32[2,32,768]{2,1,0:T(8,128)S(1)}, f32[2,32,768]{2,1,0:T(8,128)S(1)}, u32[]{:S(2)}, u32[]{:S(2)}) collective-permute-start(f32[2,32,768]{2,1,0:T(8,128)S(1)} %shard_map.97.refs_0_), channel_id=1, source_target_pairs={{0,2},{1,3},{2,0},{3,1},{4,6},{5,7},{6,4},{7,5},{8,10},{9,11},{10,... | collective-permute-start | bytes 589832 | tf_op jit(solution)/shard_map/ppermute | solution.py:302
  83.3 7.6 %collective-permute-done.24.refs_1_ = f32[2,32,768]{2,1,0:T(8,128)S(1)} collective-permute-done((f32[2,32,768]{2,1,0:T(8,128)S(1)}, f32[2,32,768]{2,1,0:T(8,128)S(1)}, u32[]{:S(2)}, u32[]{:S(2)}) %collective-permute-start.24) | collective-permute-done | bytes 196640 | tf_op jit(solution)/shard_map/ppermute | solution.py:302
  91.5 5.3 %shard_map.98 = (f32[2,32,768]{2,1,0:T(8,128)S(1)}, f32[2,32,256]{2,1,0:T(8,128)S(1)}, f32[2,32,256]{2,1,0:T(8,128)S(1)}, f32[2,32,256]{2,1,0:T(8,128)S(1)}, f32[2,32,256]{2,1,0:T(8,128)S(1)}) custom-call(s32[4]{0:T(128)S(1)} %pad_add_fusion.meta_ref, f32[2,32,768]{2,1,0:T(8,128)S(1)} %shard_map.97.refs_0_, ...), custom_call_target="tpu_custom_call" | custom-call | tf_op jit(solution)/shard_map/pallas_call | solution.py:45
  103.9 8.6 %shard_map.100 = (f32[2,32,2048]{2,1,0:T(8,128)S(1)}, bf16[2,32,2048]{2,1,0:T(8,128)(2,1)S(1)}, bf16[2,32,2048]{2,1,0:T(8,128)(2,1)S(1)}, bf16[2,32,2048]{2,1,0:T(8,128)(2,1)S(1)}) custom-call(bf16[128,2176]{1,0:T(8,128)(2,1)S(1)} %shard_map.86.refs_0_, bf16[128,2176]{1,0:T(8,128)(2,1)S(1)} %copy-done.10, bf16[128,2176]{1,0:T(8,128)(2,1)} %collective-permute-done.refs_2_, ...), custom_call_target="tpu_custom_call" | custom-call | flops 4294967296 | bytes 8589934 | tf_op jit(solution)/shard_map/pallas_call | solution.py:45
  112.5 2.8 %collective-permute-start.30 = (bf16[2,32,2048]{2,1,0:T(8,128)(2,1)S(1)}, bf16[2,32,2048]{2,1,0:T(8,128)(2,1)S(1)}, u32[]{:S(2)}, u32[]{:S(2)}) collective-permute-start(bf16[2,32,2048]{2,1,0:T(8,128)(2,1)S(1)} %get-tuple-element.61), channel_id=1, source_target_pairs={{0,8},{4,12},{8,16},{12,20},{16,24},{20,28},{24,0},{28,4},{32,40},... | collective-permute-start | bytes 786440 | tf_op jit(solution)/shard_map/ppermute | solution.py:299
  116.2 7.5 %collective-permute-done.30 = bf16[2,32,2048]{2,1,0:T(8,128)(2,1)S(1)} collective-permute-done((bf16[2,32,2048]{2,1,0:T(8,128)(2,1)S(1)}, bf16[2,32,2048]{2,1,0:T(8,128)(2,1)S(1)}, u32[]{:S(2)}, u32[]{:S(2)}) %collective-permute-start.30) | collective-permute-done | bytes 262176 | tf_op jit(solution)/shard_map/ppermute | solution.py:299
  124.7 2.7 %collective-permute-done.32 = bf16[2,32,2048]{2,1,0:T(8,128)(2,1)S(1)} collective-permute-done((bf16[2,32,2048]{2,1,0:T(8,128)(2,1)S(1)}, bf16[2,32,2048]{2,1,0:T(8,128)(2,1)S(1)}, u32[]{:S(2)}, u32[]{:S(2)}) %collective-permute-start.32) | collective-permute-done | bytes 262176 | tf_op jit(solution)/shard_map/ppermute | solution.py:299
  129.4 3.4 %collective-permute-start.34 = (f32[2,32,512]{2,1,0:T(8,128)S(1)}, f32[2,32,512]{2,1,0:T(8,128)S(1)}, u32[]{:S(2)}, u32[]{:S(2)}) collective-permute-start(f32[2,32,512]{2,1,0:T(8,128)S(1)} %get-tuple-element.66), channel_id=1, source_target_pairs={{0,2},{1,3},{2,0},{3,1},{4,6},{5,7},{6,4},{7,5},{8,10},{9,11},{10,... | collective-permute-start | bytes 393224 | tf_op jit(solution)/shard_map/ppermute | solution.py:302
  134.8 3.8 %collective-permute-done.34 = f32[2,32,512]{2,1,0:T(8,128)S(1)} collective-permute-done((f32[2,32,512]{2,1,0:T(8,128)S(1)}, f32[2,32,512]{2,1,0:T(8,128)S(1)}, u32[]{:S(2)}, u32[]{:S(2)}) %collective-permute-start.34) | collective-permute-done | bytes 131104 | tf_op jit(solution)/shard_map/ppermute | solution.py:302
  (89 shorter events, 42.1 us)
Async XLA Ops:
  3.3 13.6 %collective-permute-start = (bf16[128,2176]{1,0:T(8,128)(2,1)S(1)}, bf16[128,2176]{1,0:T(8,128)(2,1)}, u32[]{:S(2)}, u32[]{:S(2)}) collective-permute-start(bf16[128,2176]{1,0:T(8,128)(2,1)S(1)} %shard_map.86.refs_0_), channel_id=1, source_target_pairs={{0,32},{4,228},{8,40},{12,236},{16,48},{20,244},{24,56},{28,252},{... | collective-permute-start | bytes 1671176 | tf_op jit(solution)/shard_map/ppermute | solution.py:336
  5.3 17.5 %collective-permute-start.3 = (bf16[128,2176]{1,0:T(8,128)(2,1)S(1)}, bf16[128,2176]{1,0:T(8,128)(2,1)}, u32[]{:S(2)}, u32[]{:S(2)}) collective-permute-start(bf16[128,2176]{1,0:T(8,128)(2,1)S(1)} %collective-permute-done.2.refs_1_), channel_id=1, source_target_pairs={{0,32},{4,228},{8,40},{12,236},{16,48},{20,244},{24,56},{28,252},{... | collective-permute-start | bytes 1671176 | tf_op jit(solution)/shard_map/ppermute | solution.py:336
  8.4 16.0 %collective-permute-start.5 = (bf16[2,64,2048]{2,1,0:T(8,128)(2,1)S(1)}, bf16[2,64,2048]{2,1,0:T(8,128)(2,1)S(1)}, u32[]{:S(2)}, u32[]{:S(2)}) collective-permute-start(bf16[2,64,2048]{2,1,0:T(8,128)(2,1)S(1)} %shard_map.87.refs_6_), channel_id=1, source_target_pairs={{0,24},{4,28},{8,0},{12,4},{16,8},{20,12},{24,16},{28,20},{32,56},... | collective-permute-start | bytes 1572872 | tf_op jit(solution)/shard_map/ppermute | solution.py:299
  9.3 17.3 %collective-permute-start.6 = (bf16[2,64,2048]{2,1,0:T(8,128)(2,1)S(1)}, bf16[2,64,2048]{2,1,0:T(8,128)(2,1)}, u32[]{:S(2)}, u32[]{:S(2)}) collective-permute-start(bf16[2,64,2048]{2,1,0:T(8,128)(2,1)S(1)} %shard_map.87.refs_6_), channel_id=1, source_target_pairs={{0,8},{4,12},{8,16},{12,20},{16,24},{20,28},{24,0},{28,4},{32,40},... | collective-permute-start | bytes 1572872 | tf_op jit(solution)/shard_map/ppermute | solution.py:299
  16.9 12.5 %collective-permute-start.1 = (bf16[128,2176]{1,0:T(8,128)(2,1)}, bf16[128,2176]{1,0:T(8,128)(2,1)S(1)}, u32[]{:S(2)}, u32[]{:S(2)}) collective-permute-start(bf16[128,2176]{1,0:T(8,128)(2,1)} %collective-permute-done.refs_2_), channel_id=1, source_target_pairs={{0,32},{4,228},{8,40},{12,236},{16,48},{20,244},{24,56},{28,252},{... | collective-permute-start | bytes 1671176 | tf_op jit(solution)/shard_map/ppermute | solution.py:336
  22.9 11.8 %collective-permute-start.4 = (bf16[128,2176]{1,0:T(8,128)(2,1)}, bf16[128,2176]{1,0:T(8,128)(2,1)S(1)}, u32[]{:S(2)}, u32[]{:S(2)}) collective-permute-start(bf16[128,2176]{1,0:T(8,128)(2,1)} %collective-permute-done.3.refs_3_), channel_id=1, source_target_pairs={{0,32},{4,228},{8,40},{12,236},{16,48},{20,244},{24,56},{28,252},{... | collective-permute-start | bytes 1671176 | tf_op jit(solution)/shard_map/ppermute | solution.py:336
  24.4 18.8 %collective-permute-start.9 = (bf16[128,2176]{1,0:T(8,128)(2,1)}, bf16[128,2176]{1,0:T(8,128)(2,1)S(1)}, u32[]{:S(2)}, u32[]{:S(2)}) collective-permute-start(bf16[128,2176]{1,0:T(8,128)(2,1)} %collective-permute-done.refs_2_), channel_id=1, source_target_pairs={{0,4},{4,0},{8,12},{12,8},{16,20},{20,16},{24,28},{28,24},{32,36},... | collective-permute-start | bytes 1671176 | tf_op jit(solution)/shard_map/ppermute | solution.py:299
  26.6 17.0 %collective-permute-start.10 = (bf16[128,2176]{1,0:T(8,128)(2,1)}, bf16[128,2176]{1,0:T(8,128)(2,1)S(1)}, u32[]{:S(2)}, u32[]{:S(2)}) collective-permute-start(bf16[128,2176]{1,0:T(8,128)(2,1)} %collective-permute-done.3.refs_3_), channel_id=1, source_target_pairs={{0,4},{4,0},{8,12},{12,8},{16,20},{20,16},{24,28},{28,24},{32,36},... | collective-permute-start | bytes 1671176 | tf_op jit(solution)/shard_map/ppermute | solution.py:299
  28.6 12.6 %collective-permute-start.11 = (bf16[2,64,2048]{2,1,0:T(8,128)(2,1)S(1)}, bf16[2,64,2048]{2,1,0:T(8,128)(2,1)S(1)}, u32[]{:S(2)}, u32[]{:S(2)}) collective-permute-start(bf16[2,64,2048]{2,1,0:T(8,128)(2,1)S(1)} %get-tuple-element.36), channel_id=1, source_target_pairs={{0,24},{4,12},{8,0},{12,20},{16,8},{20,28},{24,16},{28,4},{32,56},... | collective-permute-start | bytes 1572872 | tf_op jit(solution)/shard_map/ppermute | solution.py:336
  29.4 8.4 %collective-permute-start.13 = (f32[2,32,192]{2,1,0:T(8,128)S(1)}, f32[2,32,192]{2,1,0:T(8,128)S(1)}, u32[]{:S(2)}, u32[]{:S(2)}) collective-permute-start(f32[2,32,192]{2,1,0:T(8,128)S(1)} %bitcast.17), channel_id=1, source_target_pairs={{0,2},{1,3},{2,0},{3,1},{4,6},{5,7},{6,4},{7,5},{8,10},{9,11},{10,... | collective-permute-start | bytes 147464 | tf_op jit(solution)/shard_map/ppermute | solution.py:302
  37.8 12.0 %collective-permute-start.7 = (bf16[128,2176]{1,0:T(8,128)(2,1)S(1)}, bf16[128,2176]{1,0:T(8,128)(2,1)S(1)}, u32[]{:S(2)}, u32[]{:S(2)}) collective-permute-start(bf16[128,2176]{1,0:T(8,128)(2,1)S(1)} %get-tuple-element.34.refs_0_.refs_6_), channel_id=1, source_target_pairs={{0,32},{4,228},{8,40},{12,236},{16,48},{20,244},{24,56},{28,252},{... | collective-permute-start | bytes 1671176 | tf_op jit(solution)/shard_map/ppermute | solution.py:336
  39.6 15.0 %collective-permute-start.8 = (bf16[128,2176]{1,0:T(8,128)(2,1)S(1)}, bf16[128,2176]{1,0:T(8,128)(2,1)S(1)}, u32[]{:S(2)}, u32[]{:S(2)}) collective-permute-start(bf16[128,2176]{1,0:T(8,128)(2,1)S(1)} %get-tuple-element.35.refs_1_.refs_7_), channel_id=1, source_target_pairs={{0,32},{4,228},{8,40},{12,236},{16,48},{20,244},{24,56},{28,252},{... | collective-permute-start | bytes 1671176 | tf_op jit(solution)/shard_map/ppermute | solution.py:336
  41.2 14.7 %collective-permute-start.16 = (bf16[128,2176]{1,0:T(8,128)(2,1)S(1)}, bf16[128,2176]{1,0:T(8,128)(2,1)S(1)}, u32[]{:S(2)}, u32[]{:S(2)}) collective-permute-start(bf16[128,2176]{1,0:T(8,128)(2,1)S(1)} %get-tuple-element.34.refs_0_.refs_6_), channel_id=1, source_target_pairs={{0,4},{4,0},{8,12},{12,8},{16,20},{20,16},{24,28},{28,24},{32,36},... | collective-permute-start | bytes 1671176 | tf_op jit(solution)/shard_map/ppermute | solution.py:299
  43.3 12.6 %collective-permute-start.17 = (bf16[128,2176]{1,0:T(8,128)(2,1)S(1)}, bf16[128,2176]{1,0:T(8,128)(2,1)S(1)}, u32[]{:S(2)}, u32[]{:S(2)}) collective-permute-start(bf16[128,2176]{1,0:T(8,128)(2,1)S(1)} %get-tuple-element.35.refs_1_.refs_7_), channel_id=1, source_target_pairs={{0,4},{4,0},{8,12},{12,8},{16,20},{20,16},{24,28},{28,24},{32,36},... | collective-permute-start | bytes 1671176 | tf_op jit(solution)/shard_map/ppermute | solution.py:299
  54.7 10.8 %collective-permute-start.15 = (bf16[128,2176]{1,0:T(8,128)(2,1)S(1)}, bf16[128,2176]{1,0:T(8,128)(2,1)S(1)}, u32[]{:S(2)}, u32[]{:S(2)}) collective-permute-start(bf16[128,2176]{1,0:T(8,128)(2,1)S(1)} %get-tuple-element.39.refs_0_.refs_10_), channel_id=1, source_target_pairs={{0,32},{4,228},{8,40},{12,236},{16,48},{20,244},{24,56},{28,252},{... | collective-permute-start | bytes 1671176 | tf_op jit(solution)/shard_map/ppermute | solution.py:336
  54.8 10.9 %collective-permute-start.19 = (bf16[128,2176]{1,0:T(8,128)(2,1)S(1)}, bf16[128,2176]{1,0:T(8,128)(2,1)S(1)}, u32[]{:S(2)}, u32[]{:S(2)}) collective-permute-start(bf16[128,2176]{1,0:T(8,128)(2,1)S(1)} %get-tuple-element.39.refs_0_.refs_10_), channel_id=1, source_target_pairs={{0,4},{4,0},{8,12},{12,8},{16,20},{20,16},{24,28},{28,24},{32,36},... | collective-permute-start | bytes 1671176 | tf_op jit(solution)/shard_map/ppermute | solution.py:299
  55.8 9.8 %collective-permute-start.20 = (bf16[128,2176]{1,0:T(8,128)(2,1)S(1)}, bf16[128,2176]{1,0:T(8,128)(2,1)S(1)}, u32[]{:S(2)}, u32[]{:S(2)}) collective-permute-start(bf16[128,2176]{1,0:T(8,128)(2,1)S(1)} %get-tuple-element.43.refs_1_.refs_11_), channel_id=1, source_target_pairs={{0,4},{4,0},{8,12},{12,8},{16,20},{20,16},{24,28},{28,24},{32,36},... | collective-permute-start | bytes 1671176 | tf_op jit(solution)/shard_map/ppermute | solution.py:299
  79.8 11.1 %collective-permute-start.24 = (f32[2,32,768]{2,1,0:T(8,128)S(1)}, f32[2,32,768]{2,1,0:T(8,128)S(1)}, u32[]{:S(2)}, u32[]{:S(2)}) collective-permute-start(f32[2,32,768]{2,1,0:T(8,128)S(1)} %shard_map.97.refs_0_), channel_id=1, source_target_pairs={{0,1},{1,2},{2,3},{3,0},{4,5},{5,6},{6,7},{7,4},{8,9},{9,10},{10,1... | collective-permute-start | bytes 589832 | tf_op jit(solution)/shard_map/ppermute | solution.py:302
  79.9 11.0 %collective-permute-start.25 = (f32[2,32,768]{2,1,0:T(8,128)S(1)}, f32[2,32,768]{2,1,0:T(8,128)S(1)}, u32[]{:S(2)}, u32[]{:S(2)}) collective-permute-start(f32[2,32,768]{2,1,0:T(8,128)S(1)} %shard_map.97.refs_0_), channel_id=1, source_target_pairs={{0,2},{1,3},{2,0},{3,1},{4,6},{5,7},{6,4},{7,5},{8,10},{9,11},{10,... | collective-permute-start | bytes 589832 | tf_op jit(solution)/shard_map/ppermute | solution.py:302
  82.1 9.4 %collective-permute-start.26 = (f32[2,32,768]{2,1,0:T(8,128)S(1)}, f32[2,32,768]{2,1,0:T(8,128)S(1)}, u32[]{:S(2)}, u32[]{:S(2)}) collective-permute-start(f32[2,32,768]{2,1,0:T(8,128)S(1)} %shard_map.97.refs_0_), channel_id=1, source_target_pairs={{0,3},{1,0},{2,1},{3,2},{4,7},{5,4},{6,5},{7,6},{8,11},{9,8},{10,9... | collective-permute-start | bytes 589832 | tf_op jit(solution)/shard_map/ppermute | solution.py:302
  112.5 11.2 %collective-permute-start.30 = (bf16[2,32,2048]{2,1,0:T(8,128)(2,1)S(1)}, bf16[2,32,2048]{2,1,0:T(8,128)(2,1)S(1)}, u32[]{:S(2)}, u32[]{:S(2)}) collective-permute-start(bf16[2,32,2048]{2,1,0:T(8,128)(2,1)S(1)} %get-tuple-element.61), channel_id=1, source_target_pairs={{0,8},{4,12},{8,16},{12,20},{16,24},{20,28},{24,0},{28,4},{32,40},... | collective-permute-start | bytes 786440 | tf_op jit(solution)/shard_map/ppermute | solution.py:299
  115.2 9.5 %collective-permute-start.31 = (bf16[2,32,2048]{2,1,0:T(8,128)(2,1)S(1)}, bf16[2,32,2048]{2,1,0:T(8,128)(2,1)S(1)}, u32[]{:S(2)}, u32[]{:S(2)}) collective-permute-start(bf16[2,32,2048]{2,1,0:T(8,128)(2,1)S(1)} %get-tuple-element.62), channel_id=1, source_target_pairs={{0,16},{4,20},{8,24},{12,28},{16,0},{20,4},{24,8},{28,12},{32,48},... | collective-permute-start | bytes 786440 | tf_op jit(solution)/shard_map/ppermute | solution.py:299
  116.0 11.4 %collective-permute-start.32 = (bf16[2,32,2048]{2,1,0:T(8,128)(2,1)S(1)}, bf16[2,32,2048]{2,1,0:T(8,128)(2,1)S(1)}, u32[]{:S(2)}, u32[]{:S(2)}) collective-permute-start(bf16[2,32,2048]{2,1,0:T(8,128)(2,1)S(1)} %get-tuple-element.63), channel_id=1, source_target_pairs={{0,24},{4,28},{8,0},{12,4},{16,8},{20,12},{24,16},{28,20},{32,56},... | collective-permute-start | bytes 786440 | tf_op jit(solution)/shard_map/ppermute | solution.py:299
  129.4 9.2 %collective-permute-start.34 = (f32[2,32,512]{2,1,0:T(8,128)S(1)}, f32[2,32,512]{2,1,0:T(8,128)S(1)}, u32[]{:S(2)}, u32[]{:S(2)}) collective-permute-start(f32[2,32,512]{2,1,0:T(8,128)S(1)} %get-tuple-element.66), channel_id=1, source_target_pairs={{0,2},{1,3},{2,0},{3,1},{4,6},{5,7},{6,4},{7,5},{8,10},{9,11},{10,... | collective-permute-start | bytes 393224 | tf_op jit(solution)/shard_map/ppermute | solution.py:302
  (23 other events, 217.7 us)
where the time goes:
time: 140 us; the launch traced here: 139 us
  waiting for transfers between devices  60.7 us (43%)
  starting transfers between devices  40.2 us (29%)
  Pallas kernels  32 us (23%)
  local copies, waits for them, and re-layouts  4.64 us (3%)
    pallas_call x15, Pallas kernels, call(): pl.pallas_call(kernel, out_shape=outs, in_specs=specs or [VMEM] * len(arg...  32 us
    ppermute x8, waiting for transfers between devices, along(): return lax.ppermute(v, 'expert', pairs)  26 us
    ppermute x19, starting transfers between devices, shift(): return lax.ppermute(v, 'expert', pairs)  19.4 us
    ppermute x19, waiting for transfers between devices, shift(): return lax.ppermute(v, 'expert', pairs)  18.3 us
    ppermute x9, waiting for transfers between devices, shift_y(): return lax.ppermute(v, 'zero', [(a, (a + dy) % ny) for a in range(ny)])  16.4 us
    ppermute x9, starting transfers between devices, shift_y(): return lax.ppermute(v, 'zero', [(a, (a + dy) % ny) for a in range(ny)])  15.8 us
    ppermute x8, starting transfers between devices, along(): return lax.ppermute(v, 'expert', pairs)  4.92 us
    unnamed x22, local copies, waits for them, and re-layouts  4.6 us
  transfers between devices with their start and end apart: 36, of which 19 were waited for; matrix products, arithmetic and copies ran while one was open for 0% of the time, Pallas kernels for 11%

commit v1 on v0

--- a/solution.py
+++ b/solution.py
@@ -11,7 +11,7 @@
 CAP = 16
 MOMENTUM_DECAY = 0.9
 
-WIDE, NARROW = 20 << 20, 12 << 20
+WIDE, NARROW = 20 << 20, 8 << 20
 
 BF, F32 = jnp.bfloat16, jnp.float32
 HIGHEST = lax.Precision.HIGHEST
@@ -242,7 +242,7 @@
         mom_ref[i] = dot(inner, r_ref[i], NN, HIGHEST)
 
 
-def coefficient_kernel(counts, nd, unread, *refs):
+def coefficient_kernel(counts, skipped, nd, unread, *refs):
     nb = sum(counts)
     pieces, refs = refs[:nb], refs[nb:]
     zs, refs = refs[:nd], refs[nd:]
@@ -250,6 +250,7 @@
     outs, w_scr = refs[:nd], refs[nd]
     local, rank, slots = zs[0].shape
     count = nd * local
+    every = poss[0].shape[0] // (2 * counts[0])
     tokens = poss[0].shape[1]
     rows = count * rank
     width = outs[0].shape[-1]
@@ -257,7 +258,7 @@
     for q in range(count):
         line = lambda gate: jnp.concatenate(
             [
-                r[(gate * n + b) * count + q : (gate * n + b) * count + q + 1]
+                r[(gate * n + b) * every + skipped + q : (gate * n + b) * every + skipped + q + 1]
                 for r, n in zip(poss, counts)
                 for b in range(n)
             ],
@@ -309,6 +310,7 @@
         shaped((tokens, width + tokens), BF),
         (cotangent, gates.T, expert_ids.T),
         specs=[ANY] * 3,
+        limit=58 << 20,
         scratch=[
             pltpu.VMEM((gates.shape[1], tokens), F32),
             pltpu.VMEM((gates.shape[1], tokens), jnp.int32),
@@ -378,11 +380,11 @@
         specs=[SMEM] + [VMEM] * (2 + ny),
         scratch=[pltpu.VMEM((ny, local, rank, ff // ny), F32)],
     )
-    p, q = after([along(p), along(q)], token)
+    [p], q = after([along(p)], token, mom), along(q)
     second = ring(2, p, q)
     a = project(first, [two, near[0], far, near[1]], [])
     all_s = [a[4]]
-    p, q = after([along(p), along(q)], a[3], mom)
+    [p], q = after([along(p)], a[3]), along(q)
     third = ring(3, p, q)
     b = project(second, all_s, a[2])
     [p] = after([along(p)], b[3])
@@ -419,17 +421,18 @@
         specs=[SMEM] + [VMEM] * 3,
         limit=NARROW,
     )
-    coeff = call(
-        functools.partial(coefficient_kernel, counts, nx, 1),
-        [shaped((local, rank, width))] + [shaped((local, rank, width), BF)] * (nx - 1),
-        (*pieces, *coded, *[v[3] for v in steps], own_mom),
-        specs=[VMEM] * (len(pieces) + nx + len(steps) + 1),
-        limit=WIDE,
-        scratch=[
-            pltpu.VMEM((2 * count * rank, sum(counts) * tokens), BF),
-        ],
-        flops=2 * 2 * count * rank * sum(counts) * tokens * width,
-    )
+    def coefficients(groups, *unread):
+        return call(
+            functools.partial(
+                coefficient_kernel, counts, groups[0] * local, len(groups), len(unread)
+            ),
+            [shaped((local, rank, width), BF if d else F32) for d in groups],
+            (*pieces, *[coded[d] for d in groups], *[v[3] for v in steps], *unread),
+            scratch=[pltpu.VMEM((2 * len(groups) * local * rank, sum(counts) * tokens), BF)],
+            flops=2 * 2 * len(groups) * local * rank * sum(counts) * tokens * width,
+        )
+
+    coeff = coefficients(list(range(nx)), own_mom)
     total = coeff[0]
     for d in range(1, nx):
         total = total + shift(coeff[d], dx=d).astype(F32)

time: 140 us -> 137 us (0.979)
  local copies, waits for them, and re-layouts: 4.64 us -> 1.1 us
    ppermute x8, waiting for transfers between devices: 26 us -> 17 us  [along(): return lax.ppermute(v, 'expert', pairs)]
    ppermute x9, waiting for transfers between devices: 16.4 us -> 24.4 us  [shift_y(): return lax.ppermute(v, 'zero', [(a, (a + dy) % ny) for a in range(ny)])]
    ppermute x8, starting transfers between devices: 4.92 us -> 11.5 us  [along(): return lax.ppermute(v, 'expert', pairs)]
    ppermute x19, starting transfers between devices: 19.4 us -> 14 us  [shift(): return lax.ppermute(v, 'expert', pairs)]
    unnamed x22 -> x12, local copies, waits for them, and re-layouts: 4.6 us -> 1.07 us
    ppermute x9, starting transfers between devices: 15.8 us -> 14.4 us  [shift_y(): return lax.ppermute(v, 'zero', [(a, (a + dy) % ny) for a in range(ny)])]
    pallas_call x15, Pallas kernels: 32 us -> 33.4 us  [call(): pl.pallas_call(kernel, out_shape=outs, in_specs=specs or [VMEM] * len(arg...]
  transfers between devices with their start and end apart: 36 -> 36, of which waited for: 19 -> 21; matrix products, arithmetic and copies ran while one was open for 0% -> 0% of each run, Pallas kernels for 11% -> 10%
where the time goes in v1:
time: 137 us; the launch traced here: 136 us
  waiting for transfers between devices  59.9 us (44%)
  starting transfers between devices  39.9 us (29%)
  Pallas kernels  33.4 us (24%)
    pallas_call x15, Pallas kernels, call(): pl.pallas_call(kernel, out_shape=outs, in_specs=specs or [VMEM] * len(arg...  33.4 us
    ppermute x9, waiting for transfers between devices, shift_y(): return lax.ppermute(v, 'zero', [(a, (a + dy) % ny) for a in range(ny)])  24.4 us
    ppermute x19, waiting for transfers between devices, shift(): return lax.ppermute(v, 'expert', pairs)  18.6 us
    ppermute x8, waiting for transfers between devices, along(): return lax.ppermute(v, 'expert', pairs)  17 us
    ppermute x9, starting transfers between devices, shift_y(): return lax.ppermute(v, 'zero', [(a, (a + dy) % ny) for a in range(ny)])  14.4 us
    ppermute x19, starting transfers between devices, shift(): return lax.ppermute(v, 'expert', pairs)  14 us
    ppermute x8, starting transfers between devices, along(): return lax.ppermute(v, 'expert', pairs)  11.5 us
  transfers between devices with their start and end apart: 36, of which 21 were waited for; matrix products, arithmetic and copies ran while one was open for 0% of the time, Pallas kernels for 10%

profile of v1, /device:TPU:6, one launch (start us, length us, event | category | flops | bytes accessed | tf_op | source)
XLA Modules:
  0.0 136.1 jit_solution(7934269593757981251)
XLA Ops:
  9.0 2.4 %collective-permute-start.3 = (bf16[2,64,2048]{2,1,0:T(8,128)(2,1)S(1)}, bf16[2,64,2048]{2,1,0:T(8,128)(2,1)S(1)}, u32[]{:S(2)}, u32[]{:S(2)}) collective-permute-start(bf16[2,64,2048]{2,1,0:T(8,128)(2,1)S(1)} %shard_map.87.refs_6_), channel_id=1, source_target_pairs={{0,8},{4,12},{8,16},{12,20},{16,24},{20,28},{24,0},{28,4},{32,40},... | collective-permute-start | bytes 1572872 | tf_op jit(solution)/shard_map/ppermute | solution.py:300
  11.4 5.1 %collective-permute-done.refs_2_ = bf16[128,2176]{1,0:T(8,128)(2,1)} collective-permute-done((bf16[128,2176]{1,0:T(8,128)(2,1)}, bf16[128,2176]{1,0:T(8,128)(2,1)}, u32[]{:S(2)}, u32[]{:S(2)}) %collective-permute-start) | collective-permute-done | bytes 557088 | tf_op jit(solution)/shard_map/ppermute | solution.py:338
  18.1 4.1 %collective-permute-done.4.refs_1_ = f32[2,32,192]{2,1,0:T(8,128)S(1)} collective-permute-done((f32[2,32,192]{2,1,0:T(8,128)}, f32[2,32,192]{2,1,0:T(8,128)S(1)}, u32[]{:S(2)}, u32[]{:S(2)}) %collective-permute-start.4) | collective-permute-done | bytes 49184 | tf_op jit(solution)/shard_map/ppermute | solution.py:303
  24.1 4.1 %collective-permute-done.5.refs_2_ = f32[2,32,192]{2,1,0:T(8,128)S(1)} collective-permute-done((f32[2,32,192]{2,1,0:T(8,128)}, f32[2,32,192]{2,1,0:T(8,128)S(1)}, u32[]{:S(2)}, u32[]{:S(2)}) %collective-permute-start.5) | collective-permute-done | bytes 49184 | tf_op jit(solution)/shard_map/ppermute | solution.py:303
  37.0 6.3 %collective-permute-done.12.refs_8_ = bf16[2,64,2048]{2,1,0:T(8,128)(2,1)S(1)} collective-permute-done((bf16[2,64,2048]{2,1,0:T(8,128)(2,1)S(1)}, bf16[2,64,2048]{2,1,0:T(8,128)(2,1)S(1)}, u32[]{:S(2)}, u32[]{:S(2)}) %collective-permute-start.12) | collective-permute-done | bytes 524320 | tf_op jit(solution)/shard_map/ppermute | solution.py:338
  45.6 5.1 %shard_map.91 = (f32[8,32,256]{2,1,0:T(8,128)S(1)}, bf16[512,2048]{1,0:T(8,128)(2,1)S(1)}, f32[96,128]{1,0:T(8,128)S(1)}) custom-call(s32[4]{0:T(128)S(1)} %pad_add_fusion.meta_ref, bf16[128,2176]{1,0:T(8,128)(2,1)S(1)} %copy-done.3, bf16[128,2176]{1,0:T(8,128)(2,1)} %collective-permute-done.8.refs_1_, bf16[128,2176]{1,0:T(8,128)(2,1)} %collective-permute-done.refs_2_, ...), custom_call_target="tpu_custom_call" | custom-call | flops 1610612736 | bytes 3221225 | tf_op jit(solution)/shard_map/pallas_call | solution.py:45
  50.8 2.9 %collective-permute-start.13 = (bf16[128,2176]{1,0:T(8,128)(2,1)S(1)}, bf16[128,2176]{1,0:T(8,128)(2,1)S(1)}, u32[]{:S(2)}, u32[]{:S(2)}) collective-permute-start(bf16[128,2176]{1,0:T(8,128)(2,1)S(1)} %shard_map.92.refs_0_.refs_10_), channel_id=1, source_target_pairs={{0,32},{4,228},{8,40},{12,236},{16,48},{20,244},{24,56},{28,252},{... | collective-permute-start | bytes 1671176 | tf_op jit(solution)/shard_map/ppermute | solution.py:338
  54.6 2.4 %shard_map.93 = (f32[8,32,256]{2,1,0:T(8,128)S(1)}, f32[64,128]{1,0:T(8,128)S(1)}) custom-call(s32[4]{0:T(128)S(1)} %pad_add_fusion.meta_ref, bf16[128,2176]{1,0:T(8,128)(2,1)S(1)} %shard_map.90.refs_0_.refs_6_, bf16[128,2176]{1,0:T(8,128)(2,1)S(1)} %collective-permute-done.14.refs_1_.refs_7_, bf16[128,2176]{1,0:T(8,128)(2,1)S(1)} %collective-permute-done.15.refs_2_.refs_8_, ...), custom_call_target="tpu_custom_call" | custom-call | flops 1073741824 | bytes 2147483 | tf_op jit(solution)/shard_map/pallas_call | solution.py:45
  57.0 4.6 %collective-permute-done.13.refs_0_ = bf16[128,2176]{1,0:T(8,128)(2,1)S(1)} collective-permute-done((bf16[128,2176]{1,0:T(8,128)(2,1)S(1)}, bf16[128,2176]{1,0:T(8,128)(2,1)S(1)}, u32[]{:S(2)}, u32[]{:S(2)}) %collective-permute-start.13) | collective-permute-done | bytes 557088 | tf_op jit(solution)/shard_map/ppermute | solution.py:338
  61.8 2.4 %shard_map.95 = (f32[8,32,256]{2,1,0:T(8,128)S(1)}, f32[64,128]{1,0:T(8,128)S(1)}) custom-call(s32[4]{0:T(128)S(1)} %pad_add_fusion.meta_ref, bf16[128,2176]{1,0:T(8,128)(2,1)S(1)} %shard_map.92.refs_0_.refs_10_, bf16[128,2176]{1,0:T(8,128)(2,1)S(1)} %collective-permute-done.18.refs_1_.refs_11_, ...), custom_call_target="tpu_custom_call" | custom-call | flops 1073741824 | bytes 2147483 | tf_op jit(solution)/shard_map/pallas_call | solution.py:45
  64.2 2.1 %shard_map.96 = (f32[2,32,256]{2,1,0:T(8,128)S(1)}, f32[2,32,256]{2,1,0:T(8,128)S(1)}, f32[2,32,256]{2,1,0:T(8,128)S(1)}, f32[2,32,256]{2,1,0:T(8,128)S(1)}, f32[32,128]{1,0:T(8,128)S(1)}) custom-call(s32[4]{0:T(128)S(1)} %pad_add_fusion.meta_ref, bf16[128,2176]{1,0:T(8,128)(2,1)S(1)} %shard_map.94.refs_0_.refs_14_, ...), custom_call_target="tpu_custom_call" | custom-call | flops 536870912 | bytes 1073741 | tf_op jit(solution)/shard_map/pallas_call | solution.py:45
  68.4 2.9 %collective-permute-done.21.refs_1_ = f32[2,32,256]{2,1,0:T(8,128)S(1)} collective-permute-done((f32[2,32,256]{2,1,0:T(8,128)S(1)}, f32[2,32,256]{2,1,0:T(8,128)S(1)}, u32[]{:S(2)}, u32[]{:S(2)}) %collective-permute-start.21) | collective-permute-done | bytes 65568 | tf_op jit(solution)/shard_map/ppermute | solution.py:300
  75.2 3.4 %collective-permute-start.25 = (f32[2,32,768]{2,1,0:T(8,128)S(1)}, f32[2,32,768]{2,1,0:T(8,128)S(1)}, u32[]{:S(2)}, u32[]{:S(2)}) collective-permute-start(f32[2,32,768]{2,1,0:T(8,128)S(1)} %shard_map.97.refs_0_), channel_id=1, source_target_pairs={{0,2},{1,3},{2,0},{3,1},{4,6},{5,7},{6,4},{7,5},{8,10},{9,11},{10,... | collective-permute-start | bytes 589832 | tf_op jit(solution)/shard_map/ppermute | solution.py:303
  78.9 5.5 %collective-permute-done.24.refs_1_ = f32[2,32,768]{2,1,0:T(8,128)S(1)} collective-permute-done((f32[2,32,768]{2,1,0:T(8,128)S(1)}, f32[2,32,768]{2,1,0:T(8,128)S(1)}, u32[]{:S(2)}, u32[]{:S(2)}) %collective-permute-start.24) | collective-permute-done | bytes 196640 | tf_op jit(solution)/shard_map/ppermute | solution.py:303
  84.4 2.9 %collective-permute-done.25.refs_2_ = f32[2,32,768]{2,1,0:T(8,128)S(1)} collective-permute-done((f32[2,32,768]{2,1,0:T(8,128)S(1)}, f32[2,32,768]{2,1,0:T(8,128)S(1)}, u32[]{:S(2)}, u32[]{:S(2)}) %collective-permute-start.25) | collective-permute-done | bytes 196640 | tf_op jit(solution)/shard_map/ppermute | solution.py:303
  87.9 5.3 %shard_map.98 = (f32[2,32,768]{2,1,0:T(8,128)S(1)}, f32[2,32,256]{2,1,0:T(8,128)S(1)}, f32[2,32,256]{2,1,0:T(8,128)S(1)}, f32[2,32,256]{2,1,0:T(8,128)S(1)}, f32[2,32,256]{2,1,0:T(8,128)S(1)}) custom-call(s32[4]{0:T(128)S(1)} %pad_add_fusion.meta_ref, f32[2,32,768]{2,1,0:T(8,128)S(1)} %shard_map.97.refs_0_, ...), custom_call_target="tpu_custom_call" | custom-call | tf_op jit(solution)/shard_map/pallas_call | solution.py:45
  93.2 2.3 %collective-permute-start.28 = (f32[2,32,256]{2,1,0:T(8,128)S(1)}, f32[2,32,256]{2,1,0:T(8,128)S(1)}, u32[]{:S(2)}, u32[]{:S(2)}) collective-permute-start(f32[2,32,256]{2,1,0:T(8,128)S(1)} %get-tuple-element.47), channel_id=1, source_target_pairs={{0,16},{4,20},{8,24},{12,28},{16,0},{20,4},{24,8},{28,12},{32,48},... | collective-permute-start | bytes 196616 | tf_op jit(solution)/shard_map/ppermute | solution.py:300
  100.3 8.8 %shard_map.100 = (f32[2,32,2048]{2,1,0:T(8,128)S(1)}, bf16[2,32,2048]{2,1,0:T(8,128)(2,1)S(1)}, bf16[2,32,2048]{2,1,0:T(8,128)(2,1)S(1)}, bf16[2,32,2048]{2,1,0:T(8,128)(2,1)S(1)}) custom-call(bf16[128,2176]{1,0:T(8,128)(2,1)S(1)} %copy-done.3, bf16[128,2176]{1,0:T(8,128)(2,1)} %collective-permute-done.8.refs_1_, ...), custom_call_target="tpu_custom_call" | custom-call | flops 4294967296 | bytes 8589934 | tf_op jit(solution)/shard_map/pallas_call | solution.py:45
  109.0 2.8 %collective-permute-start.30 = (bf16[2,32,2048]{2,1,0:T(8,128)(2,1)S(1)}, bf16[2,32,2048]{2,1,0:T(8,128)(2,1)S(1)}, u32[]{:S(2)}, u32[]{:S(2)}) collective-permute-start(bf16[2,32,2048]{2,1,0:T(8,128)(2,1)S(1)} %get-tuple-element.53), channel_id=1, source_target_pairs={{0,8},{4,12},{8,16},{12,20},{16,24},{20,28},{24,0},{28,4},{32,40},... | collective-permute-start | bytes 786440 | tf_op jit(solution)/shard_map/ppermute | solution.py:300
  112.7 7.7 %collective-permute-done.30 = bf16[2,32,2048]{2,1,0:T(8,128)(2,1)S(1)} collective-permute-done((bf16[2,32,2048]{2,1,0:T(8,128)(2,1)S(1)}, bf16[2,32,2048]{2,1,0:T(8,128)(2,1)S(1)}, u32[]{:S(2)}, u32[]{:S(2)}) %collective-permute-start.30) | collective-permute-done | bytes 262176 | tf_op jit(solution)/shard_map/ppermute | solution.py:300
  121.5 2.6 %collective-permute-done.32 = bf16[2,32,2048]{2,1,0:T(8,128)(2,1)S(1)} collective-permute-done((bf16[2,32,2048]{2,1,0:T(8,128)(2,1)S(1)}, bf16[2,32,2048]{2,1,0:T(8,128)(2,1)S(1)}, u32[]{:S(2)}, u32[]{:S(2)}) %collective-permute-start.32) | collective-permute-done | bytes 262176 | tf_op jit(solution)/shard_map/ppermute | solution.py:300
  124.2 2.1 %collective-permute-start.33 = (f32[2,32,512]{2,1,0:T(8,128)S(1)}, f32[2,32,512]{2,1,0:T(8,128)S(1)}, u32[]{:S(2)}, u32[]{:S(2)}) collective-permute-start(f32[2,32,512]{2,1,0:T(8,128)S(1)} %get-tuple-element.56), channel_id=1, source_target_pairs={{0,1},{1,2},{2,3},{3,0},{4,5},{5,6},{6,7},{7,4},{8,9},{9,10},{10,1... | collective-permute-start | bytes 393224 | tf_op jit(solution)/shard_map/ppermute | solution.py:303
  126.3 3.1 %collective-permute-start.34 = (f32[2,32,512]{2,1,0:T(8,128)S(1)}, f32[2,32,512]{2,1,0:T(8,128)S(1)}, u32[]{:S(2)}, u32[]{:S(2)}) collective-permute-start(f32[2,32,512]{2,1,0:T(8,128)S(1)} %get-tuple-element.58), channel_id=1, source_target_pairs={{0,2},{1,3},{2,0},{3,1},{4,6},{5,7},{6,4},{7,5},{8,10},{9,11},{10,... | collective-permute-start | bytes 393224 | tf_op jit(solution)/shard_map/ppermute | solution.py:303
  131.4 4.0 %collective-permute-done.34 = f32[2,32,512]{2,1,0:T(8,128)S(1)} collective-permute-done((f32[2,32,512]{2,1,0:T(8,128)S(1)}, f32[2,32,512]{2,1,0:T(8,128)S(1)}, u32[]{:S(2)}, u32[]{:S(2)}) %collective-permute-start.34) | collective-permute-done | bytes 131104 | tf_op jit(solution)/shard_map/ppermute | solution.py:303
  (79 shorter events, 40.5 us)
Async XLA Ops:
  2.7 13.8 %collective-permute-start = (bf16[128,2176]{1,0:T(8,128)(2,1)}, bf16[128,2176]{1,0:T(8,128)(2,1)}, u32[]{:S(2)}, u32[]{:S(2)}) collective-permute-start(bf16[128,2176]{1,0:T(8,128)(2,1)} %shard_map.86.refs_0_), channel_id=1, source_target_pairs={{0,32},{4,228},{8,40},{12,236},{16,48},{20,244},{24,56},{28,252},{... | collective-permute-start | bytes 1671176 | tf_op jit(solution)/shard_map/ppermute | solution.py:338
  5.0 25.2 %collective-permute-start.9 = (bf16[128,2176]{1,0:T(8,128)(2,1)}, bf16[128,2176]{1,0:T(8,128)(2,1)}, u32[]{:S(2)}, u32[]{:S(2)}) collective-permute-start(bf16[128,2176]{1,0:T(8,128)(2,1)} %collective-permute-done.8.refs_1_), channel_id=1, source_target_pairs={{0,32},{4,228},{8,40},{12,236},{16,48},{20,244},{24,56},{28,252},{... | collective-permute-start | bytes 1671176 | tf_op jit(solution)/shard_map/ppermute | solution.py:338
  8.1 22.0 %collective-permute-start.2 = (bf16[2,64,2048]{2,1,0:T(8,128)(2,1)S(1)}, bf16[2,64,2048]{2,1,0:T(8,128)(2,1)S(1)}, u32[]{:S(2)}, u32[]{:S(2)}) collective-permute-start(bf16[2,64,2048]{2,1,0:T(8,128)(2,1)S(1)} %shard_map.87.refs_6_), channel_id=1, source_target_pairs={{0,24},{4,28},{8,0},{12,4},{16,8},{20,12},{24,16},{28,20},{32,56},... | collective-permute-start | bytes 1572872 | tf_op jit(solution)/shard_map/ppermute | solution.py:300
  9.0 21.6 %collective-permute-start.3 = (bf16[2,64,2048]{2,1,0:T(8,128)(2,1)S(1)}, bf16[2,64,2048]{2,1,0:T(8,128)(2,1)S(1)}, u32[]{:S(2)}, u32[]{:S(2)}) collective-permute-start(bf16[2,64,2048]{2,1,0:T(8,128)(2,1)S(1)} %shard_map.87.refs_6_), channel_id=1, source_target_pairs={{0,8},{4,12},{8,16},{12,20},{16,24},{20,28},{24,0},{28,4},{32,40},... | collective-permute-start | bytes 1572872 | tf_op jit(solution)/shard_map/ppermute | solution.py:300
  16.5 18.8 %collective-permute-start.1 = (bf16[128,2176]{1,0:T(8,128)(2,1)}, bf16[128,2176]{1,0:T(8,128)(2,1)S(1)}, u32[]{:S(2)}, u32[]{:S(2)}) collective-permute-start(bf16[128,2176]{1,0:T(8,128)(2,1)} %collective-permute-done.refs_2_), channel_id=1, source_target_pairs={{0,32},{4,228},{8,40},{12,236},{16,48},{20,244},{24,56},{28,252},{... | collective-permute-start | bytes 1671176 | tf_op jit(solution)/shard_map/ppermute | solution.py:338
  30.1 13.7 %collective-permute-start.10 = (bf16[128,2176]{1,0:T(8,128)(2,1)}, bf16[128,2176]{1,0:T(8,128)(2,1)S(1)}, u32[]{:S(2)}, u32[]{:S(2)}) collective-permute-start(bf16[128,2176]{1,0:T(8,128)(2,1)} %collective-permute-done.refs_2_), channel_id=1, source_target_pairs={{0,4},{4,0},{8,12},{12,8},{16,20},{20,16},{24,28},{28,24},{32,36},... | collective-permute-start | bytes 1671176 | tf_op jit(solution)/shard_map/ppermute | solution.py:300
  30.2 15.3 %collective-permute-start.11 = (bf16[128,2176]{1,0:T(8,128)(2,1)}, bf16[128,2176]{1,0:T(8,128)(2,1)S(1)}, u32[]{:S(2)}, u32[]{:S(2)}) collective-permute-start(bf16[128,2176]{1,0:T(8,128)(2,1)} %collective-permute-done.9.refs_3_), channel_id=1, source_target_pairs={{0,4},{4,0},{8,12},{12,8},{16,20},{20,16},{24,28},{28,24},{32,36},... | collective-permute-start | bytes 1671176 | tf_op jit(solution)/shard_map/ppermute | solution.py:300
  30.6 12.7 %collective-permute-start.14 = (bf16[128,2176]{1,0:T(8,128)(2,1)}, bf16[128,2176]{1,0:T(8,128)(2,1)S(1)}, u32[]{:S(2)}, u32[]{:S(2)}) collective-permute-start(bf16[128,2176]{1,0:T(8,128)(2,1)} %collective-permute-done.9.refs_3_), channel_id=1, source_target_pairs={{0,32},{4,228},{8,40},{12,236},{16,48},{20,244},{24,56},{28,252},{... | collective-permute-start | bytes 1671176 | tf_op jit(solution)/shard_map/ppermute | solution.py:338
  32.9 10.4 %collective-permute-start.12 = (bf16[2,64,2048]{2,1,0:T(8,128)(2,1)S(1)}, bf16[2,64,2048]{2,1,0:T(8,128)(2,1)S(1)}, u32[]{:S(2)}, u32[]{:S(2)}) collective-permute-start(bf16[2,64,2048]{2,1,0:T(8,128)(2,1)S(1)} %get-tuple-element.31), channel_id=1, source_target_pairs={{0,24},{4,12},{8,0},{12,20},{16,8},{20,28},{24,16},{28,4},{32,56},... | collective-permute-start | bytes 1572872 | tf_op jit(solution)/shard_map/ppermute | solution.py:338
  35.4 15.4 %collective-permute-start.7 = (bf16[128,2176]{1,0:T(8,128)(2,1)S(1)}, bf16[128,2176]{1,0:T(8,128)(2,1)S(1)}, u32[]{:S(2)}, u32[]{:S(2)}) collective-permute-start(bf16[128,2176]{1,0:T(8,128)(2,1)S(1)} %shard_map.90.refs_0_.refs_6_), channel_id=1, source_target_pairs={{0,32},{4,228},{8,40},{12,236},{16,48},{20,244},{24,56},{28,252},{... | collective-permute-start | bytes 1671176 | tf_op jit(solution)/shard_map/ppermute | solution.py:338
  43.3 11.3 %collective-permute-start.15 = (bf16[128,2176]{1,0:T(8,128)(2,1)S(1)}, bf16[128,2176]{1,0:T(8,128)(2,1)S(1)}, u32[]{:S(2)}, u32[]{:S(2)}) collective-permute-start(bf16[128,2176]{1,0:T(8,128)(2,1)S(1)} %shard_map.90.refs_0_.refs_6_), channel_id=1, source_target_pairs={{0,4},{4,0},{8,12},{12,8},{16,20},{20,16},{24,28},{28,24},{32,36},... | collective-permute-start | bytes 1671176 | tf_op jit(solution)/shard_map/ppermute | solution.py:300
  43.3 11.3 %collective-permute-start.16 = (bf16[128,2176]{1,0:T(8,128)(2,1)S(1)}, bf16[128,2176]{1,0:T(8,128)(2,1)S(1)}, u32[]{:S(2)}, u32[]{:S(2)}) collective-permute-start(bf16[128,2176]{1,0:T(8,128)(2,1)S(1)} %collective-permute-done.14.refs_1_.refs_7_), channel_id=1, source_target_pairs={{0,4},{4,0},{8,12},{12,8},{16,20},{20,16},{24,28},{28,24},{32,36},... | collective-permute-start | bytes 1671176 | tf_op jit(solution)/shard_map/ppermute | solution.py:300
  43.8 10.7 %collective-permute-start.18 = (bf16[128,2176]{1,0:T(8,128)(2,1)S(1)}, bf16[128,2176]{1,0:T(8,128)(2,1)S(1)}, u32[]{:S(2)}, u32[]{:S(2)}) collective-permute-start(bf16[128,2176]{1,0:T(8,128)(2,1)S(1)} %collective-permute-done.14.refs_1_.refs_7_), channel_id=1, source_target_pairs={{0,32},{4,228},{8,40},{12,236},{16,48},{20,244},{24,56},{28,252},{... | collective-permute-start | bytes 1671176 | tf_op jit(solution)/shard_map/ppermute | solution.py:338
  50.8 10.8 %collective-permute-start.13 = (bf16[128,2176]{1,0:T(8,128)(2,1)S(1)}, bf16[128,2176]{1,0:T(8,128)(2,1)S(1)}, u32[]{:S(2)}, u32[]{:S(2)}) collective-permute-start(bf16[128,2176]{1,0:T(8,128)(2,1)S(1)} %shard_map.92.refs_0_.refs_10_), channel_id=1, source_target_pairs={{0,32},{4,228},{8,40},{12,236},{16,48},{20,244},{24,56},{28,252},{... | collective-permute-start | bytes 1671176 | tf_op jit(solution)/shard_map/ppermute | solution.py:338
  53.7 8.1 %collective-permute-start.19 = (bf16[128,2176]{1,0:T(8,128)(2,1)S(1)}, bf16[128,2176]{1,0:T(8,128)(2,1)S(1)}, u32[]{:S(2)}, u32[]{:S(2)}) collective-permute-start(bf16[128,2176]{1,0:T(8,128)(2,1)S(1)} %shard_map.92.refs_0_.refs_10_), channel_id=1, source_target_pairs={{0,4},{4,0},{8,12},{12,8},{16,20},{20,16},{24,28},{28,24},{32,36},... | collective-permute-start | bytes 1671176 | tf_op jit(solution)/shard_map/ppermute | solution.py:300
  54.6 7.2 %collective-permute-start.20 = (bf16[128,2176]{1,0:T(8,128)(2,1)S(1)}, bf16[128,2176]{1,0:T(8,128)(2,1)S(1)}, u32[]{:S(2)}, u32[]{:S(2)}) collective-permute-start(bf16[128,2176]{1,0:T(8,128)(2,1)S(1)} %collective-permute-done.18.refs_1_.refs_11_), channel_id=1, source_target_pairs={{0,4},{4,0},{8,12},{12,8},{16,20},{20,16},{24,28},{28,24},{32,36},... | collective-permute-start | bytes 1671176 | tf_op jit(solution)/shard_map/ppermute | solution.py:300
  75.0 9.3 %collective-permute-start.24 = (f32[2,32,768]{2,1,0:T(8,128)S(1)}, f32[2,32,768]{2,1,0:T(8,128)S(1)}, u32[]{:S(2)}, u32[]{:S(2)}) collective-permute-start(f32[2,32,768]{2,1,0:T(8,128)S(1)} %shard_map.97.refs_0_), channel_id=1, source_target_pairs={{0,1},{1,2},{2,3},{3,0},{4,5},{5,6},{6,7},{7,4},{8,9},{9,10},{10,1... | collective-permute-start | bytes 589832 | tf_op jit(solution)/shard_map/ppermute | solution.py:303
  75.2 12.1 %collective-permute-start.25 = (f32[2,32,768]{2,1,0:T(8,128)S(1)}, f32[2,32,768]{2,1,0:T(8,128)S(1)}, u32[]{:S(2)}, u32[]{:S(2)}) collective-permute-start(f32[2,32,768]{2,1,0:T(8,128)S(1)} %shard_map.97.refs_0_), channel_id=1, source_target_pairs={{0,2},{1,3},{2,0},{3,1},{4,6},{5,7},{6,4},{7,5},{8,10},{9,11},{10,... | collective-permute-start | bytes 589832 | tf_op jit(solution)/shard_map/ppermute | solution.py:303
  78.5 9.3 %collective-permute-start.26 = (f32[2,32,768]{2,1,0:T(8,128)S(1)}, f32[2,32,768]{2,1,0:T(8,128)S(1)}, u32[]{:S(2)}, u32[]{:S(2)}) collective-permute-start(f32[2,32,768]{2,1,0:T(8,128)S(1)} %shard_map.97.refs_0_), channel_id=1, source_target_pairs={{0,3},{1,0},{2,1},{3,2},{4,7},{5,4},{6,5},{7,6},{8,11},{9,8},{10,9... | collective-permute-start | bytes 589832 | tf_op jit(solution)/shard_map/ppermute | solution.py:303
  109.0 11.4 %collective-permute-start.30 = (bf16[2,32,2048]{2,1,0:T(8,128)(2,1)S(1)}, bf16[2,32,2048]{2,1,0:T(8,128)(2,1)S(1)}, u32[]{:S(2)}, u32[]{:S(2)}) collective-permute-start(bf16[2,32,2048]{2,1,0:T(8,128)(2,1)S(1)} %get-tuple-element.53), channel_id=1, source_target_pairs={{0,8},{4,12},{8,16},{12,20},{16,24},{20,28},{24,0},{28,4},{32,40},... | collective-permute-start | bytes 786440 | tf_op jit(solution)/shard_map/ppermute | solution.py:300
  111.8 9.7 %collective-permute-start.31 = (bf16[2,32,2048]{2,1,0:T(8,128)(2,1)S(1)}, bf16[2,32,2048]{2,1,0:T(8,128)(2,1)S(1)}, u32[]{:S(2)}, u32[]{:S(2)}) collective-permute-start(bf16[2,32,2048]{2,1,0:T(8,128)(2,1)S(1)} %get-tuple-element.54), channel_id=1, source_target_pairs={{0,16},{4,20},{8,24},{12,28},{16,0},{20,4},{24,8},{28,12},{32,48},... | collective-permute-start | bytes 786440 | tf_op jit(solution)/shard_map/ppermute | solution.py:300
  112.5 11.6 %collective-permute-start.32 = (bf16[2,32,2048]{2,1,0:T(8,128)(2,1)S(1)}, bf16[2,32,2048]{2,1,0:T(8,128)(2,1)S(1)}, u32[]{:S(2)}, u32[]{:S(2)}) collective-permute-start(bf16[2,32,2048]{2,1,0:T(8,128)(2,1)S(1)} %get-tuple-element.55), channel_id=1, source_target_pairs={{0,24},{4,28},{8,0},{12,4},{16,8},{20,12},{24,16},{28,20},{32,56},... | collective-permute-start | bytes 786440 | tf_op jit(solution)/shard_map/ppermute | solution.py:300
  124.2 7.2 %collective-permute-start.33 = (f32[2,32,512]{2,1,0:T(8,128)S(1)}, f32[2,32,512]{2,1,0:T(8,128)S(1)}, u32[]{:S(2)}, u32[]{:S(2)}) collective-permute-start(f32[2,32,512]{2,1,0:T(8,128)S(1)} %get-tuple-element.56), channel_id=1, source_target_pairs={{0,1},{1,2},{2,3},{3,0},{4,5},{5,6},{6,7},{7,4},{8,9},{9,10},{10,1... | collective-permute-start | bytes 393224 | tf_op jit(solution)/shard_map/ppermute | solution.py:303
  126.3 9.1 %collective-permute-start.34 = (f32[2,32,512]{2,1,0:T(8,128)S(1)}, f32[2,32,512]{2,1,0:T(8,128)S(1)}, u32[]{:S(2)}, u32[]{:S(2)}) collective-permute-start(f32[2,32,512]{2,1,0:T(8,128)S(1)} %get-tuple-element.58), channel_id=1, source_target_pairs={{0,2},{1,3},{2,0},{3,1},{4,6},{5,7},{6,4},{7,5},{8,10},{9,11},{10,... | collective-permute-start | bytes 393224 | tf_op jit(solution)/shard_map/ppermute | solution.py:303
  (18 other events, 211.7 us)

commit v2 on v1

--- a/solution.py
+++ b/solution.py
@@ -360,9 +360,18 @@
     def ring(k, p, q):
         return [((k, 1), p), ((k, 0), q), ((-k, 0), swap(p)), ((-k, 1), swap(q))]
 
+    lefts = [lt] + [shift_y(lt, d) for d in range(1, ny)]
+    left_full, mom = call(
+        momentum_kernel,
+        [shaped((local, rank, ff))] * 2,
+        (meta, st, momentum_right, *lefts),
+        specs=[SMEM] + [VMEM] * (2 + ny),
+        scratch=[pltpu.VMEM((ny, local, rank, ff // ny), F32)],
+    )
     p = along(mine)
     sibling = swap(mine)
     q = along(sibling)
+    [p], [q] = after([p], lefts[1]), after([q], lefts[2])
     near = [shift(two, dx=-1), shift(two, dx=1)]
     first = [((0, 1), mine), ((0, 0), sibling)] + ring(1, p, q)
     farther, token = call(
@@ -372,22 +381,14 @@
         specs=[SMEM, VMEM, VMEM],
     )
     far = along(farther, "x")
-    lefts = [lt] + [shift_y(lt, d) for d in range(1, ny)]
-    left_full, mom = call(
-        momentum_kernel,
-        [shaped((local, rank, ff))] * 2,
-        (meta, st, momentum_right, *lefts),
-        specs=[SMEM] + [VMEM] * (2 + ny),
-        scratch=[pltpu.VMEM((ny, local, rank, ff // ny), F32)],
-    )
-    [p], q = after([along(p)], token, mom), along(q)
+    [p], q = after([along(p)], token, *lefts[3:]), along(q)
     second = ring(2, p, q)
     a = project(first, [two, near[0], far, near[1]], [])
     all_s = [a[4]]
-    [p], q = after([along(p)], a[3]), along(q)
+    p, q = along(p), along(q)
     third = ring(3, p, q)
     b = project(second, all_s, a[2])
-    [p] = after([along(p)], b[3])
+    [p] = after([along(p)], b[3], mom)
     fourth = [((4, 1), p), ((4, 0), swap(p))]
     e = project(third, all_s, b[2])
     f = project(fourth, all_s, e[2], nx)

time: 137 us -> 132 us (0.964)
  waiting for transfers between devices: 59.9 us -> 45.1 us
  starting transfers between devices: 39.9 us -> 49.9 us
    ppermute x19, starting transfers between devices: 14 us -> 23.9 us  [shift(): return lax.ppermute(v, 'expert', pairs)]
    ppermute x8, waiting for transfers between devices: 17 us -> 9.4 us  [along(): return lax.ppermute(v, 'expert', pairs)]
    ppermute x9, waiting for transfers between devices: 24.4 us -> 18.4 us  [shift_y(): return lax.ppermute(v, 'zero', [(a, (a + dy) % ny) for a in range(ny)])]
    ppermute x9, starting transfers between devices: 14.4 us -> 18.3 us  [shift_y(): return lax.ppermute(v, 'zero', [(a, (a + dy) % ny) for a in range(ny)])]
    ppermute x8, starting transfers between devices: 11.5 us -> 7.74 us  [along(): return lax.ppermute(v, 'expert', pairs)]
    pallas_call x15 -> x16, Pallas kernels: 33.4 us -> 34.1 us  [call(): pl.pallas_call(kernel, out_shape=outs, in_specs=specs or [VMEM] * len(arg...]
  transfers between devices with their start and end apart: 36 -> 36, of which waited for: 21 -> 15; matrix products, arithmetic and copies ran while one was open for 0% -> 0% of each run, Pallas kernels for 10% -> 12%
where the time goes in v2:
time: 132 us
  starting transfers between devices  49.9 us (38%)
  waiting for transfers between devices  45.1 us (34%)
  Pallas kernels  34.1 us (26%)
    pallas_call x16, Pallas kernels, call(): pl.pallas_call(kernel, out_shape=outs, in_specs=specs or [VMEM] * len(arg...  34.1 us
    ppermute x19, starting transfers between devices, shift(): return lax.ppermute(v, 'expert', pairs)  23.9 us
    ppermute x9, waiting for transfers between devices, shift_y(): return lax.ppermute(v, 'zero', [(a, (a + dy) % ny) for a in range(ny)])  18.4 us
    ppermute x9, starting transfers between devices, shift_y(): return lax.ppermute(v, 'zero', [(a, (a + dy) % ny) for a in range(ny)])  18.3 us
    ppermute x19, waiting for transfers between devices, shift(): return lax.ppermute(v, 'expert', pairs)  17.3 us
    ppermute x8, waiting for transfers between devices, along(): return lax.ppermute(v, 'expert', pairs)  9.4 us
    ppermute x8, starting transfers between devices, along(): return lax.ppermute(v, 'expert', pairs)  7.74 us
  transfers between devices with their start and end apart: 36, of which 15 were waited for; matrix products, arithmetic and copies ran while one was open for 0% of the time, Pallas kernels for 12%

profile of v2, /device:TPU:6, one launch (start us, length us, event | category | flops | bytes accessed | tf_op | source)
XLA Modules:
  0.0 131.9 jit_solution(10392919768643693475)
XLA Ops:
  10.5 2.4 %collective-permute-start.4 = (bf16[2,64,2048]{2,1,0:T(8,128)(2,1)S(1)}, bf16[2,64,2048]{2,1,0:T(8,128)(2,1)}, u32[]{:S(2)}, u32[]{:S(2)}) collective-permute-start(bf16[2,64,2048]{2,1,0:T(8,128)(2,1)S(1)} %shard_map.88.refs_6_), channel_id=1, source_target_pairs={{0,8},{4,12},{8,16},{12,20},{16,24},{20,28},{24,0},{28,4},{32,40},... | collective-permute-start | bytes 1572872 | tf_op jit(solution)/shard_map/ppermute | solution.py:300
  13.0 3.4 %collective-permute-done.refs_0_ = bf16[128,2176]{1,0:T(8,128)(2,1)S(1)} collective-permute-done((bf16[128,2176]{1,0:T(8,128)(2,1)}, bf16[128,2176]{1,0:T(8,128)(2,1)S(1)}, u32[]{:S(2)}, u32[]{:S(2)}) %collective-permute-start) | collective-permute-done | bytes 557088 | tf_op jit(solution)/shard_map/ppermute | solution.py:338
  16.5 3.3 %collective-permute-start.10 = (f32[2,32,192]{2,1,0:T(8,128)}, f32[2,32,192]{2,1,0:T(8,128)S(1)}, u32[]{:S(2)}, u32[]{:S(2)}) collective-permute-start(f32[2,32,192]{2,1,0:T(8,128)} %bitcast.6.refs_0_), channel_id=1, source_target_pairs={{0,2},{1,3},{2,0},{3,1},{4,6},{5,7},{6,4},{7,5},{8,10},{9,11},{10,... | collective-permute-start | bytes 147464 | tf_op jit(solution)/shard_map/ppermute | solution.py:303
  19.8 2.8 %collective-permute-done.10.refs_1_.refs_2_ = f32[2,32,192]{2,1,0:T(8,128)S(1)} collective-permute-done((f32[2,32,192]{2,1,0:T(8,128)}, f32[2,32,192]{2,1,0:T(8,128)S(1)}, u32[]{:S(2)}, u32[]{:S(2)}) %collective-permute-start.10) | collective-permute-done | bytes 49184 | tf_op jit(solution)/shard_map/ppermute | solution.py:303
  26.0 3.0 %collective-permute-start.5 = (f32[2,32,192]{2,1,0:T(8,128)}, f32[2,32,192]{2,1,0:T(8,128)S(1)}, u32[]{:S(2)}, u32[]{:S(2)}) collective-permute-start(f32[2,32,192]{2,1,0:T(8,128)} %bitcast.6.refs_0_), channel_id=1, source_target_pairs={{0,3},{1,0},{2,1},{3,2},{4,7},{5,4},{6,5},{7,6},{8,11},{9,8},{10,9... | collective-permute-start | bytes 147464 | tf_op jit(solution)/shard_map/ppermute | solution.py:303
  31.2 2.4 %collective-permute-start.6 = (bf16[128,2176]{1,0:T(8,128)(2,1)S(1)}, bf16[128,2176]{1,0:T(8,128)(2,1)S(1)}, u32[]{:S(2)}, u32[]{:S(2)}) collective-permute-start(bf16[128,2176]{1,0:T(8,128)(2,1)S(1)} %shard_map.90.refs_0_.refs_6_), channel_id=1, source_target_pairs={{0,32},{4,228},{8,40},{12,236},{16,48},{20,244},{24,56},{28,252},{... | collective-permute-start | bytes 1671176 | tf_op jit(solution)/shard_map/ppermute | solution.py:338
  33.7 2.7 %collective-permute-start.15 = (bf16[128,2176]{1,0:T(8,128)(2,1)S(1)}, bf16[128,2176]{1,0:T(8,128)(2,1)S(1)}, u32[]{:S(2)}, u32[]{:S(2)}) collective-permute-start(bf16[128,2176]{1,0:T(8,128)(2,1)S(1)} %shard_map.91.refs_3_), channel_id=1, source_target_pairs={{0,4},{4,0},{8,12},{12,8},{16,20},{20,16},{24,28},{28,24},{32,36},... | collective-permute-start | bytes 1671176 | tf_op jit(solution)/shard_map/ppermute | solution.py:300
  37.0 5.9 %collective-permute-done.6.refs_0_.refs_10_ = bf16[128,2176]{1,0:T(8,128)(2,1)S(1)} collective-permute-done((bf16[128,2176]{1,0:T(8,128)(2,1)S(1)}, bf16[128,2176]{1,0:T(8,128)(2,1)S(1)}, u32[]{:S(2)}, u32[]{:S(2)}) %collective-permute-start.6) | collective-permute-done | bytes 557088 | tf_op jit(solution)/shard_map/ppermute | solution.py:338
  45.4 2.5 %collective-permute-start.19 = (bf16[128,2176]{1,0:T(8,128)(2,1)S(1)}, bf16[128,2176]{1,0:T(8,128)(2,1)S(1)}, u32[]{:S(2)}, u32[]{:S(2)}) collective-permute-start(bf16[128,2176]{1,0:T(8,128)(2,1)S(1)} %collective-permute-done.6.refs_0_.refs_10_), channel_id=1, source_target_pairs={{0,4},{4,0},{8,12},{12,8},{16,20},{20,16},{24,28},{28,24},{32,36},... | collective-permute-start | bytes 1671176 | tf_op jit(solution)/shard_map/ppermute | solution.py:300
  47.9 5.1 %shard_map.92 = (f32[8,32,256]{2,1,0:T(8,128)S(1)}, bf16[512,2048]{1,0:T(8,128)(2,1)S(1)}, f32[96,128]{1,0:T(8,128)S(1)}) custom-call(s32[4]{0:T(128)S(1)} %pad_add_fusion.meta_ref, bf16[128,2176]{1,0:T(8,128)(2,1)S(1)} %copy-done.3, bf16[128,2176]{1,0:T(8,128)(2,1)} %collective-permute-done.8.refs_1_, bf16[128,2176]{1,0:T(8,128)(2,1)S(1)} %shard_map.87.refs_2_, ...), custom_call_target="tpu_custom_call" | custom-call | flops 1610612736 | bytes 3221225 | tf_op jit(solution)/shard_map/pallas_call | solution.py:45
  53.2 2.4 %shard_map.93 = (f32[8,32,256]{2,1,0:T(8,128)S(1)}, f32[64,128]{1,0:T(8,128)S(1)}) custom-call(s32[4]{0:T(128)S(1)} %pad_add_fusion.meta_ref, bf16[128,2176]{1,0:T(8,128)(2,1)S(1)} %shard_map.90.refs_0_.refs_6_, bf16[128,2176]{1,0:T(8,128)(2,1)S(1)} %collective-permute-done.11.refs_1_.refs_7_, bf16[128,2176]{1,0:T(8,128)(2,1)S(1)} %collective-permute-done.12.refs_2_.refs_8_, ...), custom_call_target="tpu_custom_call" | custom-call | flops 1073741824 | bytes 2147483 | tf_op jit(solution)/shard_map/pallas_call | solution.py:45
  56.2 2.4 %shard_map.96 = (f32[8,32,256]{2,1,0:T(8,128)S(1)}, f32[64,128]{1,0:T(8,128)S(1)}) custom-call(s32[4]{0:T(128)S(1)} %pad_add_fusion.meta_ref, bf16[128,2176]{1,0:T(8,128)(2,1)S(1)} %collective-permute-done.6.refs_0_.refs_10_, bf16[128,2176]{1,0:T(8,128)(2,1)S(1)} %collective-permute-done.18.refs_1_.refs_11_, ...), custom_call_target="tpu_custom_call" | custom-call | flops 1073741824 | bytes 2147483 | tf_op jit(solution)/shard_map/pallas_call | solution.py:45
  65.4 3.9 %collective-permute-done.22.refs_2_ = f32[2,32,256]{2,1,0:T(8,128)S(1)} collective-permute-done((f32[2,32,256]{2,1,0:T(8,128)S(1)}, f32[2,32,256]{2,1,0:T(8,128)S(1)}, u32[]{:S(2)}, u32[]{:S(2)}) %collective-permute-start.22) | collective-permute-done | bytes 65568 | tf_op jit(solution)/shard_map/ppermute | solution.py:300
  72.9 2.8 %collective-permute-start.25 = (f32[2,32,768]{2,1,0:T(8,128)S(1)}, f32[2,32,768]{2,1,0:T(8,128)S(1)}, u32[]{:S(2)}, u32[]{:S(2)}) collective-permute-start(f32[2,32,768]{2,1,0:T(8,128)S(1)} %shard_map.98.refs_0_), channel_id=1, source_target_pairs={{0,2},{1,3},{2,0},{3,1},{4,6},{5,7},{6,4},{7,5},{8,10},{9,11},{10,... | collective-permute-start | bytes 589832 | tf_op jit(solution)/shard_map/ppermute | solution.py:303
  76.8 2.3 %collective-permute-done.24.refs_1_ = f32[2,32,768]{2,1,0:T(8,128)S(1)} collective-permute-done((f32[2,32,768]{2,1,0:T(8,128)S(1)}, f32[2,32,768]{2,1,0:T(8,128)S(1)}, u32[]{:S(2)}, u32[]{:S(2)}) %collective-permute-start.24) | collective-permute-done | bytes 196640 | tf_op jit(solution)/shard_map/ppermute | solution.py:303
  79.2 5.3 %collective-permute-done.25.refs_2_ = f32[2,32,768]{2,1,0:T(8,128)S(1)} collective-permute-done((f32[2,32,768]{2,1,0:T(8,128)S(1)}, f32[2,32,768]{2,1,0:T(8,128)S(1)}, u32[]{:S(2)}, u32[]{:S(2)}) %collective-permute-start.25) | collective-permute-done | bytes 196640 | tf_op jit(solution)/shard_map/ppermute | solution.py:303
  84.5 5.3 %shard_map.99 = (f32[2,32,768]{2,1,0:T(8,128)S(1)}, f32[2,32,256]{2,1,0:T(8,128)S(1)}, f32[2,32,256]{2,1,0:T(8,128)S(1)}, f32[2,32,256]{2,1,0:T(8,128)S(1)}, f32[2,32,256]{2,1,0:T(8,128)S(1)}) custom-call(s32[4]{0:T(128)S(1)} %pad_add_fusion.meta_ref, f32[2,32,768]{2,1,0:T(8,128)S(1)} %shard_map.98.refs_0_, ...), custom_call_target="tpu_custom_call" | custom-call | tf_op jit(solution)/shard_map/pallas_call | solution.py:45
  91.5 2.5 %collective-permute-start.29 = (f32[2,32,256]{2,1,0:T(8,128)S(1)}, f32[2,32,256]{2,1,0:T(8,128)S(1)}, u32[]{:S(2)}, u32[]{:S(2)}) collective-permute-start(f32[2,32,256]{2,1,0:T(8,128)S(1)} %get-tuple-element.47), channel_id=1, source_target_pairs={{0,8},{4,12},{8,16},{12,20},{16,24},{20,28},{24,0},{28,4},{32,40},... | collective-permute-start | bytes 196616 | tf_op jit(solution)/shard_map/ppermute | solution.py:300
  96.8 8.4 %shard_map.101 = (f32[2,32,2048]{2,1,0:T(8,128)S(1)}, bf16[2,32,2048]{2,1,0:T(8,128)(2,1)S(1)}, bf16[2,32,2048]{2,1,0:T(8,128)(2,1)S(1)}, bf16[2,32,2048]{2,1,0:T(8,128)(2,1)S(1)}) custom-call(bf16[128,2176]{1,0:T(8,128)(2,1)S(1)} %copy-done.3, bf16[128,2176]{1,0:T(8,128)(2,1)} %collective-permute-done.8.refs_1_, bf16[128,2176]{1,0:T(8,128)(2,1)S(1)} %shard_map.87.refs_2_, ...), custom_call_target="tpu_custom_call" | custom-call | flops 4294967296 | bytes 8589934 | tf_op jit(solution)/shard_map/pallas_call | solution.py:45
  105.3 2.8 %collective-permute-start.30 = (bf16[2,32,2048]{2,1,0:T(8,128)(2,1)S(1)}, bf16[2,32,2048]{2,1,0:T(8,128)(2,1)S(1)}, u32[]{:S(2)}, u32[]{:S(2)}) collective-permute-start(bf16[2,32,2048]{2,1,0:T(8,128)(2,1)S(1)} %get-tuple-element.53), channel_id=1, source_target_pairs={{0,8},{4,12},{8,16},{12,20},{16,24},{20,28},{24,0},{28,4},{32,40},... | collective-permute-start | bytes 786440 | tf_op jit(solution)/shard_map/ppermute | solution.py:300
  109.0 7.8 %collective-permute-done.30 = bf16[2,32,2048]{2,1,0:T(8,128)(2,1)S(1)} collective-permute-done((bf16[2,32,2048]{2,1,0:T(8,128)(2,1)S(1)}, bf16[2,32,2048]{2,1,0:T(8,128)(2,1)S(1)}, u32[]{:S(2)}, u32[]{:S(2)}) %collective-permute-start.30) | collective-permute-done | bytes 262176 | tf_op jit(solution)/shard_map/ppermute | solution.py:300
  117.8 2.7 %collective-permute-done.32 = bf16[2,32,2048]{2,1,0:T(8,128)(2,1)S(1)} collective-permute-done((bf16[2,32,2048]{2,1,0:T(8,128)(2,1)S(1)}, bf16[2,32,2048]{2,1,0:T(8,128)(2,1)S(1)}, u32[]{:S(2)}, u32[]{:S(2)}) %collective-permute-start.32) | collective-permute-done | bytes 262176 | tf_op jit(solution)/shard_map/ppermute | solution.py:300
  122.4 2.8 %collective-permute-start.34 = (f32[2,32,512]{2,1,0:T(8,128)S(1)}, f32[2,32,512]{2,1,0:T(8,128)S(1)}, u32[]{:S(2)}, u32[]{:S(2)}) collective-permute-start(f32[2,32,512]{2,1,0:T(8,128)S(1)} %get-tuple-element.58), channel_id=1, source_target_pairs={{0,2},{1,3},{2,0},{3,1},{4,6},{5,7},{6,4},{7,5},{8,10},{9,11},{10,... | collective-permute-start | bytes 393224 | tf_op jit(solution)/shard_map/ppermute | solution.py:303
  127.3 3.9 %collective-permute-done.34 = f32[2,32,512]{2,1,0:T(8,128)S(1)} collective-permute-done((f32[2,32,512]{2,1,0:T(8,128)S(1)}, f32[2,32,512]{2,1,0:T(8,128)S(1)}, u32[]{:S(2)}, u32[]{:S(2)}) %collective-permute-start.34) | collective-permute-done | bytes 131104 | tf_op jit(solution)/shard_map/ppermute | solution.py:303
  (78 shorter events, 42.1 us)
Async XLA Ops:
  2.7 13.7 %collective-permute-start = (bf16[128,2176]{1,0:T(8,128)(2,1)}, bf16[128,2176]{1,0:T(8,128)(2,1)S(1)}, u32[]{:S(2)}, u32[]{:S(2)}) collective-permute-start(bf16[128,2176]{1,0:T(8,128)(2,1)} %shard_map.86.refs_0_), channel_id=1, source_target_pairs={{0,32},{4,228},{8,40},{12,236},{16,48},{20,244},{24,56},{28,252},{... | collective-permute-start | bytes 1671176 | tf_op jit(solution)/shard_map/ppermute | solution.py:338
  5.0 18.9 %collective-permute-start.9 = (bf16[128,2176]{1,0:T(8,128)(2,1)}, bf16[128,2176]{1,0:T(8,128)(2,1)S(1)}, u32[]{:S(2)}, u32[]{:S(2)}) collective-permute-start(bf16[128,2176]{1,0:T(8,128)(2,1)} %collective-permute-done.8.refs_1_), channel_id=1, source_target_pairs={{0,32},{4,228},{8,40},{12,236},{16,48},{20,244},{24,56},{28,252},{... | collective-permute-start | bytes 1671176 | tf_op jit(solution)/shard_map/ppermute | solution.py:338
  9.6 14.5 %collective-permute-start.3 = (bf16[2,64,2048]{2,1,0:T(8,128)(2,1)S(1)}, bf16[2,64,2048]{2,1,0:T(8,128)(2,1)}, u32[]{:S(2)}, u32[]{:S(2)}) collective-permute-start(bf16[2,64,2048]{2,1,0:T(8,128)(2,1)S(1)} %shard_map.88.refs_6_), channel_id=1, source_target_pairs={{0,24},{4,28},{8,0},{12,4},{16,8},{20,12},{24,16},{28,20},{32,56},... | collective-permute-start | bytes 1572872 | tf_op jit(solution)/shard_map/ppermute | solution.py:300
  10.5 13.6 %collective-permute-start.4 = (bf16[2,64,2048]{2,1,0:T(8,128)(2,1)S(1)}, bf16[2,64,2048]{2,1,0:T(8,128)(2,1)}, u32[]{:S(2)}, u32[]{:S(2)}) collective-permute-start(bf16[2,64,2048]{2,1,0:T(8,128)(2,1)S(1)} %shard_map.88.refs_6_), channel_id=1, source_target_pairs={{0,8},{4,12},{8,16},{12,20},{16,24},{20,28},{24,0},{28,4},{32,40},... | collective-permute-start | bytes 1572872 | tf_op jit(solution)/shard_map/ppermute | solution.py:300
  16.4 14.8 %collective-permute-start.2 = (bf16[128,2176]{1,0:T(8,128)(2,1)S(1)}, bf16[128,2176]{1,0:T(8,128)(2,1)S(1)}, u32[]{:S(2)}, u32[]{:S(2)}) collective-permute-start(bf16[128,2176]{1,0:T(8,128)(2,1)S(1)} %shard_map.87.refs_2_), channel_id=1, source_target_pairs={{0,32},{4,228},{8,40},{12,236},{16,48},{20,244},{24,56},{28,252},{... | collective-permute-start | bytes 1671176 | tf_op jit(solution)/shard_map/ppermute | solution.py:338
  22.6 14.2 %collective-permute-start.14 = (bf16[128,2176]{1,0:T(8,128)(2,1)S(1)}, bf16[128,2176]{1,0:T(8,128)(2,1)S(1)}, u32[]{:S(2)}, u32[]{:S(2)}) collective-permute-start(bf16[128,2176]{1,0:T(8,128)(2,1)S(1)} %shard_map.87.refs_2_), channel_id=1, source_target_pairs={{0,4},{4,0},{8,12},{12,8},{16,20},{20,16},{24,28},{28,24},{32,36},... | collective-permute-start | bytes 1671176 | tf_op jit(solution)/shard_map/ppermute | solution.py:300
  24.0 12.4 %collective-permute-start.11 = (bf16[128,2176]{1,0:T(8,128)(2,1)S(1)}, bf16[128,2176]{1,0:T(8,128)(2,1)S(1)}, u32[]{:S(2)}, u32[]{:S(2)}) collective-permute-start(bf16[128,2176]{1,0:T(8,128)(2,1)S(1)} %shard_map.91.refs_3_), channel_id=1, source_target_pairs={{0,32},{4,228},{8,40},{12,236},{16,48},{20,244},{24,56},{28,252},{... | collective-permute-start | bytes 1671176 | tf_op jit(solution)/shard_map/ppermute | solution.py:338
  25.4 11.0 %collective-permute-start.16 = (bf16[2,64,2048]{2,1,0:T(8,128)(2,1)S(1)}, bf16[2,64,2048]{2,1,0:T(8,128)(2,1)S(1)}, u32[]{:S(2)}, u32[]{:S(2)}) collective-permute-start(bf16[2,64,2048]{2,1,0:T(8,128)(2,1)S(1)} %get-tuple-element.30), channel_id=1, source_target_pairs={{0,24},{4,12},{8,0},{12,20},{16,8},{20,28},{24,16},{28,4},{32,56},... | collective-permute-start | bytes 1572872 | tf_op jit(solution)/shard_map/ppermute | solution.py:338
  31.2 11.7 %collective-permute-start.6 = (bf16[128,2176]{1,0:T(8,128)(2,1)S(1)}, bf16[128,2176]{1,0:T(8,128)(2,1)S(1)}, u32[]{:S(2)}, u32[]{:S(2)}) collective-permute-start(bf16[128,2176]{1,0:T(8,128)(2,1)S(1)} %shard_map.90.refs_0_.refs_6_), channel_id=1, source_target_pairs={{0,32},{4,228},{8,40},{12,236},{16,48},{20,244},{24,56},{28,252},{... | collective-permute-start | bytes 1671176 | tf_op jit(solution)/shard_map/ppermute | solution.py:338
  33.7 11.7 %collective-permute-start.15 = (bf16[128,2176]{1,0:T(8,128)(2,1)S(1)}, bf16[128,2176]{1,0:T(8,128)(2,1)S(1)}, u32[]{:S(2)}, u32[]{:S(2)}) collective-permute-start(bf16[128,2176]{1,0:T(8,128)(2,1)S(1)} %shard_map.91.refs_3_), channel_id=1, source_target_pairs={{0,4},{4,0},{8,12},{12,8},{16,20},{20,16},{24,28},{28,24},{32,36},... | collective-permute-start | bytes 1671176 | tf_op jit(solution)/shard_map/ppermute | solution.py:300
  36.4 16.6 %collective-permute-start.18 = (bf16[128,2176]{1,0:T(8,128)(2,1)S(1)}, bf16[128,2176]{1,0:T(8,128)(2,1)S(1)}, u32[]{:S(2)}, u32[]{:S(2)}) collective-permute-start(bf16[128,2176]{1,0:T(8,128)(2,1)S(1)} %collective-permute-done.11.refs_1_.refs_7_), channel_id=1, source_target_pairs={{0,32},{4,228},{8,40},{12,236},{16,48},{20,244},{24,56},{28,252},{... | collective-permute-start | bytes 1671176 | tf_op jit(solution)/shard_map/ppermute | solution.py:338
  36.5 16.7 %collective-permute-start.12 = (bf16[128,2176]{1,0:T(8,128)(2,1)S(1)}, bf16[128,2176]{1,0:T(8,128)(2,1)S(1)}, u32[]{:S(2)}, u32[]{:S(2)}) collective-permute-start(bf16[128,2176]{1,0:T(8,128)(2,1)S(1)} %shard_map.90.refs_0_.refs_6_), channel_id=1, source_target_pairs={{0,4},{4,0},{8,12},{12,8},{16,20},{20,16},{24,28},{28,24},{32,36},... | collective-permute-start | bytes 1671176 | tf_op jit(solution)/shard_map/ppermute | solution.py:300
  36.8 16.3 %collective-permute-start.13 = (bf16[128,2176]{1,0:T(8,128)(2,1)S(1)}, bf16[128,2176]{1,0:T(8,128)(2,1)S(1)}, u32[]{:S(2)}, u32[]{:S(2)}) collective-permute-start(bf16[128,2176]{1,0:T(8,128)(2,1)S(1)} %collective-permute-done.11.refs_1_.refs_7_), channel_id=1, source_target_pairs={{0,4},{4,0},{8,12},{12,8},{16,20},{20,16},{24,28},{28,24},{32,36},... | collective-permute-start | bytes 1671176 | tf_op jit(solution)/shard_map/ppermute | solution.py:300
  42.9 12.6 %collective-permute-start.7 = (bf16[128,2176]{1,0:T(8,128)(2,1)S(1)}, bf16[128,2176]{1,0:T(8,128)(2,1)S(1)}, u32[]{:S(2)}, u32[]{:S(2)}) collective-permute-start(bf16[128,2176]{1,0:T(8,128)(2,1)S(1)} %collective-permute-done.6.refs_0_.refs_10_), channel_id=1, source_target_pairs={{0,32},{4,228},{8,40},{12,236},{16,48},{20,244},{24,56},{28,252},{... | collective-permute-start | bytes 1671176 | tf_op jit(solution)/shard_map/ppermute | solution.py:338
  45.4 10.8 %collective-permute-start.19 = (bf16[128,2176]{1,0:T(8,128)(2,1)S(1)}, bf16[128,2176]{1,0:T(8,128)(2,1)S(1)}, u32[]{:S(2)}, u32[]{:S(2)}) collective-permute-start(bf16[128,2176]{1,0:T(8,128)(2,1)S(1)} %collective-permute-done.6.refs_0_.refs_10_), channel_id=1, source_target_pairs={{0,4},{4,0},{8,12},{12,8},{16,20},{20,16},{24,28},{28,24},{32,36},... | collective-permute-start | bytes 1671176 | tf_op jit(solution)/shard_map/ppermute | solution.py:300
  62.8 6.5 %collective-permute-start.22 = (f32[2,32,256]{2,1,0:T(8,128)S(1)}, f32[2,32,256]{2,1,0:T(8,128)S(1)}, u32[]{:S(2)}, u32[]{:S(2)}) collective-permute-start(f32[2,32,256]{2,1,0:T(8,128)S(1)} %get-tuple-element.39), channel_id=1, source_target_pairs={{0,16},{4,20},{8,24},{12,28},{16,0},{20,4},{24,8},{28,12},{32,48},... | collective-permute-start | bytes 196616 | tf_op jit(solution)/shard_map/ppermute | solution.py:300
  71.2 7.9 %collective-permute-start.24 = (f32[2,32,768]{2,1,0:T(8,128)S(1)}, f32[2,32,768]{2,1,0:T(8,128)S(1)}, u32[]{:S(2)}, u32[]{:S(2)}) collective-permute-start(f32[2,32,768]{2,1,0:T(8,128)S(1)} %shard_map.98.refs_0_), channel_id=1, source_target_pairs={{0,1},{1,2},{2,3},{3,0},{4,5},{5,6},{6,7},{7,4},{8,9},{9,10},{10,1... | collective-permute-start | bytes 589832 | tf_op jit(solution)/shard_map/ppermute | solution.py:303
  72.9 11.6 %collective-permute-start.25 = (f32[2,32,768]{2,1,0:T(8,128)S(1)}, f32[2,32,768]{2,1,0:T(8,128)S(1)}, u32[]{:S(2)}, u32[]{:S(2)}) collective-permute-start(f32[2,32,768]{2,1,0:T(8,128)S(1)} %shard_map.98.refs_0_), channel_id=1, source_target_pairs={{0,2},{1,3},{2,0},{3,1},{4,6},{5,7},{6,4},{7,5},{8,10},{9,11},{10,... | collective-permute-start | bytes 589832 | tf_op jit(solution)/shard_map/ppermute | solution.py:303
  75.7 8.8 %collective-permute-start.26 = (f32[2,32,768]{2,1,0:T(8,128)S(1)}, f32[2,32,768]{2,1,0:T(8,128)S(1)}, u32[]{:S(2)}, u32[]{:S(2)}) collective-permute-start(f32[2,32,768]{2,1,0:T(8,128)S(1)} %shard_map.98.refs_0_), channel_id=1, source_target_pairs={{0,3},{1,0},{2,1},{3,2},{4,7},{5,4},{6,5},{7,6},{8,11},{9,8},{10,9... | collective-permute-start | bytes 589832 | tf_op jit(solution)/shard_map/ppermute | solution.py:303
  105.3 11.6 %collective-permute-start.30 = (bf16[2,32,2048]{2,1,0:T(8,128)(2,1)S(1)}, bf16[2,32,2048]{2,1,0:T(8,128)(2,1)S(1)}, u32[]{:S(2)}, u32[]{:S(2)}) collective-permute-start(bf16[2,32,2048]{2,1,0:T(8,128)(2,1)S(1)} %get-tuple-element.53), channel_id=1, source_target_pairs={{0,8},{4,12},{8,16},{12,20},{16,24},{20,28},{24,0},{28,4},{32,40},... | collective-permute-start | bytes 786440 | tf_op jit(solution)/shard_map/ppermute | solution.py:300
  108.0 9.8 %collective-permute-start.31 = (bf16[2,32,2048]{2,1,0:T(8,128)(2,1)S(1)}, bf16[2,32,2048]{2,1,0:T(8,128)(2,1)S(1)}, u32[]{:S(2)}, u32[]{:S(2)}) collective-permute-start(bf16[2,32,2048]{2,1,0:T(8,128)(2,1)S(1)} %get-tuple-element.54), channel_id=1, source_target_pairs={{0,16},{4,20},{8,24},{12,28},{16,0},{20,4},{24,8},{28,12},{32,48},... | collective-permute-start | bytes 786440 | tf_op jit(solution)/shard_map/ppermute | solution.py:300
  108.7 11.8 %collective-permute-start.32 = (bf16[2,32,2048]{2,1,0:T(8,128)(2,1)S(1)}, bf16[2,32,2048]{2,1,0:T(8,128)(2,1)S(1)}, u32[]{:S(2)}, u32[]{:S(2)}) collective-permute-start(bf16[2,32,2048]{2,1,0:T(8,128)(2,1)S(1)} %get-tuple-element.55), channel_id=1, source_target_pairs={{0,24},{4,28},{8,0},{12,4},{16,8},{20,12},{24,16},{28,20},{32,56},... | collective-permute-start | bytes 786440 | tf_op jit(solution)/shard_map/ppermute | solution.py:300
  120.7 6.6 %collective-permute-start.33 = (f32[2,32,512]{2,1,0:T(8,128)S(1)}, f32[2,32,512]{2,1,0:T(8,128)S(1)}, u32[]{:S(2)}, u32[]{:S(2)}) collective-permute-start(f32[2,32,512]{2,1,0:T(8,128)S(1)} %get-tuple-element.56), channel_id=1, source_target_pairs={{0,1},{1,2},{2,3},{3,0},{4,5},{5,6},{6,7},{7,4},{8,9},{9,10},{10,1... | collective-permute-start | bytes 393224 | tf_op jit(solution)/shard_map/ppermute | solution.py:303
  122.4 8.8 %collective-permute-start.34 = (f32[2,32,512]{2,1,0:T(8,128)S(1)}, f32[2,32,512]{2,1,0:T(8,128)S(1)}, u32[]{:S(2)}, u32[]{:S(2)}) collective-permute-start(f32[2,32,512]{2,1,0:T(8,128)S(1)} %get-tuple-element.58), channel_id=1, source_target_pairs={{0,2},{1,3},{2,0},{3,1},{4,6},{5,7},{6,4},{7,5},{8,10},{9,11},{10,... | collective-permute-start | bytes 393224 | tf_op jit(solution)/shard_map/ppermute | solution.py:303
  (17 other events, 199.3 us)

commit v3 on v2

--- a/solution.py
+++ b/solution.py
@@ -193,7 +193,7 @@
             h = h_ref[i, :, lax.rem(meta_ref[1] - d + nd, nd)]
             h = h.reshape(-1, h.shape[-1])
             total = total + folded(dot(stacked(parts[d][i]), h))
-        out_ref[i] = total
+        out_ref[i] = total.astype(out_ref.dtype)
 
 
 def basis_kernel(ny, nd, meta_ref, *refs):
@@ -203,9 +203,9 @@
     lane = lax.broadcasted_iota(jnp.int32, (rank, 2 * rank), 1)
     sk, work = [], []
     for i in range(count):
-        s = parts[0][i]
+        s = parts[0][i].astype(F32)
         for d in range(1, ny):
-            s = s + parts[d][i]
+            s = s + parts[d][i].astype(F32)
         sk.append(s)
         both = jnp.concatenate([jnp.zeros_like(s), s], axis=0)
         a = dot(s, both, NT, HIGHEST) / ff
@@ -213,9 +213,10 @@
     for j in range(rank):
         for i in range(count):
             a = work[i]
-            pivot = a[j : j + 1, rank + j : rank + j + 1]
-            factor = a[:, rank + j : rank + j + 1] / pivot
-            work[i] = a - jnp.where(row > j, factor, 0.0) * a[j : j + 1]
+            line = a[j : j + 1]
+            pivot = jnp.broadcast_to(line[:, rank + j : rank + j + 1], line.shape)
+            column = jnp.broadcast_to(a[:, rank + j : rank + j + 1], a.shape)
+            work[i] = a - jnp.where(row > j, column, 0.0) * (line / pivot)
     for i in range(count):
         diag = jnp.sum(jnp.where(lane == row + rank, work[i], 0.0), axis=1, keepdims=True)
         inverse = (work[i] / jnp.sqrt(diag))[:, :rank]
@@ -400,7 +401,7 @@
     h = hidden.reshape(local, nz, nx, nc * CAP, ff)
     part = call(
         functools.partial(sum_kernel, nx),
-        shaped((local, rank, ff)),
+        shaped((local, rank, ff), BF),
         (meta, *products, h, mom),
         specs=[SMEM] + [VMEM] * (nx + 2),
         limit=NARROW,

time: 132 us -> 127 us (0.962)
  waiting for transfers between devices: 45.1 us -> 39.7 us
    ppermute x9, waiting for transfers between devices: 18.4 us -> 13 us  [shift_y(): return lax.ppermute(v, 'zero', [(a, (a + dy) % ny) for a in range(ny)])]
  transfers between devices with their start and end apart: 36 -> 36, of which waited for: 15 -> 17; matrix products, arithmetic and copies ran while one was open for 0% -> 0% of each run, Pallas kernels for 12% -> 12%
where the time goes in v3:
time: 127 us
  starting transfers between devices  49.8 us (39%)
  waiting for transfers between devices  39.7 us (31%)
  Pallas kernels  34.2 us (27%)
    pallas_call x16, Pallas kernels, call(): pl.pallas_call(kernel, out_shape=outs, in_specs=specs or [VMEM] * len(arg...  34.2 us
    ppermute x19, starting transfers between devices, shift(): return lax.ppermute(v, 'expert', pairs)  23.8 us
    ppermute x9, starting transfers between devices, shift_y(): return lax.ppermute(v, 'zero', [(a, (a + dy) % ny) for a in range(ny)])  18.3 us
    ppermute x19, waiting for transfers between devices, shift(): return lax.ppermute(v, 'expert', pairs)  17.4 us
    ppermute x9, waiting for transfers between devices, shift_y(): return lax.ppermute(v, 'zero', [(a, (a + dy) % ny) for a in range(ny)])  13 us
    ppermute x8, waiting for transfers between devices, along(): return lax.ppermute(v, 'expert', pairs)  9.4 us
    ppermute x8, starting transfers between devices, along(): return lax.ppermute(v, 'expert', pairs)  7.74 us
  transfers between devices with their start and end apart: 36, of which 17 were waited for; matrix products, arithmetic and copies ran while one was open for 0% of the time, Pallas kernels for 12%

profile of v3, /device:TPU:6, one launch (start us, length us, event | category | flops | bytes accessed | tf_op | source)
XLA Modules:
  0.0 126.6 jit_solution(12978258392693444321)
XLA Ops:
  10.5 2.4 %collective-permute-start.4 = (bf16[2,64,2048]{2,1,0:T(8,128)(2,1)S(1)}, bf16[2,64,2048]{2,1,0:T(8,128)(2,1)}, u32[]{:S(2)}, u32[]{:S(2)}) collective-permute-start(bf16[2,64,2048]{2,1,0:T(8,128)(2,1)S(1)} %shard_map.88.refs_6_), channel_id=1, source_target_pairs={{0,8},{4,12},{8,16},{12,20},{16,24},{20,28},{24,0},{28,4},{32,40},... | collective-permute-start | bytes 1572872 | tf_op jit(solution)/shard_map/ppermute | solution.py:301
  13.0 3.4 %collective-permute-done.refs_0_ = bf16[128,2176]{1,0:T(8,128)(2,1)S(1)} collective-permute-done((bf16[128,2176]{1,0:T(8,128)(2,1)}, bf16[128,2176]{1,0:T(8,128)(2,1)S(1)}, u32[]{:S(2)}, u32[]{:S(2)}) %collective-permute-start) | collective-permute-done | bytes 557088 | tf_op jit(solution)/shard_map/ppermute | solution.py:339
  16.5 3.3 %collective-permute-start.10 = (f32[2,32,192]{2,1,0:T(8,128)}, f32[2,32,192]{2,1,0:T(8,128)S(1)}, u32[]{:S(2)}, u32[]{:S(2)}) collective-permute-start(f32[2,32,192]{2,1,0:T(8,128)} %bitcast.6.refs_0_), channel_id=1, source_target_pairs={{0,2},{1,3},{2,0},{3,1},{4,6},{5,7},{6,4},{7,5},{8,10},{9,11},{10,... | collective-permute-start | bytes 147464 | tf_op jit(solution)/shard_map/ppermute | solution.py:304
  19.8 2.8 %collective-permute-done.10.refs_1_.refs_2_ = f32[2,32,192]{2,1,0:T(8,128)S(1)} collective-permute-done((f32[2,32,192]{2,1,0:T(8,128)}, f32[2,32,192]{2,1,0:T(8,128)S(1)}, u32[]{:S(2)}, u32[]{:S(2)}) %collective-permute-start.10) | collective-permute-done | bytes 49184 | tf_op jit(solution)/shard_map/ppermute | solution.py:304
  26.0 3.0 %collective-permute-start.5 = (f32[2,32,192]{2,1,0:T(8,128)}, f32[2,32,192]{2,1,0:T(8,128)S(1)}, u32[]{:S(2)}, u32[]{:S(2)}) collective-permute-start(f32[2,32,192]{2,1,0:T(8,128)} %bitcast.6.refs_0_), channel_id=1, source_target_pairs={{0,3},{1,0},{2,1},{3,2},{4,7},{5,4},{6,5},{7,6},{8,11},{9,8},{10,9... | collective-permute-start | bytes 147464 | tf_op jit(solution)/shard_map/ppermute | solution.py:304
  29.0 2.2 %collective-permute-done.5.refs_2_.refs_3_ = f32[2,32,192]{2,1,0:T(8,128)S(1)} collective-permute-done((f32[2,32,192]{2,1,0:T(8,128)}, f32[2,32,192]{2,1,0:T(8,128)S(1)}, u32[]{:S(2)}, u32[]{:S(2)}) %collective-permute-start.5) | collective-permute-done | bytes 49184 | tf_op jit(solution)/shard_map/ppermute | solution.py:304
  31.2 2.4 %collective-permute-start.6 = (bf16[128,2176]{1,0:T(8,128)(2,1)S(1)}, bf16[128,2176]{1,0:T(8,128)(2,1)S(1)}, u32[]{:S(2)}, u32[]{:S(2)}) collective-permute-start(bf16[128,2176]{1,0:T(8,128)(2,1)S(1)} %shard_map.90.refs_0_.refs_6_), channel_id=1, source_target_pairs={{0,32},{4,228},{8,40},{12,236},{16,48},{20,244},{24,56},{28,252},{... | collective-permute-start | bytes 1671176 | tf_op jit(solution)/shard_map/ppermute | solution.py:339
  33.7 2.7 %collective-permute-start.15 = (bf16[128,2176]{1,0:T(8,128)(2,1)S(1)}, bf16[128,2176]{1,0:T(8,128)(2,1)S(1)}, u32[]{:S(2)}, u32[]{:S(2)}) collective-permute-start(bf16[128,2176]{1,0:T(8,128)(2,1)S(1)} %shard_map.91.refs_3_), channel_id=1, source_target_pairs={{0,4},{4,0},{8,12},{12,8},{16,20},{20,16},{24,28},{28,24},{32,36},... | collective-permute-start | bytes 1671176 | tf_op jit(solution)/shard_map/ppermute | solution.py:301
  37.0 5.9 %collective-permute-done.6.refs_0_.refs_10_ = bf16[128,2176]{1,0:T(8,128)(2,1)S(1)} collective-permute-done((bf16[128,2176]{1,0:T(8,128)(2,1)S(1)}, bf16[128,2176]{1,0:T(8,128)(2,1)S(1)}, u32[]{:S(2)}, u32[]{:S(2)}) %collective-permute-start.6) | collective-permute-done | bytes 557088 | tf_op jit(solution)/shard_map/ppermute | solution.py:339
  45.4 2.5 %collective-permute-start.19 = (bf16[128,2176]{1,0:T(8,128)(2,1)S(1)}, bf16[128,2176]{1,0:T(8,128)(2,1)S(1)}, u32[]{:S(2)}, u32[]{:S(2)}) collective-permute-start(bf16[128,2176]{1,0:T(8,128)(2,1)S(1)} %collective-permute-done.6.refs_0_.refs_10_), channel_id=1, source_target_pairs={{0,4},{4,0},{8,12},{12,8},{16,20},{20,16},{24,28},{28,24},{32,36},... | collective-permute-start | bytes 1671176 | tf_op jit(solution)/shard_map/ppermute | solution.py:301
  47.9 5.1 %shard_map.92 = (f32[8,32,256]{2,1,0:T(8,128)S(1)}, bf16[512,2048]{1,0:T(8,128)(2,1)S(1)}, f32[96,128]{1,0:T(8,128)S(1)}) custom-call(s32[4]{0:T(128)S(1)} %pad_add_fusion.meta_ref, bf16[128,2176]{1,0:T(8,128)(2,1)S(1)} %copy-done.3, bf16[128,2176]{1,0:T(8,128)(2,1)} %collective-permute-done.8.refs_1_, bf16[128,2176]{1,0:T(8,128)(2,1)S(1)} %shard_map.87.refs_2_, ...), custom_call_target="tpu_custom_call" | custom-call | flops 1610612736 | bytes 3221225 | tf_op jit(solution)/shard_map/pallas_call | solution.py:45
  53.2 2.4 %shard_map.93 = (f32[8,32,256]{2,1,0:T(8,128)S(1)}, f32[64,128]{1,0:T(8,128)S(1)}) custom-call(s32[4]{0:T(128)S(1)} %pad_add_fusion.meta_ref, bf16[128,2176]{1,0:T(8,128)(2,1)S(1)} %shard_map.90.refs_0_.refs_6_, bf16[128,2176]{1,0:T(8,128)(2,1)S(1)} %collective-permute-done.11.refs_1_.refs_7_, bf16[128,2176]{1,0:T(8,128)(2,1)S(1)} %collective-permute-done.12.refs_2_.refs_8_, ...), custom_call_target="tpu_custom_call" | custom-call | flops 1073741824 | bytes 2147483 | tf_op jit(solution)/shard_map/pallas_call | solution.py:45
  56.2 2.4 %shard_map.96 = (f32[8,32,256]{2,1,0:T(8,128)S(1)}, f32[64,128]{1,0:T(8,128)S(1)}) custom-call(s32[4]{0:T(128)S(1)} %pad_add_fusion.meta_ref, bf16[128,2176]{1,0:T(8,128)(2,1)S(1)} %collective-permute-done.6.refs_0_.refs_10_, bf16[128,2176]{1,0:T(8,128)(2,1)S(1)} %collective-permute-done.18.refs_1_.refs_11_, ...), custom_call_target="tpu_custom_call" | custom-call | flops 1073741824 | bytes 2147483 | tf_op jit(solution)/shard_map/pallas_call | solution.py:45
  65.4 3.9 %collective-permute-done.22.refs_2_ = f32[2,32,256]{2,1,0:T(8,128)S(1)} collective-permute-done((f32[2,32,256]{2,1,0:T(8,128)S(1)}, f32[2,32,256]{2,1,0:T(8,128)S(1)}, u32[]{:S(2)}, u32[]{:S(2)}) %collective-permute-start.22) | collective-permute-done | bytes 65568 | tf_op jit(solution)/shard_map/ppermute | solution.py:301
  72.9 2.8 %collective-permute-start.25 = (bf16[2,32,768]{2,1,0:T(8,128)(2,1)S(1)}, bf16[2,32,768]{2,1,0:T(8,128)(2,1)S(1)}, u32[]{:S(2)}, u32[]{:S(2)}) collective-permute-start(bf16[2,32,768]{2,1,0:T(8,128)(2,1)S(1)} %shard_map.98.refs_0_), channel_id=1, source_target_pairs={{0,2},{1,3},{2,0},{3,1},{4,6},{5,7},{6,4},{7,5},{8,10},{9,11},{10,... | collective-permute-start | bytes 294920 | tf_op jit(solution)/shard_map/ppermute | solution.py:304
  77.2 3.1 %collective-permute-done.25.refs_2_ = bf16[2,32,768]{2,1,0:T(8,128)(2,1)S(1)} collective-permute-done((bf16[2,32,768]{2,1,0:T(8,128)(2,1)S(1)}, bf16[2,32,768]{2,1,0:T(8,128)(2,1)S(1)}, u32[]{:S(2)}, u32[]{:S(2)}) %collective-permute-start.25) | collective-permute-done | bytes 98336 | tf_op jit(solution)/shard_map/ppermute | solution.py:304
  80.3 5.4 %shard_map.99 = (f32[2,32,768]{2,1,0:T(8,128)S(1)}, f32[2,32,256]{2,1,0:T(8,128)S(1)}, f32[2,32,256]{2,1,0:T(8,128)S(1)}, f32[2,32,256]{2,1,0:T(8,128)S(1)}, f32[2,32,256]{2,1,0:T(8,128)S(1)}) custom-call(s32[4]{0:T(128)S(1)} %pad_add_fusion.meta_ref, bf16[2,32,768]{2,1,0:T(8,128)(2,1)S(1)} %shard_map.98.refs_0_, ...), custom_call_target="tpu_custom_call" | custom-call | tf_op jit(solution)/shard_map/pallas_call | solution.py:45
  87.6 2.3 %collective-permute-start.29 = (f32[2,32,256]{2,1,0:T(8,128)S(1)}, f32[2,32,256]{2,1,0:T(8,128)S(1)}, u32[]{:S(2)}, u32[]{:S(2)}) collective-permute-start(f32[2,32,256]{2,1,0:T(8,128)S(1)} %get-tuple-element.47), channel_id=1, source_target_pairs={{0,8},{4,12},{8,16},{12,20},{16,24},{20,28},{24,0},{28,4},{32,40},... | collective-permute-start | bytes 196616 | tf_op jit(solution)/shard_map/ppermute | solution.py:301
  92.8 8.4 %shard_map.101 = (f32[2,32,2048]{2,1,0:T(8,128)S(1)}, bf16[2,32,2048]{2,1,0:T(8,128)(2,1)S(1)}, bf16[2,32,2048]{2,1,0:T(8,128)(2,1)S(1)}, bf16[2,32,2048]{2,1,0:T(8,128)(2,1)S(1)}) custom-call(bf16[128,2176]{1,0:T(8,128)(2,1)S(1)} %copy-done.3, bf16[128,2176]{1,0:T(8,128)(2,1)} %collective-permute-done.8.refs_1_, bf16[128,2176]{1,0:T(8,128)(2,1)S(1)} %shard_map.87.refs_2_, ...), custom_call_target="tpu_custom_call" | custom-call | flops 4294967296 | bytes 8589934 | tf_op jit(solution)/shard_map/pallas_call | solution.py:45
  101.2 2.7 %collective-permute-start.30 = (bf16[2,32,2048]{2,1,0:T(8,128)(2,1)S(1)}, bf16[2,32,2048]{2,1,0:T(8,128)(2,1)S(1)}, u32[]{:S(2)}, u32[]{:S(2)}) collective-permute-start(bf16[2,32,2048]{2,1,0:T(8,128)(2,1)S(1)} %get-tuple-element.53), channel_id=1, source_target_pairs={{0,8},{4,12},{8,16},{12,20},{16,24},{20,28},{24,0},{28,4},{32,40},... | collective-permute-start | bytes 786440 | tf_op jit(solution)/shard_map/ppermute | solution.py:301
  104.9 7.8 %collective-permute-done.30 = bf16[2,32,2048]{2,1,0:T(8,128)(2,1)S(1)} collective-permute-done((bf16[2,32,2048]{2,1,0:T(8,128)(2,1)S(1)}, bf16[2,32,2048]{2,1,0:T(8,128)(2,1)S(1)}, u32[]{:S(2)}, u32[]{:S(2)}) %collective-permute-start.30) | collective-permute-done | bytes 262176 | tf_op jit(solution)/shard_map/ppermute | solution.py:301
  113.7 2.7 %collective-permute-done.32 = bf16[2,32,2048]{2,1,0:T(8,128)(2,1)S(1)} collective-permute-done((bf16[2,32,2048]{2,1,0:T(8,128)(2,1)S(1)}, bf16[2,32,2048]{2,1,0:T(8,128)(2,1)S(1)}, u32[]{:S(2)}, u32[]{:S(2)}) %collective-permute-start.32) | collective-permute-done | bytes 262176 | tf_op jit(solution)/shard_map/ppermute | solution.py:301
  117.9 2.8 %collective-permute-start.34 = (f32[2,32,512]{2,1,0:T(8,128)S(1)}, f32[2,32,512]{2,1,0:T(8,128)S(1)}, u32[]{:S(2)}, u32[]{:S(2)}) collective-permute-start(f32[2,32,512]{2,1,0:T(8,128)S(1)} %get-tuple-element.58), channel_id=1, source_target_pairs={{0,2},{1,3},{2,0},{3,1},{4,6},{5,7},{6,4},{7,5},{8,10},{9,11},{10,... | collective-permute-start | bytes 393224 | tf_op jit(solution)/shard_map/ppermute | solution.py:304
  121.4 2.9 %collective-permute-done.33 = f32[2,32,512]{2,1,0:T(8,128)S(1)} collective-permute-done((f32[2,32,512]{2,1,0:T(8,128)S(1)}, f32[2,32,512]{2,1,0:T(8,128)S(1)}, u32[]{:S(2)}, u32[]{:S(2)}) %collective-permute-start.33) | collective-permute-done | bytes 131104 | tf_op jit(solution)/shard_map/ppermute | solution.py:304
  (78 shorter events, 40.3 us)
Async XLA Ops:
  2.7 13.7 %collective-permute-start = (bf16[128,2176]{1,0:T(8,128)(2,1)}, bf16[128,2176]{1,0:T(8,128)(2,1)S(1)}, u32[]{:S(2)}, u32[]{:S(2)}) collective-permute-start(bf16[128,2176]{1,0:T(8,128)(2,1)} %shard_map.86.refs_0_), channel_id=1, source_target_pairs={{0,32},{4,228},{8,40},{12,236},{16,48},{20,244},{24,56},{28,252},{... | collective-permute-start | bytes 1671176 | tf_op jit(solution)/shard_map/ppermute | solution.py:339
  5.0 18.9 %collective-permute-start.9 = (bf16[128,2176]{1,0:T(8,128)(2,1)}, bf16[128,2176]{1,0:T(8,128)(2,1)S(1)}, u32[]{:S(2)}, u32[]{:S(2)}) collective-permute-start(bf16[128,2176]{1,0:T(8,128)(2,1)} %collective-permute-done.8.refs_1_), channel_id=1, source_target_pairs={{0,32},{4,228},{8,40},{12,236},{16,48},{20,244},{24,56},{28,252},{... | collective-permute-start | bytes 1671176 | tf_op jit(solution)/shard_map/ppermute | solution.py:339
  9.6 14.5 %collective-permute-start.3 = (bf16[2,64,2048]{2,1,0:T(8,128)(2,1)S(1)}, bf16[2,64,2048]{2,1,0:T(8,128)(2,1)}, u32[]{:S(2)}, u32[]{:S(2)}) collective-permute-start(bf16[2,64,2048]{2,1,0:T(8,128)(2,1)S(1)} %shard_map.88.refs_6_), channel_id=1, source_target_pairs={{0,24},{4,28},{8,0},{12,4},{16,8},{20,12},{24,16},{28,20},{32,56},... | collective-permute-start | bytes 1572872 | tf_op jit(solution)/shard_map/ppermute | solution.py:301
  10.5 13.6 %collective-permute-start.4 = (bf16[2,64,2048]{2,1,0:T(8,128)(2,1)S(1)}, bf16[2,64,2048]{2,1,0:T(8,128)(2,1)}, u32[]{:S(2)}, u32[]{:S(2)}) collective-permute-start(bf16[2,64,2048]{2,1,0:T(8,128)(2,1)S(1)} %shard_map.88.refs_6_), channel_id=1, source_target_pairs={{0,8},{4,12},{8,16},{12,20},{16,24},{20,28},{24,0},{28,4},{32,40},... | collective-permute-start | bytes 1572872 | tf_op jit(solution)/shard_map/ppermute | solution.py:301
  16.4 14.8 %collective-permute-start.2 = (bf16[128,2176]{1,0:T(8,128)(2,1)S(1)}, bf16[128,2176]{1,0:T(8,128)(2,1)S(1)}, u32[]{:S(2)}, u32[]{:S(2)}) collective-permute-start(bf16[128,2176]{1,0:T(8,128)(2,1)S(1)} %shard_map.87.refs_2_), channel_id=1, source_target_pairs={{0,32},{4,228},{8,40},{12,236},{16,48},{20,244},{24,56},{28,252},{... | collective-permute-start | bytes 1671176 | tf_op jit(solution)/shard_map/ppermute | solution.py:339
  22.6 14.2 %collective-permute-start.14 = (bf16[128,2176]{1,0:T(8,128)(2,1)S(1)}, bf16[128,2176]{1,0:T(8,128)(2,1)S(1)}, u32[]{:S(2)}, u32[]{:S(2)}) collective-permute-start(bf16[128,2176]{1,0:T(8,128)(2,1)S(1)} %shard_map.87.refs_2_), channel_id=1, source_target_pairs={{0,4},{4,0},{8,12},{12,8},{16,20},{20,16},{24,28},{28,24},{32,36},... | collective-permute-start | bytes 1671176 | tf_op jit(solution)/shard_map/ppermute | solution.py:301
  24.0 12.4 %collective-permute-start.11 = (bf16[128,2176]{1,0:T(8,128)(2,1)S(1)}, bf16[128,2176]{1,0:T(8,128)(2,1)S(1)}, u32[]{:S(2)}, u32[]{:S(2)}) collective-permute-start(bf16[128,2176]{1,0:T(8,128)(2,1)S(1)} %shard_map.91.refs_3_), channel_id=1, source_target_pairs={{0,32},{4,228},{8,40},{12,236},{16,48},{20,244},{24,56},{28,252},{... | collective-permute-start | bytes 1671176 | tf_op jit(solution)/shard_map/ppermute | solution.py:339
  25.4 11.0 %collective-permute-start.16 = (bf16[2,64,2048]{2,1,0:T(8,128)(2,1)S(1)}, bf16[2,64,2048]{2,1,0:T(8,128)(2,1)S(1)}, u32[]{:S(2)}, u32[]{:S(2)}) collective-permute-start(bf16[2,64,2048]{2,1,0:T(8,128)(2,1)S(1)} %get-tuple-element.30), channel_id=1, source_target_pairs={{0,24},{4,12},{8,0},{12,20},{16,8},{20,28},{24,16},{28,4},{32,56},... | collective-permute-start | bytes 1572872 | tf_op jit(solution)/shard_map/ppermute | solution.py:339
  31.2 11.7 %collective-permute-start.6 = (bf16[128,2176]{1,0:T(8,128)(2,1)S(1)}, bf16[128,2176]{1,0:T(8,128)(2,1)S(1)}, u32[]{:S(2)}, u32[]{:S(2)}) collective-permute-start(bf16[128,2176]{1,0:T(8,128)(2,1)S(1)} %shard_map.90.refs_0_.refs_6_), channel_id=1, source_target_pairs={{0,32},{4,228},{8,40},{12,236},{16,48},{20,244},{24,56},{28,252},{... | collective-permute-start | bytes 1671176 | tf_op jit(solution)/shard_map/ppermute | solution.py:339
  33.7 11.7 %collective-permute-start.15 = (bf16[128,2176]{1,0:T(8,128)(2,1)S(1)}, bf16[128,2176]{1,0:T(8,128)(2,1)S(1)}, u32[]{:S(2)}, u32[]{:S(2)}) collective-permute-start(bf16[128,2176]{1,0:T(8,128)(2,1)S(1)} %shard_map.91.refs_3_), channel_id=1, source_target_pairs={{0,4},{4,0},{8,12},{12,8},{16,20},{20,16},{24,28},{28,24},{32,36},... | collective-permute-start | bytes 1671176 | tf_op jit(solution)/shard_map/ppermute | solution.py:301
  36.4 16.6 %collective-permute-start.18 = (bf16[128,2176]{1,0:T(8,128)(2,1)S(1)}, bf16[128,2176]{1,0:T(8,128)(2,1)S(1)}, u32[]{:S(2)}, u32[]{:S(2)}) collective-permute-start(bf16[128,2176]{1,0:T(8,128)(2,1)S(1)} %collective-permute-done.11.refs_1_.refs_7_), channel_id=1, source_target_pairs={{0,32},{4,228},{8,40},{12,236},{16,48},{20,244},{24,56},{28,252},{... | collective-permute-start | bytes 1671176 | tf_op jit(solution)/shard_map/ppermute | solution.py:339
  36.5 16.7 %collective-permute-start.12 = (bf16[128,2176]{1,0:T(8,128)(2,1)S(1)}, bf16[128,2176]{1,0:T(8,128)(2,1)S(1)}, u32[]{:S(2)}, u32[]{:S(2)}) collective-permute-start(bf16[128,2176]{1,0:T(8,128)(2,1)S(1)} %shard_map.90.refs_0_.refs_6_), channel_id=1, source_target_pairs={{0,4},{4,0},{8,12},{12,8},{16,20},{20,16},{24,28},{28,24},{32,36},... | collective-permute-start | bytes 1671176 | tf_op jit(solution)/shard_map/ppermute | solution.py:301
  36.8 16.3 %collective-permute-start.13 = (bf16[128,2176]{1,0:T(8,128)(2,1)S(1)}, bf16[128,2176]{1,0:T(8,128)(2,1)S(1)}, u32[]{:S(2)}, u32[]{:S(2)}) collective-permute-start(bf16[128,2176]{1,0:T(8,128)(2,1)S(1)} %collective-permute-done.11.refs_1_.refs_7_), channel_id=1, source_target_pairs={{0,4},{4,0},{8,12},{12,8},{16,20},{20,16},{24,28},{28,24},{32,36},... | collective-permute-start | bytes 1671176 | tf_op jit(solution)/shard_map/ppermute | solution.py:301
  42.9 12.6 %collective-permute-start.7 = (bf16[128,2176]{1,0:T(8,128)(2,1)S(1)}, bf16[128,2176]{1,0:T(8,128)(2,1)S(1)}, u32[]{:S(2)}, u32[]{:S(2)}) collective-permute-start(bf16[128,2176]{1,0:T(8,128)(2,1)S(1)} %collective-permute-done.6.refs_0_.refs_10_), channel_id=1, source_target_pairs={{0,32},{4,228},{8,40},{12,236},{16,48},{20,244},{24,56},{28,252},{... | collective-permute-start | bytes 1671176 | tf_op jit(solution)/shard_map/ppermute | solution.py:339
  45.4 10.8 %collective-permute-start.19 = (bf16[128,2176]{1,0:T(8,128)(2,1)S(1)}, bf16[128,2176]{1,0:T(8,128)(2,1)S(1)}, u32[]{:S(2)}, u32[]{:S(2)}) collective-permute-start(bf16[128,2176]{1,0:T(8,128)(2,1)S(1)} %collective-permute-done.6.refs_0_.refs_10_), channel_id=1, source_target_pairs={{0,4},{4,0},{8,12},{12,8},{16,20},{20,16},{24,28},{28,24},{32,36},... | collective-permute-start | bytes 1671176 | tf_op jit(solution)/shard_map/ppermute | solution.py:301
  62.8 6.5 %collective-permute-start.22 = (f32[2,32,256]{2,1,0:T(8,128)S(1)}, f32[2,32,256]{2,1,0:T(8,128)S(1)}, u32[]{:S(2)}, u32[]{:S(2)}) collective-permute-start(f32[2,32,256]{2,1,0:T(8,128)S(1)} %get-tuple-element.39), channel_id=1, source_target_pairs={{0,16},{4,20},{8,24},{12,28},{16,0},{20,4},{24,8},{28,12},{32,48},... | collective-permute-start | bytes 196616 | tf_op jit(solution)/shard_map/ppermute | solution.py:301
  72.9 7.4 %collective-permute-start.25 = (bf16[2,32,768]{2,1,0:T(8,128)(2,1)S(1)}, bf16[2,32,768]{2,1,0:T(8,128)(2,1)S(1)}, u32[]{:S(2)}, u32[]{:S(2)}) collective-permute-start(bf16[2,32,768]{2,1,0:T(8,128)(2,1)S(1)} %shard_map.98.refs_0_), channel_id=1, source_target_pairs={{0,2},{1,3},{2,0},{3,1},{4,6},{5,7},{6,4},{7,5},{8,10},{9,11},{10,... | collective-permute-start | bytes 294920 | tf_op jit(solution)/shard_map/ppermute | solution.py:304
  85.7 6.2 %collective-permute-start.27 = (f32[2,32,256]{2,1,0:T(8,128)S(1)}, f32[2,32,256]{2,1,0:T(8,128)S(1)}, u32[]{:S(2)}, u32[]{:S(2)}) collective-permute-start(f32[2,32,256]{2,1,0:T(8,128)S(1)} %get-tuple-element.45), channel_id=1, source_target_pairs={{0,24},{4,28},{8,0},{12,4},{16,8},{20,12},{24,16},{28,20},{32,56},... | collective-permute-start | bytes 196616 | tf_op jit(solution)/shard_map/ppermute | solution.py:301
  85.8 6.2 %collective-permute-start.28 = (f32[2,32,256]{2,1,0:T(8,128)S(1)}, f32[2,32,256]{2,1,0:T(8,128)S(1)}, u32[]{:S(2)}, u32[]{:S(2)}) collective-permute-start(f32[2,32,256]{2,1,0:T(8,128)S(1)} %get-tuple-element.46), channel_id=1, source_target_pairs={{0,16},{4,20},{8,24},{12,28},{16,0},{20,4},{24,8},{28,12},{32,48},... | collective-permute-start | bytes 196616 | tf_op jit(solution)/shard_map/ppermute | solution.py:301
  101.2 11.5 %collective-permute-start.30 = (bf16[2,32,2048]{2,1,0:T(8,128)(2,1)S(1)}, bf16[2,32,2048]{2,1,0:T(8,128)(2,1)S(1)}, u32[]{:S(2)}, u32[]{:S(2)}) collective-permute-start(bf16[2,32,2048]{2,1,0:T(8,128)(2,1)S(1)} %get-tuple-element.53), channel_id=1, source_target_pairs={{0,8},{4,12},{8,16},{12,20},{16,24},{20,28},{24,0},{28,4},{32,40},... | collective-permute-start | bytes 786440 | tf_op jit(solution)/shard_map/ppermute | solution.py:301
  104.0 9.7 %collective-permute-start.31 = (bf16[2,32,2048]{2,1,0:T(8,128)(2,1)S(1)}, bf16[2,32,2048]{2,1,0:T(8,128)(2,1)S(1)}, u32[]{:S(2)}, u32[]{:S(2)}) collective-permute-start(bf16[2,32,2048]{2,1,0:T(8,128)(2,1)S(1)} %get-tuple-element.54), channel_id=1, source_target_pairs={{0,16},{4,20},{8,24},{12,28},{16,0},{20,4},{24,8},{28,12},{32,48},... | collective-permute-start | bytes 786440 | tf_op jit(solution)/shard_map/ppermute | solution.py:301
  104.7 11.7 %collective-permute-start.32 = (bf16[2,32,2048]{2,1,0:T(8,128)(2,1)S(1)}, bf16[2,32,2048]{2,1,0:T(8,128)(2,1)S(1)}, u32[]{:S(2)}, u32[]{:S(2)}) collective-permute-start(bf16[2,32,2048]{2,1,0:T(8,128)(2,1)S(1)} %get-tuple-element.55), channel_id=1, source_target_pairs={{0,24},{4,28},{8,0},{12,4},{16,8},{20,12},{24,16},{28,20},{32,56},... | collective-permute-start | bytes 786440 | tf_op jit(solution)/shard_map/ppermute | solution.py:301
  116.6 7.7 %collective-permute-start.33 = (f32[2,32,512]{2,1,0:T(8,128)S(1)}, f32[2,32,512]{2,1,0:T(8,128)S(1)}, u32[]{:S(2)}, u32[]{:S(2)}) collective-permute-start(f32[2,32,512]{2,1,0:T(8,128)S(1)} %get-tuple-element.56), channel_id=1, source_target_pairs={{0,1},{1,2},{2,3},{3,0},{4,5},{5,6},{6,7},{7,4},{8,9},{9,10},{10,1... | collective-permute-start | bytes 393224 | tf_op jit(solution)/shard_map/ppermute | solution.py:304
  117.9 7.9 %collective-permute-start.34 = (f32[2,32,512]{2,1,0:T(8,128)S(1)}, f32[2,32,512]{2,1,0:T(8,128)S(1)}, u32[]{:S(2)}, u32[]{:S(2)}) collective-permute-start(f32[2,32,512]{2,1,0:T(8,128)S(1)} %get-tuple-element.58), channel_id=1, source_target_pairs={{0,2},{1,3},{2,0},{3,1},{4,6},{5,7},{6,4},{7,5},{8,10},{9,11},{10,... | collective-permute-start | bytes 393224 | tf_op jit(solution)/shard_map/ppermute | solution.py:304
  (17 other events, 196.4 us)

commit v4 on v3

--- a/solution.py
+++ b/solution.py
@@ -382,7 +382,7 @@
         specs=[SMEM, VMEM, VMEM],
     )
     far = along(farther, "x")
-    [p], q = after([along(p)], token, *lefts[3:]), along(q)
+    p, [q] = along(p), after([along(q)], token, *lefts[3:])
     second = ring(2, p, q)
     a = project(first, [two, near[0], far, near[1]], [])
     all_s = [a[4]]

time: 127 us -> 122 us (0.961)
  starting transfers between devices: 49.8 us -> 41.7 us
  waiting for transfers between devices: 39.7 us -> 42.8 us
    ppermute x19, starting transfers between devices: 23.8 us -> 17 us  [shift(): return lax.ppermute(v, 'expert', pairs)]
    ppermute x9, waiting for transfers between devices: 13 us -> 14.3 us  [shift_y(): return lax.ppermute(v, 'zero', [(a, (a + dy) % ny) for a in range(ny)])]
  transfers between devices with their start and end apart: 36 -> 36, of which waited for: 17 -> 22; matrix products, arithmetic and copies ran while one was open for 0% -> 0% of each run, Pallas kernels for 12% -> 12%
where the time goes in v4:
time: 122 us
  waiting for transfers between devices  42.8 us (35%)
  starting transfers between devices  41.7 us (34%)
  Pallas kernels  34.2 us (28%)
    pallas_call x16, Pallas kernels, call(): pl.pallas_call(kernel, out_shape=outs, in_specs=specs or [VMEM] * len(arg...  34.2 us
    ppermute x19, waiting for transfers between devices, shift(): return lax.ppermute(v, 'expert', pairs)  18.2 us
    ppermute x9, starting transfers between devices, shift_y(): return lax.ppermute(v, 'zero', [(a, (a + dy) % ny) for a in range(ny)])  17.2 us
    ppermute x19, starting transfers between devices, shift(): return lax.ppermute(v, 'expert', pairs)  17 us
    ppermute x9, waiting for transfers between devices, shift_y(): return lax.ppermute(v, 'zero', [(a, (a + dy) % ny) for a in range(ny)])  14.3 us
    ppermute x8, waiting for transfers between devices, along(): return lax.ppermute(v, 'expert', pairs)  10.4 us
    ppermute x8, starting transfers between devices, along(): return lax.ppermute(v, 'expert', pairs)  7.55 us
  transfers between devices with their start and end apart: 36, of which 22 were waited for; matrix products, arithmetic and copies ran while one was open for 0% of the time, Pallas kernels for 12%

profile of v4, /device:TPU:6, one launch (start us, length us, event | category | flops | bytes accessed | tf_op | source)
XLA Modules:
  0.0 121.6 jit_solution(14268078302775397072)
XLA Ops:
  0.7 2.0 %shard_map.86.refs_0_ = bf16[128,2176]{1,0:T(8,128)(2,1)} custom-call(bf16[128,2048]{1,0:T(8,128)(2,1)} %cot_ref.1, f32[8,128]{1,0:T(8,128)} %bitcast.16, s32[8,128]{1,0:T(8,128)} %bitcast.17), custom_call_target="tpu_custom_call" | custom-call | tf_op jit(solution)/shard_map/pallas_call | solution.py:45
  2.7 2.0 %collective-permute-start = (bf16[128,2176]{1,0:T(8,128)(2,1)}, bf16[128,2176]{1,0:T(8,128)(2,1)S(1)}, u32[]{:S(2)}, u32[]{:S(2)}) collective-permute-start(bf16[128,2176]{1,0:T(8,128)(2,1)} %shard_map.86.refs_0_), channel_id=1, source_target_pairs={{0,32},{4,228},{8,40},{12,236},{16,48},{20,244},{24,56},{28,252},{... | collective-permute-start | bytes 1671176 | tf_op jit(solution)/shard_map/ppermute | solution.py:339
  12.6 3.8 %collective-permute-done.refs_0_ = bf16[128,2176]{1,0:T(8,128)(2,1)S(1)} collective-permute-done((bf16[128,2176]{1,0:T(8,128)(2,1)}, bf16[128,2176]{1,0:T(8,128)(2,1)S(1)}, u32[]{:S(2)}, u32[]{:S(2)}) %collective-permute-start) | collective-permute-done | bytes 557088 | tf_op jit(solution)/shard_map/ppermute | solution.py:339
  16.5 3.3 %collective-permute-start.7 = (f32[2,32,192]{2,1,0:T(8,128)}, f32[2,32,192]{2,1,0:T(8,128)S(1)}, u32[]{:S(2)}, u32[]{:S(2)}) collective-permute-start(f32[2,32,192]{2,1,0:T(8,128)} %bitcast.6.refs_0_), channel_id=1, source_target_pairs={{0,2},{1,3},{2,0},{3,1},{4,6},{5,7},{6,4},{7,5},{8,10},{9,11},{10,... | collective-permute-start | bytes 147464 | tf_op jit(solution)/shard_map/ppermute | solution.py:304
  19.8 2.8 %collective-permute-done.7.refs_1_.refs_2_ = f32[2,32,192]{2,1,0:T(8,128)S(1)} collective-permute-done((f32[2,32,192]{2,1,0:T(8,128)}, f32[2,32,192]{2,1,0:T(8,128)S(1)}, u32[]{:S(2)}, u32[]{:S(2)}) %collective-permute-start.7) | collective-permute-done | bytes 49184 | tf_op jit(solution)/shard_map/ppermute | solution.py:304
  26.0 2.4 %collective-permute-done.2.refs_0_.refs_6_ = bf16[128,2176]{1,0:T(8,128)(2,1)S(1)} collective-permute-done((bf16[128,2176]{1,0:T(8,128)(2,1)S(1)}, bf16[128,2176]{1,0:T(8,128)(2,1)S(1)}, u32[]{:S(2)}, u32[]{:S(2)}) %collective-permute-start.2) | collective-permute-done | bytes 557088 | tf_op jit(solution)/shard_map/ppermute | solution.py:339
  31.3 3.4 %collective-permute-done.11.refs_2_.refs_3_ = f32[2,32,192]{2,1,0:T(8,128)S(1)} collective-permute-done((f32[2,32,192]{2,1,0:T(8,128)}, f32[2,32,192]{2,1,0:T(8,128)S(1)}, u32[]{:S(2)}, u32[]{:S(2)}) %collective-permute-start.11) | collective-permute-done | bytes 49184 | tf_op jit(solution)/shard_map/ppermute | solution.py:304
  37.2 3.5 %collective-permute-done.3.refs_0_.refs_10_ = bf16[128,2176]{1,0:T(8,128)(2,1)S(1)} collective-permute-done((bf16[128,2176]{1,0:T(8,128)(2,1)S(1)}, bf16[128,2176]{1,0:T(8,128)(2,1)S(1)}, u32[]{:S(2)}, u32[]{:S(2)}) %collective-permute-start.3) | collective-permute-done | bytes 557088 | tf_op jit(solution)/shard_map/ppermute | solution.py:339
  44.4 5.1 %shard_map.92 = (f32[8,32,256]{2,1,0:T(8,128)S(1)}, bf16[512,2048]{1,0:T(8,128)(2,1)S(1)}, f32[96,128]{1,0:T(8,128)S(1)}) custom-call(s32[4]{0:T(128)S(1)} %pad_add_fusion.meta_ref, bf16[128,2176]{1,0:T(8,128)(2,1)S(1)} %copy-done.3, bf16[128,2176]{1,0:T(8,128)(2,1)} %collective-permute-done.5.refs_1_, bf16[128,2176]{1,0:T(8,128)(2,1)S(1)} %shard_map.87.refs_2_, ...), custom_call_target="tpu_custom_call" | custom-call | flops 1610612736 | bytes 3221225 | tf_op jit(solution)/shard_map/pallas_call | solution.py:45
  49.7 2.4 %shard_map.93 = (f32[8,32,256]{2,1,0:T(8,128)S(1)}, f32[64,128]{1,0:T(8,128)S(1)}) custom-call(s32[4]{0:T(128)S(1)} %pad_add_fusion.meta_ref, bf16[128,2176]{1,0:T(8,128)(2,1)S(1)} %collective-permute-done.2.refs_0_.refs_6_, bf16[128,2176]{1,0:T(8,128)(2,1)S(1)} %shard_map.91.refs_1_.refs_7_, bf16[128,2176]{1,0:T(8,128)(2,1)S(1)} %collective-permute-done.12.refs_2_.refs_8_, ...), custom_call_target="tpu_custom_call" | custom-call | flops 1073741824 | bytes 2147483 | tf_op jit(solution)/shard_map/pallas_call | solution.py:45
  52.9 2.4 %shard_map.96 = (f32[8,32,256]{2,1,0:T(8,128)S(1)}, f32[64,128]{1,0:T(8,128)S(1)}) custom-call(s32[4]{0:T(128)S(1)} %pad_add_fusion.meta_ref, bf16[128,2176]{1,0:T(8,128)(2,1)S(1)} %collective-permute-done.3.refs_0_.refs_10_, bf16[128,2176]{1,0:T(8,128)(2,1)S(1)} %collective-permute-done.18.refs_1_.refs_11_, ...), custom_call_target="tpu_custom_call" | custom-call | flops 1073741824 | bytes 2147483 | tf_op jit(solution)/shard_map/pallas_call | solution.py:45
  55.3 2.1 %shard_map.97 = (f32[2,32,256]{2,1,0:T(8,128)S(1)}, f32[2,32,256]{2,1,0:T(8,128)S(1)}, f32[2,32,256]{2,1,0:T(8,128)S(1)}, f32[2,32,256]{2,1,0:T(8,128)S(1)}, f32[32,128]{1,0:T(8,128)S(1)}) custom-call(s32[4]{0:T(128)S(1)} %pad_add_fusion.meta_ref, bf16[128,2176]{1,0:T(8,128)(2,1)S(1)} %shard_map.95.refs_0_.refs_14_, ...), custom_call_target="tpu_custom_call" | custom-call | flops 536870912 | bytes 1073741 | tf_op jit(solution)/shard_map/pallas_call | solution.py:45
  60.2 2.2 %collective-permute-done.21.refs_1_ = f32[2,32,256]{2,1,0:T(8,128)S(1)} collective-permute-done((f32[2,32,256]{2,1,0:T(8,128)S(1)}, f32[2,32,256]{2,1,0:T(8,128)S(1)}, u32[]{:S(2)}, u32[]{:S(2)}) %collective-permute-start.21) | collective-permute-done | bytes 65568 | tf_op jit(solution)/shard_map/ppermute | solution.py:301
  62.3 2.5 %collective-permute-done.22.refs_2_ = f32[2,32,256]{2,1,0:T(8,128)S(1)} collective-permute-done((f32[2,32,256]{2,1,0:T(8,128)S(1)}, f32[2,32,256]{2,1,0:T(8,128)S(1)}, u32[]{:S(2)}, u32[]{:S(2)}) %collective-permute-start.22) | collective-permute-done | bytes 65568 | tf_op jit(solution)/shard_map/ppermute | solution.py:301
  68.7 2.7 %collective-permute-start.25 = (bf16[2,32,768]{2,1,0:T(8,128)(2,1)S(1)}, bf16[2,32,768]{2,1,0:T(8,128)(2,1)S(1)}, u32[]{:S(2)}, u32[]{:S(2)}) collective-permute-start(bf16[2,32,768]{2,1,0:T(8,128)(2,1)S(1)} %shard_map.98.refs_0_), channel_id=1, source_target_pairs={{0,2},{1,3},{2,0},{3,1},{4,6},{5,7},{6,4},{7,5},{8,10},{9,11},{10,... | collective-permute-start | bytes 294920 | tf_op jit(solution)/shard_map/ppermute | solution.py:304
  76.1 5.4 %shard_map.99 = (f32[2,32,768]{2,1,0:T(8,128)S(1)}, f32[2,32,256]{2,1,0:T(8,128)S(1)}, f32[2,32,256]{2,1,0:T(8,128)S(1)}, f32[2,32,256]{2,1,0:T(8,128)S(1)}, f32[2,32,256]{2,1,0:T(8,128)S(1)}) custom-call(s32[4]{0:T(128)S(1)} %pad_add_fusion.meta_ref, bf16[2,32,768]{2,1,0:T(8,128)(2,1)S(1)} %shard_map.98.refs_0_, ...), custom_call_target="tpu_custom_call" | custom-call | tf_op jit(solution)/shard_map/pallas_call | solution.py:45
  81.5 2.2 %collective-permute-start.28 = (f32[2,32,256]{2,1,0:T(8,128)S(1)}, f32[2,32,256]{2,1,0:T(8,128)S(1)}, u32[]{:S(2)}, u32[]{:S(2)}) collective-permute-start(f32[2,32,256]{2,1,0:T(8,128)S(1)} %get-tuple-element.46), channel_id=1, source_target_pairs={{0,16},{4,20},{8,24},{12,28},{16,0},{20,4},{24,8},{28,12},{32,48},... | collective-permute-start | bytes 196616 | tf_op jit(solution)/shard_map/ppermute | solution.py:301
  85.5 2.0 %shard_map.100 = (f32[2,32,192]{2,1,0:T(8,128)}, f32[2,32,512]{2,1,0:T(8,128)S(1)}) custom-call(s32[4]{0:T(128)S(1)} %pad_add_fusion.meta_ref, f32[2,32,768]{2,1,0:T(8,128)S(1)} %get-tuple-element.41.basis_ref, f32[2,32,768]{2,1,0:T(8,128)S(1)} %get-tuple-element.42.left_ref, f32[2,32,512]{2,1,0:T(8,128)S(1)} %copy-done.4), custom_call_target="tpu_custom_call" | custom-call | tf_op jit(solution)/shard_map/pallas_call | solution.py:45
  88.5 8.4 %shard_map.101 = (f32[2,32,2048]{2,1,0:T(8,128)S(1)}, bf16[2,32,2048]{2,1,0:T(8,128)(2,1)S(1)}, bf16[2,32,2048]{2,1,0:T(8,128)(2,1)S(1)}, bf16[2,32,2048]{2,1,0:T(8,128)(2,1)S(1)}) custom-call(bf16[128,2176]{1,0:T(8,128)(2,1)S(1)} %copy-done.3, bf16[128,2176]{1,0:T(8,128)(2,1)} %collective-permute-done.5.refs_1_, bf16[128,2176]{1,0:T(8,128)(2,1)S(1)} %shard_map.87.refs_2_, ...), custom_call_target="tpu_custom_call" | custom-call | flops 4294967296 | bytes 8589934 | tf_op jit(solution)/shard_map/pallas_call | solution.py:45
  97.0 2.7 %collective-permute-start.30 = (bf16[2,32,2048]{2,1,0:T(8,128)(2,1)S(1)}, bf16[2,32,2048]{2,1,0:T(8,128)(2,1)S(1)}, u32[]{:S(2)}, u32[]{:S(2)}) collective-permute-start(bf16[2,32,2048]{2,1,0:T(8,128)(2,1)S(1)} %get-tuple-element.53), channel_id=1, source_target_pairs={{0,8},{4,12},{8,16},{12,20},{16,24},{20,28},{24,0},{28,4},{32,40},... | collective-permute-start | bytes 786440 | tf_op jit(solution)/shard_map/ppermute | solution.py:301
  100.7 7.6 %collective-permute-done.30 = bf16[2,32,2048]{2,1,0:T(8,128)(2,1)S(1)} collective-permute-done((bf16[2,32,2048]{2,1,0:T(8,128)(2,1)S(1)}, bf16[2,32,2048]{2,1,0:T(8,128)(2,1)S(1)}, u32[]{:S(2)}, u32[]{:S(2)}) %collective-permute-start.30) | collective-permute-done | bytes 262176 | tf_op jit(solution)/shard_map/ppermute | solution.py:301
  109.3 2.5 %collective-permute-done.32 = bf16[2,32,2048]{2,1,0:T(8,128)(2,1)S(1)} collective-permute-done((bf16[2,32,2048]{2,1,0:T(8,128)(2,1)S(1)}, bf16[2,32,2048]{2,1,0:T(8,128)(2,1)S(1)}, u32[]{:S(2)}, u32[]{:S(2)}) %collective-permute-start.32) | collective-permute-done | bytes 262176 | tf_op jit(solution)/shard_map/ppermute | solution.py:301
  112.4 3.5 %collective-permute-start.34 = (f32[2,32,512]{2,1,0:T(8,128)S(1)}, f32[2,32,512]{2,1,0:T(8,128)S(1)}, u32[]{:S(2)}, u32[]{:S(2)}) collective-permute-start(f32[2,32,512]{2,1,0:T(8,128)S(1)} %get-tuple-element.58), channel_id=1, source_target_pairs={{0,2},{1,3},{2,0},{3,1},{4,6},{5,7},{6,4},{7,5},{8,10},{9,11},{10,... | collective-permute-start | bytes 393224 | tf_op jit(solution)/shard_map/ppermute | solution.py:304
  116.9 2.0 %collective-permute-done.33 = f32[2,32,512]{2,1,0:T(8,128)S(1)} collective-permute-done((f32[2,32,512]{2,1,0:T(8,128)S(1)}, f32[2,32,512]{2,1,0:T(8,128)S(1)}, u32[]{:S(2)}, u32[]{:S(2)}) %collective-permute-start.33) | collective-permute-done | bytes 131104 | tf_op jit(solution)/shard_map/ppermute | solution.py:304
  (78 shorter events, 41.9 us)
Async XLA Ops:
  2.7 13.7 %collective-permute-start = (bf16[128,2176]{1,0:T(8,128)(2,1)}, bf16[128,2176]{1,0:T(8,128)(2,1)S(1)}, u32[]{:S(2)}, u32[]{:S(2)}) collective-permute-start(bf16[128,2176]{1,0:T(8,128)(2,1)} %shard_map.86.refs_0_), channel_id=1, source_target_pairs={{0,32},{4,228},{8,40},{12,236},{16,48},{20,244},{24,56},{28,252},{... | collective-permute-start | bytes 1671176 | tf_op jit(solution)/shard_map/ppermute | solution.py:339
  5.0 18.9 %collective-permute-start.6 = (bf16[128,2176]{1,0:T(8,128)(2,1)}, bf16[128,2176]{1,0:T(8,128)(2,1)S(1)}, u32[]{:S(2)}, u32[]{:S(2)}) collective-permute-start(bf16[128,2176]{1,0:T(8,128)(2,1)} %collective-permute-done.5.refs_1_), channel_id=1, source_target_pairs={{0,32},{4,228},{8,40},{12,236},{16,48},{20,244},{24,56},{28,252},{... | collective-permute-start | bytes 1671176 | tf_op jit(solution)/shard_map/ppermute | solution.py:339
  9.6 14.5 %collective-permute-start.10 = (bf16[2,64,2048]{2,1,0:T(8,128)(2,1)S(1)}, bf16[2,64,2048]{2,1,0:T(8,128)(2,1)}, u32[]{:S(2)}, u32[]{:S(2)}) collective-permute-start(bf16[2,64,2048]{2,1,0:T(8,128)(2,1)S(1)} %shard_map.89.refs_6_), channel_id=1, source_target_pairs={{0,8},{4,12},{8,16},{12,20},{16,24},{20,28},{24,0},{28,4},{32,40},... | collective-permute-start | bytes 1572872 | tf_op jit(solution)/shard_map/ppermute | solution.py:301
  10.2 14.0 %collective-permute-start.9 = (bf16[2,64,2048]{2,1,0:T(8,128)(2,1)S(1)}, bf16[2,64,2048]{2,1,0:T(8,128)(2,1)}, u32[]{:S(2)}, u32[]{:S(2)}) collective-permute-start(bf16[2,64,2048]{2,1,0:T(8,128)(2,1)S(1)} %shard_map.89.refs_6_), channel_id=1, source_target_pairs={{0,24},{4,28},{8,0},{12,4},{16,8},{20,12},{24,16},{28,20},{32,56},... | collective-permute-start | bytes 1572872 | tf_op jit(solution)/shard_map/ppermute | solution.py:301
  16.4 11.9 %collective-permute-start.2 = (bf16[128,2176]{1,0:T(8,128)(2,1)S(1)}, bf16[128,2176]{1,0:T(8,128)(2,1)S(1)}, u32[]{:S(2)}, u32[]{:S(2)}) collective-permute-start(bf16[128,2176]{1,0:T(8,128)(2,1)S(1)} %shard_map.87.refs_2_), channel_id=1, source_target_pairs={{0,32},{4,228},{8,40},{12,236},{16,48},{20,244},{24,56},{28,252},{... | collective-permute-start | bytes 1671176 | tf_op jit(solution)/shard_map/ppermute | solution.py:339
  22.6 14.6 %collective-permute-start.14 = (bf16[128,2176]{1,0:T(8,128)(2,1)S(1)}, bf16[128,2176]{1,0:T(8,128)(2,1)S(1)}, u32[]{:S(2)}, u32[]{:S(2)}) collective-permute-start(bf16[128,2176]{1,0:T(8,128)(2,1)S(1)} %shard_map.87.refs_2_), channel_id=1, source_target_pairs={{0,4},{4,0},{8,12},{12,8},{16,20},{20,16},{24,28},{28,24},{32,36},... | collective-permute-start | bytes 1671176 | tf_op jit(solution)/shard_map/ppermute | solution.py:301
  24.0 10.9 %collective-permute-start.8 = (bf16[128,2176]{1,0:T(8,128)(2,1)S(1)}, bf16[128,2176]{1,0:T(8,128)(2,1)S(1)}, u32[]{:S(2)}, u32[]{:S(2)}) collective-permute-start(bf16[128,2176]{1,0:T(8,128)(2,1)S(1)} %shard_map.88.refs_3_), channel_id=1, source_target_pairs={{0,32},{4,228},{8,40},{12,236},{16,48},{20,244},{24,56},{28,252},{... | collective-permute-start | bytes 1671176 | tf_op jit(solution)/shard_map/ppermute | solution.py:339
  25.4 11.0 %collective-permute-start.16 = (bf16[2,64,2048]{2,1,0:T(8,128)(2,1)S(1)}, bf16[2,64,2048]{2,1,0:T(8,128)(2,1)S(1)}, u32[]{:S(2)}, u32[]{:S(2)}) collective-permute-start(bf16[2,64,2048]{2,1,0:T(8,128)(2,1)S(1)} %get-tuple-element.30), channel_id=1, source_target_pairs={{0,24},{4,12},{8,0},{12,20},{16,8},{20,28},{24,16},{28,4},{32,56},... | collective-permute-start | bytes 1572872 | tf_op jit(solution)/shard_map/ppermute | solution.py:339
  28.3 12.5 %collective-permute-start.3 = (bf16[128,2176]{1,0:T(8,128)(2,1)S(1)}, bf16[128,2176]{1,0:T(8,128)(2,1)S(1)}, u32[]{:S(2)}, u32[]{:S(2)}) collective-permute-start(bf16[128,2176]{1,0:T(8,128)(2,1)S(1)} %collective-permute-done.2.refs_0_.refs_6_), channel_id=1, source_target_pairs={{0,32},{4,228},{8,40},{12,236},{16,48},{20,244},{24,56},{28,252},{... | collective-permute-start | bytes 1671176 | tf_op jit(solution)/shard_map/ppermute | solution.py:339
  34.7 7.9 %collective-permute-start.15 = (bf16[128,2176]{1,0:T(8,128)(2,1)S(1)}, bf16[128,2176]{1,0:T(8,128)(2,1)S(1)}, u32[]{:S(2)}, u32[]{:S(2)}) collective-permute-start(bf16[128,2176]{1,0:T(8,128)(2,1)S(1)} %shard_map.88.refs_3_), channel_id=1, source_target_pairs={{0,4},{4,0},{8,12},{12,8},{16,20},{20,16},{24,28},{28,24},{32,36},... | collective-permute-start | bytes 1671176 | tf_op jit(solution)/shard_map/ppermute | solution.py:301
  35.0 14.6 %collective-permute-start.18 = (bf16[128,2176]{1,0:T(8,128)(2,1)S(1)}, bf16[128,2176]{1,0:T(8,128)(2,1)S(1)}, u32[]{:S(2)}, u32[]{:S(2)}) collective-permute-start(bf16[128,2176]{1,0:T(8,128)(2,1)S(1)} %shard_map.91.refs_1_.refs_7_), channel_id=1, source_target_pairs={{0,32},{4,228},{8,40},{12,236},{16,48},{20,244},{24,56},{28,252},{... | collective-permute-start | bytes 1671176 | tf_op jit(solution)/shard_map/ppermute | solution.py:339
  36.5 13.2 %collective-permute-start.12 = (bf16[128,2176]{1,0:T(8,128)(2,1)S(1)}, bf16[128,2176]{1,0:T(8,128)(2,1)S(1)}, u32[]{:S(2)}, u32[]{:S(2)}) collective-permute-start(bf16[128,2176]{1,0:T(8,128)(2,1)S(1)} %collective-permute-done.2.refs_0_.refs_6_), channel_id=1, source_target_pairs={{0,4},{4,0},{8,12},{12,8},{16,20},{20,16},{24,28},{28,24},{32,36},... | collective-permute-start | bytes 1671176 | tf_op jit(solution)/shard_map/ppermute | solution.py:301
  37.1 12.5 %collective-permute-start.13 = (bf16[128,2176]{1,0:T(8,128)(2,1)S(1)}, bf16[128,2176]{1,0:T(8,128)(2,1)S(1)}, u32[]{:S(2)}, u32[]{:S(2)}) collective-permute-start(bf16[128,2176]{1,0:T(8,128)(2,1)S(1)} %shard_map.91.refs_1_.refs_7_), channel_id=1, source_target_pairs={{0,4},{4,0},{8,12},{12,8},{16,20},{20,16},{24,28},{28,24},{32,36},... | collective-permute-start | bytes 1671176 | tf_op jit(solution)/shard_map/ppermute | solution.py:301
  40.8 11.9 %collective-permute-start.4 = (bf16[128,2176]{1,0:T(8,128)(2,1)S(1)}, bf16[128,2176]{1,0:T(8,128)(2,1)S(1)}, u32[]{:S(2)}, u32[]{:S(2)}) collective-permute-start(bf16[128,2176]{1,0:T(8,128)(2,1)S(1)} %collective-permute-done.3.refs_0_.refs_10_), channel_id=1, source_target_pairs={{0,32},{4,228},{8,40},{12,236},{16,48},{20,244},{24,56},{28,252},{... | collective-permute-start | bytes 1671176 | tf_op jit(solution)/shard_map/ppermute | solution.py:339
  42.6 10.2 %collective-permute-start.19 = (bf16[128,2176]{1,0:T(8,128)(2,1)S(1)}, bf16[128,2176]{1,0:T(8,128)(2,1)S(1)}, u32[]{:S(2)}, u32[]{:S(2)}) collective-permute-start(bf16[128,2176]{1,0:T(8,128)(2,1)S(1)} %collective-permute-done.3.refs_0_.refs_10_), channel_id=1, source_target_pairs={{0,4},{4,0},{8,12},{12,8},{16,20},{20,16},{24,28},{28,24},{32,36},... | collective-permute-start | bytes 1671176 | tf_op jit(solution)/shard_map/ppermute | solution.py:301
  67.0 7.0 %collective-permute-start.24 = (bf16[2,32,768]{2,1,0:T(8,128)(2,1)S(1)}, bf16[2,32,768]{2,1,0:T(8,128)(2,1)S(1)}, u32[]{:S(2)}, u32[]{:S(2)}) collective-permute-start(bf16[2,32,768]{2,1,0:T(8,128)(2,1)S(1)} %shard_map.98.refs_0_), channel_id=1, source_target_pairs={{0,1},{1,2},{2,3},{3,0},{4,5},{5,6},{6,7},{7,4},{8,9},{9,10},{10,1... | collective-permute-start | bytes 294920 | tf_op jit(solution)/shard_map/ppermute | solution.py:304
  68.7 6.6 %collective-permute-start.25 = (bf16[2,32,768]{2,1,0:T(8,128)(2,1)S(1)}, bf16[2,32,768]{2,1,0:T(8,128)(2,1)S(1)}, u32[]{:S(2)}, u32[]{:S(2)}) collective-permute-start(bf16[2,32,768]{2,1,0:T(8,128)(2,1)S(1)} %shard_map.98.refs_0_), channel_id=1, source_target_pairs={{0,2},{1,3},{2,0},{3,1},{4,6},{5,7},{6,4},{7,5},{8,10},{9,11},{10,... | collective-permute-start | bytes 294920 | tf_op jit(solution)/shard_map/ppermute | solution.py:304
  81.4 6.2 %collective-permute-start.27 = (f32[2,32,256]{2,1,0:T(8,128)S(1)}, f32[2,32,256]{2,1,0:T(8,128)S(1)}, u32[]{:S(2)}, u32[]{:S(2)}) collective-permute-start(f32[2,32,256]{2,1,0:T(8,128)S(1)} %get-tuple-element.45), channel_id=1, source_target_pairs={{0,24},{4,28},{8,0},{12,4},{16,8},{20,12},{24,16},{28,20},{32,56},... | collective-permute-start | bytes 196616 | tf_op jit(solution)/shard_map/ppermute | solution.py:301
  81.5 6.2 %collective-permute-start.28 = (f32[2,32,256]{2,1,0:T(8,128)S(1)}, f32[2,32,256]{2,1,0:T(8,128)S(1)}, u32[]{:S(2)}, u32[]{:S(2)}) collective-permute-start(f32[2,32,256]{2,1,0:T(8,128)S(1)} %get-tuple-element.46), channel_id=1, source_target_pairs={{0,16},{4,20},{8,24},{12,28},{16,0},{20,4},{24,8},{28,12},{32,48},... | collective-permute-start | bytes 196616 | tf_op jit(solution)/shard_map/ppermute | solution.py:301
  97.0 11.3 %collective-permute-start.30 = (bf16[2,32,2048]{2,1,0:T(8,128)(2,1)S(1)}, bf16[2,32,2048]{2,1,0:T(8,128)(2,1)S(1)}, u32[]{:S(2)}, u32[]{:S(2)}) collective-permute-start(bf16[2,32,2048]{2,1,0:T(8,128)(2,1)S(1)} %get-tuple-element.53), channel_id=1, source_target_pairs={{0,8},{4,12},{8,16},{12,20},{16,24},{20,28},{24,0},{28,4},{32,40},... | collective-permute-start | bytes 786440 | tf_op jit(solution)/shard_map/ppermute | solution.py:301
  99.7 9.6 %collective-permute-start.31 = (bf16[2,32,2048]{2,1,0:T(8,128)(2,1)S(1)}, bf16[2,32,2048]{2,1,0:T(8,128)(2,1)S(1)}, u32[]{:S(2)}, u32[]{:S(2)}) collective-permute-start(bf16[2,32,2048]{2,1,0:T(8,128)(2,1)S(1)} %get-tuple-element.54), channel_id=1, source_target_pairs={{0,16},{4,20},{8,24},{12,28},{16,0},{20,4},{24,8},{28,12},{32,48},... | collective-permute-start | bytes 786440 | tf_op jit(solution)/shard_map/ppermute | solution.py:301
  100.4 11.4 %collective-permute-start.32 = (bf16[2,32,2048]{2,1,0:T(8,128)(2,1)S(1)}, bf16[2,32,2048]{2,1,0:T(8,128)(2,1)S(1)}, u32[]{:S(2)}, u32[]{:S(2)}) collective-permute-start(bf16[2,32,2048]{2,1,0:T(8,128)(2,1)S(1)} %get-tuple-element.55), channel_id=1, source_target_pairs={{0,24},{4,28},{8,0},{12,4},{16,8},{20,12},{24,16},{28,20},{32,56},... | collective-permute-start | bytes 786440 | tf_op jit(solution)/shard_map/ppermute | solution.py:301
  112.0 6.9 %collective-permute-start.33 = (f32[2,32,512]{2,1,0:T(8,128)S(1)}, f32[2,32,512]{2,1,0:T(8,128)S(1)}, u32[]{:S(2)}, u32[]{:S(2)}) collective-permute-start(f32[2,32,512]{2,1,0:T(8,128)S(1)} %get-tuple-element.56), channel_id=1, source_target_pairs={{0,1},{1,2},{2,3},{3,0},{4,5},{5,6},{6,7},{7,4},{8,9},{9,10},{10,1... | collective-permute-start | bytes 393224 | tf_op jit(solution)/shard_map/ppermute | solution.py:304
  112.4 7.9 %collective-permute-start.34 = (f32[2,32,512]{2,1,0:T(8,128)S(1)}, f32[2,32,512]{2,1,0:T(8,128)S(1)}, u32[]{:S(2)}, u32[]{:S(2)}) collective-permute-start(f32[2,32,512]{2,1,0:T(8,128)S(1)} %get-tuple-element.58), channel_id=1, source_target_pairs={{0,2},{1,3},{2,0},{3,1},{4,6},{5,7},{6,4},{7,5},{8,10},{9,11},{10,... | collective-permute-start | bytes 393224 | tf_op jit(solution)/shard_map/ppermute | solution.py:304
  (17 other events, 185.3 us)

commit v5 on v4

--- a/solution.py
+++ b/solution.py
@@ -222,11 +222,11 @@
         inverse = (work[i] / jnp.sqrt(diag))[:, :rank]
         basis = dot(inverse, sk[i], NN, HIGHEST)
         basis_ref[i] = basis
-        b = stacked(basis / ff)
+        hi, low = split(basis / ff)
         for d in range(nd):
             h = h_ref[i, :, lax.rem(meta_ref[1] + d, nd)]
             h = h.reshape(-1, h.shape[-1])
-            zs[d][i] = folded(dot(b, h, NT))
+            zs[d][i] = (dot(h, hi, NT) + dot(h, low, NT)).T
 
 
 def own_kernel(meta_ref, basis_ref, left_ref, r_ref, out_ref, mom_ref):

time: 122 us -> 123 us (level)
  Pallas kernels: 34.2 us -> 35.6 us
    pallas_call x16, Pallas kernels: 34.2 us -> 35.6 us  [call(): pl.pallas_call(kernel, out_shape=outs, in_specs=specs or [VMEM] * len(arg...]
where the time goes in v5:
time: 123 us
  waiting for transfers between devices  42.8 us (35%)
  starting transfers between devices  41.7 us (34%)
  Pallas kernels  35.6 us (29%)
    pallas_call x16, Pallas kernels, call(): pl.pallas_call(kernel, out_shape=outs, in_specs=specs or [VMEM] * len(arg...  35.6 us
    ppermute x19, waiting for transfers between devices, shift(): return lax.ppermute(v, 'expert', pairs)  18.2 us
    ppermute x9, starting transfers between devices, shift_y(): return lax.ppermute(v, 'zero', [(a, (a + dy) % ny) for a in range(ny)])  17.2 us
    ppermute x19, starting transfers between devices, shift(): return lax.ppermute(v, 'expert', pairs)  17 us
    ppermute x9, waiting for transfers between devices, shift_y(): return lax.ppermute(v, 'zero', [(a, (a + dy) % ny) for a in range(ny)])  14.3 us
    ppermute x8, waiting for transfers between devices, along(): return lax.ppermute(v, 'expert', pairs)  10.4 us
    ppermute x8, starting transfers between devices, along(): return lax.ppermute(v, 'expert', pairs)  7.55 us
  transfers between devices with their start and end apart: 36, of which 22 were waited for; matrix products, arithmetic and copies ran while one was open for 0% of the time, Pallas kernels for 12%

profile of v5, /device:TPU:6, one launch (start us, length us, event | category | flops | bytes accessed | tf_op | source)
XLA Modules:
  0.0 122.9 jit_solution(11324666381664722143)
XLA Ops:
  0.7 2.0 %shard_map.86.refs_0_ = bf16[128,2176]{1,0:T(8,128)(2,1)} custom-call(bf16[128,2048]{1,0:T(8,128)(2,1)} %cot_ref.1, f32[8,128]{1,0:T(8,128)} %bitcast.16, s32[8,128]{1,0:T(8,128)} %bitcast.17), custom_call_target="tpu_custom_call" | custom-call | tf_op jit(solution)/shard_map/pallas_call | solution.py:45
  2.7 2.0 %collective-permute-start = (bf16[128,2176]{1,0:T(8,128)(2,1)}, bf16[128,2176]{1,0:T(8,128)(2,1)S(1)}, u32[]{:S(2)}, u32[]{:S(2)}) collective-permute-start(bf16[128,2176]{1,0:T(8,128)(2,1)} %shard_map.86.refs_0_), channel_id=1, source_target_pairs={{0,32},{4,228},{8,40},{12,236},{16,48},{20,244},{24,56},{28,252},{... | collective-permute-start | bytes 1671176 | tf_op jit(solution)/shard_map/ppermute | solution.py:339
  12.6 3.8 %collective-permute-done.refs_0_ = bf16[128,2176]{1,0:T(8,128)(2,1)S(1)} collective-permute-done((bf16[128,2176]{1,0:T(8,128)(2,1)}, bf16[128,2176]{1,0:T(8,128)(2,1)S(1)}, u32[]{:S(2)}, u32[]{:S(2)}) %collective-permute-start) | collective-permute-done | bytes 557088 | tf_op jit(solution)/shard_map/ppermute | solution.py:339
  16.5 3.3 %collective-permute-start.7 = (f32[2,32,192]{2,1,0:T(8,128)}, f32[2,32,192]{2,1,0:T(8,128)S(1)}, u32[]{:S(2)}, u32[]{:S(2)}) collective-permute-start(f32[2,32,192]{2,1,0:T(8,128)} %bitcast.6.refs_0_), channel_id=1, source_target_pairs={{0,2},{1,3},{2,0},{3,1},{4,6},{5,7},{6,4},{7,5},{8,10},{9,11},{10,... | collective-permute-start | bytes 147464 | tf_op jit(solution)/shard_map/ppermute | solution.py:304
  19.8 2.8 %collective-permute-done.7.refs_1_.refs_2_ = f32[2,32,192]{2,1,0:T(8,128)S(1)} collective-permute-done((f32[2,32,192]{2,1,0:T(8,128)}, f32[2,32,192]{2,1,0:T(8,128)S(1)}, u32[]{:S(2)}, u32[]{:S(2)}) %collective-permute-start.7) | collective-permute-done | bytes 49184 | tf_op jit(solution)/shard_map/ppermute | solution.py:304
  26.0 2.4 %collective-permute-done.2.refs_0_.refs_6_ = bf16[128,2176]{1,0:T(8,128)(2,1)S(1)} collective-permute-done((bf16[128,2176]{1,0:T(8,128)(2,1)S(1)}, bf16[128,2176]{1,0:T(8,128)(2,1)S(1)}, u32[]{:S(2)}, u32[]{:S(2)}) %collective-permute-start.2) | collective-permute-done | bytes 557088 | tf_op jit(solution)/shard_map/ppermute | solution.py:339
  31.3 3.4 %collective-permute-done.11.refs_2_.refs_3_ = f32[2,32,192]{2,1,0:T(8,128)S(1)} collective-permute-done((f32[2,32,192]{2,1,0:T(8,128)}, f32[2,32,192]{2,1,0:T(8,128)S(1)}, u32[]{:S(2)}, u32[]{:S(2)}) %collective-permute-start.11) | collective-permute-done | bytes 49184 | tf_op jit(solution)/shard_map/ppermute | solution.py:304
  37.2 3.5 %collective-permute-done.3.refs_0_.refs_10_ = bf16[128,2176]{1,0:T(8,128)(2,1)S(1)} collective-permute-done((bf16[128,2176]{1,0:T(8,128)(2,1)S(1)}, bf16[128,2176]{1,0:T(8,128)(2,1)S(1)}, u32[]{:S(2)}, u32[]{:S(2)}) %collective-permute-start.3) | collective-permute-done | bytes 557088 | tf_op jit(solution)/shard_map/ppermute | solution.py:339
  44.4 5.1 %shard_map.92 = (f32[8,32,256]{2,1,0:T(8,128)S(1)}, bf16[512,2048]{1,0:T(8,128)(2,1)S(1)}, f32[96,128]{1,0:T(8,128)S(1)}) custom-call(s32[4]{0:T(128)S(1)} %pad_add_fusion.meta_ref, bf16[128,2176]{1,0:T(8,128)(2,1)S(1)} %copy-done.3, bf16[128,2176]{1,0:T(8,128)(2,1)} %collective-permute-done.5.refs_1_, bf16[128,2176]{1,0:T(8,128)(2,1)S(1)} %shard_map.87.refs_2_, ...), custom_call_target="tpu_custom_call" | custom-call | flops 1610612736 | bytes 3221225 | tf_op jit(solution)/shard_map/pallas_call | solution.py:45
  49.7 2.4 %shard_map.93 = (f32[8,32,256]{2,1,0:T(8,128)S(1)}, f32[64,128]{1,0:T(8,128)S(1)}) custom-call(s32[4]{0:T(128)S(1)} %pad_add_fusion.meta_ref, bf16[128,2176]{1,0:T(8,128)(2,1)S(1)} %collective-permute-done.2.refs_0_.refs_6_, bf16[128,2176]{1,0:T(8,128)(2,1)S(1)} %shard_map.91.refs_1_.refs_7_, bf16[128,2176]{1,0:T(8,128)(2,1)S(1)} %collective-permute-done.12.refs_2_.refs_8_, ...), custom_call_target="tpu_custom_call" | custom-call | flops 1073741824 | bytes 2147483 | tf_op jit(solution)/shard_map/pallas_call | solution.py:45
  52.9 2.4 %shard_map.96 = (f32[8,32,256]{2,1,0:T(8,128)S(1)}, f32[64,128]{1,0:T(8,128)S(1)}) custom-call(s32[4]{0:T(128)S(1)} %pad_add_fusion.meta_ref, bf16[128,2176]{1,0:T(8,128)(2,1)S(1)} %collective-permute-done.3.refs_0_.refs_10_, bf16[128,2176]{1,0:T(8,128)(2,1)S(1)} %collective-permute-done.18.refs_1_.refs_11_, ...), custom_call_target="tpu_custom_call" | custom-call | flops 1073741824 | bytes 2147483 | tf_op jit(solution)/shard_map/pallas_call | solution.py:45
  55.3 2.1 %shard_map.97 = (f32[2,32,256]{2,1,0:T(8,128)S(1)}, f32[2,32,256]{2,1,0:T(8,128)S(1)}, f32[2,32,256]{2,1,0:T(8,128)S(1)}, f32[2,32,256]{2,1,0:T(8,128)S(1)}, f32[32,128]{1,0:T(8,128)S(1)}) custom-call(s32[4]{0:T(128)S(1)} %pad_add_fusion.meta_ref, bf16[128,2176]{1,0:T(8,128)(2,1)S(1)} %shard_map.95.refs_0_.refs_14_, ...), custom_call_target="tpu_custom_call" | custom-call | flops 536870912 | bytes 1073741 | tf_op jit(solution)/shard_map/pallas_call | solution.py:45
  60.2 2.2 %collective-permute-done.21.refs_1_ = f32[2,32,256]{2,1,0:T(8,128)S(1)} collective-permute-done((f32[2,32,256]{2,1,0:T(8,128)S(1)}, f32[2,32,256]{2,1,0:T(8,128)S(1)}, u32[]{:S(2)}, u32[]{:S(2)}) %collective-permute-start.21) | collective-permute-done | bytes 65568 | tf_op jit(solution)/shard_map/ppermute | solution.py:301
  62.3 2.5 %collective-permute-done.22.refs_2_ = f32[2,32,256]{2,1,0:T(8,128)S(1)} collective-permute-done((f32[2,32,256]{2,1,0:T(8,128)S(1)}, f32[2,32,256]{2,1,0:T(8,128)S(1)}, u32[]{:S(2)}, u32[]{:S(2)}) %collective-permute-start.22) | collective-permute-done | bytes 65568 | tf_op jit(solution)/shard_map/ppermute | solution.py:301
  68.7 2.7 %collective-permute-start.25 = (bf16[2,32,768]{2,1,0:T(8,128)(2,1)S(1)}, bf16[2,32,768]{2,1,0:T(8,128)(2,1)S(1)}, u32[]{:S(2)}, u32[]{:S(2)}) collective-permute-start(bf16[2,32,768]{2,1,0:T(8,128)(2,1)S(1)} %shard_map.98.refs_0_), channel_id=1, source_target_pairs={{0,2},{1,3},{2,0},{3,1},{4,6},{5,7},{6,4},{7,5},{8,10},{9,11},{10,... | collective-permute-start | bytes 294920 | tf_op jit(solution)/shard_map/ppermute | solution.py:304
  76.1 6.7 %shard_map.99 = (f32[2,32,768]{2,1,0:T(8,128)S(1)}, f32[2,32,256]{2,1,0:T(8,128)S(1)}, f32[2,32,256]{2,1,0:T(8,128)S(1)}, f32[2,32,256]{2,1,0:T(8,128)S(1)}, f32[2,32,256]{2,1,0:T(8,128)S(1)}) custom-call(s32[4]{0:T(128)S(1)} %pad_add_fusion.meta_ref, bf16[2,32,768]{2,1,0:T(8,128)(2,1)S(1)} %shard_map.98.refs_0_, ...), custom_call_target="tpu_custom_call" | custom-call | tf_op jit(solution)/shard_map/pallas_call | solution.py:45
  82.8 2.2 %collective-permute-start.28 = (f32[2,32,256]{2,1,0:T(8,128)S(1)}, f32[2,32,256]{2,1,0:T(8,128)S(1)}, u32[]{:S(2)}, u32[]{:S(2)}) collective-permute-start(f32[2,32,256]{2,1,0:T(8,128)S(1)} %get-tuple-element.46), channel_id=1, source_target_pairs={{0,16},{4,20},{8,24},{12,28},{16,0},{20,4},{24,8},{28,12},{32,48},... | collective-permute-start | bytes 196616 | tf_op jit(solution)/shard_map/ppermute | solution.py:301
  86.8 2.0 %shard_map.100 = (f32[2,32,192]{2,1,0:T(8,128)}, f32[2,32,512]{2,1,0:T(8,128)S(1)}) custom-call(s32[4]{0:T(128)S(1)} %pad_add_fusion.meta_ref, f32[2,32,768]{2,1,0:T(8,128)S(1)} %get-tuple-element.41.basis_ref, f32[2,32,768]{2,1,0:T(8,128)S(1)} %get-tuple-element.42.left_ref, f32[2,32,512]{2,1,0:T(8,128)S(1)} %copy-done.4), custom_call_target="tpu_custom_call" | custom-call | tf_op jit(solution)/shard_map/pallas_call | solution.py:45
  89.9 8.4 %shard_map.101 = (f32[2,32,2048]{2,1,0:T(8,128)S(1)}, bf16[2,32,2048]{2,1,0:T(8,128)(2,1)S(1)}, bf16[2,32,2048]{2,1,0:T(8,128)(2,1)S(1)}, bf16[2,32,2048]{2,1,0:T(8,128)(2,1)S(1)}) custom-call(bf16[128,2176]{1,0:T(8,128)(2,1)S(1)} %copy-done.3, bf16[128,2176]{1,0:T(8,128)(2,1)} %collective-permute-done.5.refs_1_, bf16[128,2176]{1,0:T(8,128)(2,1)S(1)} %shard_map.87.refs_2_, ...), custom_call_target="tpu_custom_call" | custom-call | flops 4294967296 | bytes 8589934 | tf_op jit(solution)/shard_map/pallas_call | solution.py:45
  98.3 2.8 %collective-permute-start.30 = (bf16[2,32,2048]{2,1,0:T(8,128)(2,1)S(1)}, bf16[2,32,2048]{2,1,0:T(8,128)(2,1)S(1)}, u32[]{:S(2)}, u32[]{:S(2)}) collective-permute-start(bf16[2,32,2048]{2,1,0:T(8,128)(2,1)S(1)} %get-tuple-element.53), channel_id=1, source_target_pairs={{0,8},{4,12},{8,16},{12,20},{16,24},{20,28},{24,0},{28,4},{32,40},... | collective-permute-start | bytes 786440 | tf_op jit(solution)/shard_map/ppermute | solution.py:301
  102.0 7.6 %collective-permute-done.30 = bf16[2,32,2048]{2,1,0:T(8,128)(2,1)S(1)} collective-permute-done((bf16[2,32,2048]{2,1,0:T(8,128)(2,1)S(1)}, bf16[2,32,2048]{2,1,0:T(8,128)(2,1)S(1)}, u32[]{:S(2)}, u32[]{:S(2)}) %collective-permute-start.30) | collective-permute-done | bytes 262176 | tf_op jit(solution)/shard_map/ppermute | solution.py:301
  110.6 2.5 %collective-permute-done.32 = bf16[2,32,2048]{2,1,0:T(8,128)(2,1)S(1)} collective-permute-done((bf16[2,32,2048]{2,1,0:T(8,128)(2,1)S(1)}, bf16[2,32,2048]{2,1,0:T(8,128)(2,1)S(1)}, u32[]{:S(2)}, u32[]{:S(2)}) %collective-permute-start.32) | collective-permute-done | bytes 262176 | tf_op jit(solution)/shard_map/ppermute | solution.py:301
  113.7 3.5 %collective-permute-start.34 = (f32[2,32,512]{2,1,0:T(8,128)S(1)}, f32[2,32,512]{2,1,0:T(8,128)S(1)}, u32[]{:S(2)}, u32[]{:S(2)}) collective-permute-start(f32[2,32,512]{2,1,0:T(8,128)S(1)} %get-tuple-element.58), channel_id=1, source_target_pairs={{0,2},{1,3},{2,0},{3,1},{4,6},{5,7},{6,4},{7,5},{8,10},{9,11},{10,... | collective-permute-start | bytes 393224 | tf_op jit(solution)/shard_map/ppermute | solution.py:304
  118.2 2.0 %collective-permute-done.33 = f32[2,32,512]{2,1,0:T(8,128)S(1)} collective-permute-done((f32[2,32,512]{2,1,0:T(8,128)S(1)}, f32[2,32,512]{2,1,0:T(8,128)S(1)}, u32[]{:S(2)}, u32[]{:S(2)}) %collective-permute-start.33) | collective-permute-done | bytes 131104 | tf_op jit(solution)/shard_map/ppermute | solution.py:304
  (78 shorter events, 41.9 us)
Async XLA Ops:
  2.7 13.7 %collective-permute-start = (bf16[128,2176]{1,0:T(8,128)(2,1)}, bf16[128,2176]{1,0:T(8,128)(2,1)S(1)}, u32[]{:S(2)}, u32[]{:S(2)}) collective-permute-start(bf16[128,2176]{1,0:T(8,128)(2,1)} %shard_map.86.refs_0_), channel_id=1, source_target_pairs={{0,32},{4,228},{8,40},{12,236},{16,48},{20,244},{24,56},{28,252},{... | collective-permute-start | bytes 1671176 | tf_op jit(solution)/shard_map/ppermute | solution.py:339
  5.0 18.9 %collective-permute-start.6 = (bf16[128,2176]{1,0:T(8,128)(2,1)}, bf16[128,2176]{1,0:T(8,128)(2,1)S(1)}, u32[]{:S(2)}, u32[]{:S(2)}) collective-permute-start(bf16[128,2176]{1,0:T(8,128)(2,1)} %collective-permute-done.5.refs_1_), channel_id=1, source_target_pairs={{0,32},{4,228},{8,40},{12,236},{16,48},{20,244},{24,56},{28,252},{... | collective-permute-start | bytes 1671176 | tf_op jit(solution)/shard_map/ppermute | solution.py:339
  9.6 14.5 %collective-permute-start.10 = (bf16[2,64,2048]{2,1,0:T(8,128)(2,1)S(1)}, bf16[2,64,2048]{2,1,0:T(8,128)(2,1)}, u32[]{:S(2)}, u32[]{:S(2)}) collective-permute-start(bf16[2,64,2048]{2,1,0:T(8,128)(2,1)S(1)} %shard_map.89.refs_6_), channel_id=1, source_target_pairs={{0,8},{4,12},{8,16},{12,20},{16,24},{20,28},{24,0},{28,4},{32,40},... | collective-permute-start | bytes 1572872 | tf_op jit(solution)/shard_map/ppermute | solution.py:301
  10.2 14.0 %collective-permute-start.9 = (bf16[2,64,2048]{2,1,0:T(8,128)(2,1)S(1)}, bf16[2,64,2048]{2,1,0:T(8,128)(2,1)}, u32[]{:S(2)}, u32[]{:S(2)}) collective-permute-start(bf16[2,64,2048]{2,1,0:T(8,128)(2,1)S(1)} %shard_map.89.refs_6_), channel_id=1, source_target_pairs={{0,24},{4,28},{8,0},{12,4},{16,8},{20,12},{24,16},{28,20},{32,56},... | collective-permute-start | bytes 1572872 | tf_op jit(solution)/shard_map/ppermute | solution.py:301
  16.4 11.9 %collective-permute-start.2 = (bf16[128,2176]{1,0:T(8,128)(2,1)S(1)}, bf16[128,2176]{1,0:T(8,128)(2,1)S(1)}, u32[]{:S(2)}, u32[]{:S(2)}) collective-permute-start(bf16[128,2176]{1,0:T(8,128)(2,1)S(1)} %shard_map.87.refs_2_), channel_id=1, source_target_pairs={{0,32},{4,228},{8,40},{12,236},{16,48},{20,244},{24,56},{28,252},{... | collective-permute-start | bytes 1671176 | tf_op jit(solution)/shard_map/ppermute | solution.py:339
  22.6 14.6 %collective-permute-start.14 = (bf16[128,2176]{1,0:T(8,128)(2,1)S(1)}, bf16[128,2176]{1,0:T(8,128)(2,1)S(1)}, u32[]{:S(2)}, u32[]{:S(2)}) collective-permute-start(bf16[128,2176]{1,0:T(8,128)(2,1)S(1)} %shard_map.87.refs_2_), channel_id=1, source_target_pairs={{0,4},{4,0},{8,12},{12,8},{16,20},{20,16},{24,28},{28,24},{32,36},... | collective-permute-start | bytes 1671176 | tf_op jit(solution)/shard_map/ppermute | solution.py:301
  24.0 10.9 %collective-permute-start.8 = (bf16[128,2176]{1,0:T(8,128)(2,1)S(1)}, bf16[128,2176]{1,0:T(8,128)(2,1)S(1)}, u32[]{:S(2)}, u32[]{:S(2)}) collective-permute-start(bf16[128,2176]{1,0:T(8,128)(2,1)S(1)} %shard_map.88.refs_3_), channel_id=1, source_target_pairs={{0,32},{4,228},{8,40},{12,236},{16,48},{20,244},{24,56},{28,252},{... | collective-permute-start | bytes 1671176 | tf_op jit(solution)/shard_map/ppermute | solution.py:339
  25.4 11.0 %collective-permute-start.16 = (bf16[2,64,2048]{2,1,0:T(8,128)(2,1)S(1)}, bf16[2,64,2048]{2,1,0:T(8,128)(2,1)S(1)}, u32[]{:S(2)}, u32[]{:S(2)}) collective-permute-start(bf16[2,64,2048]{2,1,0:T(8,128)(2,1)S(1)} %get-tuple-element.30), channel_id=1, source_target_pairs={{0,24},{4,12},{8,0},{12,20},{16,8},{20,28},{24,16},{28,4},{32,56},... | collective-permute-start | bytes 1572872 | tf_op jit(solution)/shard_map/ppermute | solution.py:339
  28.3 12.5 %collective-permute-start.3 = (bf16[128,2176]{1,0:T(8,128)(2,1)S(1)}, bf16[128,2176]{1,0:T(8,128)(2,1)S(1)}, u32[]{:S(2)}, u32[]{:S(2)}) collective-permute-start(bf16[128,2176]{1,0:T(8,128)(2,1)S(1)} %collective-permute-done.2.refs_0_.refs_6_), channel_id=1, source_target_pairs={{0,32},{4,228},{8,40},{12,236},{16,48},{20,244},{24,56},{28,252},{... | collective-permute-start | bytes 1671176 | tf_op jit(solution)/shard_map/ppermute | solution.py:339
  34.7 7.9 %collective-permute-start.15 = (bf16[128,2176]{1,0:T(8,128)(2,1)S(1)}, bf16[128,2176]{1,0:T(8,128)(2,1)S(1)}, u32[]{:S(2)}, u32[]{:S(2)}) collective-permute-start(bf16[128,2176]{1,0:T(8,128)(2,1)S(1)} %shard_map.88.refs_3_), channel_id=1, source_target_pairs={{0,4},{4,0},{8,12},{12,8},{16,20},{20,16},{24,28},{28,24},{32,36},... | collective-permute-start | bytes 1671176 | tf_op jit(solution)/shard_map/ppermute | solution.py:301
  35.0 14.6 %collective-permute-start.18 = (bf16[128,2176]{1,0:T(8,128)(2,1)S(1)}, bf16[128,2176]{1,0:T(8,128)(2,1)S(1)}, u32[]{:S(2)}, u32[]{:S(2)}) collective-permute-start(bf16[128,2176]{1,0:T(8,128)(2,1)S(1)} %shard_map.91.refs_1_.refs_7_), channel_id=1, source_target_pairs={{0,32},{4,228},{8,40},{12,236},{16,48},{20,244},{24,56},{28,252},{... | collective-permute-start | bytes 1671176 | tf_op jit(solution)/shard_map/ppermute | solution.py:339
  36.5 13.2 %collective-permute-start.12 = (bf16[128,2176]{1,0:T(8,128)(2,1)S(1)}, bf16[128,2176]{1,0:T(8,128)(2,1)S(1)}, u32[]{:S(2)}, u32[]{:S(2)}) collective-permute-start(bf16[128,2176]{1,0:T(8,128)(2,1)S(1)} %collective-permute-done.2.refs_0_.refs_6_), channel_id=1, source_target_pairs={{0,4},{4,0},{8,12},{12,8},{16,20},{20,16},{24,28},{28,24},{32,36},... | collective-permute-start | bytes 1671176 | tf_op jit(solution)/shard_map/ppermute | solution.py:301
  37.1 12.5 %collective-permute-start.13 = (bf16[128,2176]{1,0:T(8,128)(2,1)S(1)}, bf16[128,2176]{1,0:T(8,128)(2,1)S(1)}, u32[]{:S(2)}, u32[]{:S(2)}) collective-permute-start(bf16[128,2176]{1,0:T(8,128)(2,1)S(1)} %shard_map.91.refs_1_.refs_7_), channel_id=1, source_target_pairs={{0,4},{4,0},{8,12},{12,8},{16,20},{20,16},{24,28},{28,24},{32,36},... | collective-permute-start | bytes 1671176 | tf_op jit(solution)/shard_map/ppermute | solution.py:301
  40.8 11.9 %collective-permute-start.4 = (bf16[128,2176]{1,0:T(8,128)(2,1)S(1)}, bf16[128,2176]{1,0:T(8,128)(2,1)S(1)}, u32[]{:S(2)}, u32[]{:S(2)}) collective-permute-start(bf16[128,2176]{1,0:T(8,128)(2,1)S(1)} %collective-permute-done.3.refs_0_.refs_10_), channel_id=1, source_target_pairs={{0,32},{4,228},{8,40},{12,236},{16,48},{20,244},{24,56},{28,252},{... | collective-permute-start | bytes 1671176 | tf_op jit(solution)/shard_map/ppermute | solution.py:339
  42.6 10.2 %collective-permute-start.19 = (bf16[128,2176]{1,0:T(8,128)(2,1)S(1)}, bf16[128,2176]{1,0:T(8,128)(2,1)S(1)}, u32[]{:S(2)}, u32[]{:S(2)}) collective-permute-start(bf16[128,2176]{1,0:T(8,128)(2,1)S(1)} %collective-permute-done.3.refs_0_.refs_10_), channel_id=1, source_target_pairs={{0,4},{4,0},{8,12},{12,8},{16,20},{20,16},{24,28},{28,24},{32,36},... | collective-permute-start | bytes 1671176 | tf_op jit(solution)/shard_map/ppermute | solution.py:301
  67.0 7.0 %collective-permute-start.24 = (bf16[2,32,768]{2,1,0:T(8,128)(2,1)S(1)}, bf16[2,32,768]{2,1,0:T(8,128)(2,1)S(1)}, u32[]{:S(2)}, u32[]{:S(2)}) collective-permute-start(bf16[2,32,768]{2,1,0:T(8,128)(2,1)S(1)} %shard_map.98.refs_0_), channel_id=1, source_target_pairs={{0,1},{1,2},{2,3},{3,0},{4,5},{5,6},{6,7},{7,4},{8,9},{9,10},{10,1... | collective-permute-start | bytes 294920 | tf_op jit(solution)/shard_map/ppermute | solution.py:304
  68.7 6.6 %collective-permute-start.25 = (bf16[2,32,768]{2,1,0:T(8,128)(2,1)S(1)}, bf16[2,32,768]{2,1,0:T(8,128)(2,1)S(1)}, u32[]{:S(2)}, u32[]{:S(2)}) collective-permute-start(bf16[2,32,768]{2,1,0:T(8,128)(2,1)S(1)} %shard_map.98.refs_0_), channel_id=1, source_target_pairs={{0,2},{1,3},{2,0},{3,1},{4,6},{5,7},{6,4},{7,5},{8,10},{9,11},{10,... | collective-permute-start | bytes 294920 | tf_op jit(solution)/shard_map/ppermute | solution.py:304
  82.8 6.2 %collective-permute-start.27 = (f32[2,32,256]{2,1,0:T(8,128)S(1)}, f32[2,32,256]{2,1,0:T(8,128)S(1)}, u32[]{:S(2)}, u32[]{:S(2)}) collective-permute-start(f32[2,32,256]{2,1,0:T(8,128)S(1)} %get-tuple-element.45), channel_id=1, source_target_pairs={{0,24},{4,28},{8,0},{12,4},{16,8},{20,12},{24,16},{28,20},{32,56},... | collective-permute-start | bytes 196616 | tf_op jit(solution)/shard_map/ppermute | solution.py:301
  82.8 6.2 %collective-permute-start.28 = (f32[2,32,256]{2,1,0:T(8,128)S(1)}, f32[2,32,256]{2,1,0:T(8,128)S(1)}, u32[]{:S(2)}, u32[]{:S(2)}) collective-permute-start(f32[2,32,256]{2,1,0:T(8,128)S(1)} %get-tuple-element.46), channel_id=1, source_target_pairs={{0,16},{4,20},{8,24},{12,28},{16,0},{20,4},{24,8},{28,12},{32,48},... | collective-permute-start | bytes 196616 | tf_op jit(solution)/shard_map/ppermute | solution.py:301
  98.3 11.3 %collective-permute-start.30 = (bf16[2,32,2048]{2,1,0:T(8,128)(2,1)S(1)}, bf16[2,32,2048]{2,1,0:T(8,128)(2,1)S(1)}, u32[]{:S(2)}, u32[]{:S(2)}) collective-permute-start(bf16[2,32,2048]{2,1,0:T(8,128)(2,1)S(1)} %get-tuple-element.53), channel_id=1, source_target_pairs={{0,8},{4,12},{8,16},{12,20},{16,24},{20,28},{24,0},{28,4},{32,40},... | collective-permute-start | bytes 786440 | tf_op jit(solution)/shard_map/ppermute | solution.py:301
  101.0 9.6 %collective-permute-start.31 = (bf16[2,32,2048]{2,1,0:T(8,128)(2,1)S(1)}, bf16[2,32,2048]{2,1,0:T(8,128)(2,1)S(1)}, u32[]{:S(2)}, u32[]{:S(2)}) collective-permute-start(bf16[2,32,2048]{2,1,0:T(8,128)(2,1)S(1)} %get-tuple-element.54), channel_id=1, source_target_pairs={{0,16},{4,20},{8,24},{12,28},{16,0},{20,4},{24,8},{28,12},{32,48},... | collective-permute-start | bytes 786440 | tf_op jit(solution)/shard_map/ppermute | solution.py:301
  101.8 11.4 %collective-permute-start.32 = (bf16[2,32,2048]{2,1,0:T(8,128)(2,1)S(1)}, bf16[2,32,2048]{2,1,0:T(8,128)(2,1)S(1)}, u32[]{:S(2)}, u32[]{:S(2)}) collective-permute-start(bf16[2,32,2048]{2,1,0:T(8,128)(2,1)S(1)} %get-tuple-element.55), channel_id=1, source_target_pairs={{0,24},{4,28},{8,0},{12,4},{16,8},{20,12},{24,16},{28,20},{32,56},... | collective-permute-start | bytes 786440 | tf_op jit(solution)/shard_map/ppermute | solution.py:301
  113.3 6.9 %collective-permute-start.33 = (f32[2,32,512]{2,1,0:T(8,128)S(1)}, f32[2,32,512]{2,1,0:T(8,128)S(1)}, u32[]{:S(2)}, u32[]{:S(2)}) collective-permute-start(f32[2,32,512]{2,1,0:T(8,128)S(1)} %get-tuple-element.56), channel_id=1, source_target_pairs={{0,1},{1,2},{2,3},{3,0},{4,5},{5,6},{6,7},{7,4},{8,9},{9,10},{10,1... | collective-permute-start | bytes 393224 | tf_op jit(solution)/shard_map/ppermute | solution.py:304
  113.7 7.9 %collective-permute-start.34 = (f32[2,32,512]{2,1,0:T(8,128)S(1)}, f32[2,32,512]{2,1,0:T(8,128)S(1)}, u32[]{:S(2)}, u32[]{:S(2)}) collective-permute-start(f32[2,32,512]{2,1,0:T(8,128)S(1)} %get-tuple-element.58), channel_id=1, source_target_pairs={{0,2},{1,3},{2,0},{3,1},{4,6},{5,7},{6,4},{7,5},{8,10},{9,11},{10,... | collective-permute-start | bytes 393224 | tf_op jit(solution)/shard_map/ppermute | solution.py:304
  (17 other events, 185.3 us)

commit v6 on v4

--- a/solution.py
+++ b/solution.py
@@ -445,7 +445,7 @@
 
     out = columns(0) + own_mom
     for d in range(1, ny):
-        out = out + shift_y(columns(d), d)
+        out = out + shift_y(columns(d).astype(BF), d).astype(F32)
     return jnp.swapaxes(own_basis, 1, 2), out
 
 

time: 122 us -> 121 us (level)
  transfers between devices with their start and end apart: 36 -> 36, of which waited for: 22 -> 22; matrix products, arithmetic and copies ran while one was open for 0% -> 0% of each run, Pallas kernels for 12% -> 13%
where the time goes in v6:
time: 121 us
  waiting for transfers between devices  42.1 us (35%)
  starting transfers between devices  41.7 us (34%)
  Pallas kernels  34.2 us (28%)
    pallas_call x16, Pallas kernels, call(): pl.pallas_call(kernel, out_shape=outs, in_specs=specs or [VMEM] * len(arg...  34.2 us
    ppermute x19, waiting for transfers between devices, shift(): return lax.ppermute(v, 'expert', pairs)  18.2 us
    ppermute x9, starting transfers between devices, shift_y(): return lax.ppermute(v, 'zero', [(a, (a + dy) % ny) for a in range(ny)])  17.2 us
    ppermute x19, starting transfers between devices, shift(): return lax.ppermute(v, 'expert', pairs)  17 us
    ppermute x9, waiting for transfers between devices, shift_y(): return lax.ppermute(v, 'zero', [(a, (a + dy) % ny) for a in range(ny)])  13.6 us
    ppermute x8, waiting for transfers between devices, along(): return lax.ppermute(v, 'expert', pairs)  10.4 us
    ppermute x8, starting transfers between devices, along(): return lax.ppermute(v, 'expert', pairs)  7.55 us
  transfers between devices with their start and end apart: 36, of which 22 were waited for; matrix products, arithmetic and copies ran while one was open for 0% of the time, Pallas kernels for 13%

profile of v6, /device:TPU:6, one launch (start us, length us, event | category | flops | bytes accessed | tf_op | source)
XLA Modules:
  0.0 120.9 jit_solution(2032347987508430208)
XLA Ops:
  0.7 2.0 %shard_map.86.refs_0_ = bf16[128,2176]{1,0:T(8,128)(2,1)} custom-call(bf16[128,2048]{1,0:T(8,128)(2,1)} %cot_ref.1, f32[8,128]{1,0:T(8,128)} %bitcast.16, s32[8,128]{1,0:T(8,128)} %bitcast.17), custom_call_target="tpu_custom_call" | custom-call | tf_op jit(solution)/shard_map/pallas_call | solution.py:45
  2.7 2.0 %collective-permute-start = (bf16[128,2176]{1,0:T(8,128)(2,1)}, bf16[128,2176]{1,0:T(8,128)(2,1)S(1)}, u32[]{:S(2)}, u32[]{:S(2)}) collective-permute-start(bf16[128,2176]{1,0:T(8,128)(2,1)} %shard_map.86.refs_0_), channel_id=1, source_target_pairs={{0,32},{4,228},{8,40},{12,236},{16,48},{20,244},{24,56},{28,252},{... | collective-permute-start | bytes 1671176 | tf_op jit(solution)/shard_map/ppermute | solution.py:339
  5.0 1.9 %collective-permute-start.6 = (bf16[128,2176]{1,0:T(8,128)(2,1)}, bf16[128,2176]{1,0:T(8,128)(2,1)S(1)}, u32[]{:S(2)}, u32[]{:S(2)}) collective-permute-start(bf16[128,2176]{1,0:T(8,128)(2,1)} %collective-permute-done.5.refs_1_), channel_id=1, source_target_pairs={{0,32},{4,228},{8,40},{12,236},{16,48},{20,244},{24,56},{28,252},{... | collective-permute-start | bytes 1671176 | tf_op jit(solution)/shard_map/ppermute | solution.py:339
  12.6 3.8 %collective-permute-done.refs_0_ = bf16[128,2176]{1,0:T(8,128)(2,1)S(1)} collective-permute-done((bf16[128,2176]{1,0:T(8,128)(2,1)}, bf16[128,2176]{1,0:T(8,128)(2,1)S(1)}, u32[]{:S(2)}, u32[]{:S(2)}) %collective-permute-start) | collective-permute-done | bytes 557088 | tf_op jit(solution)/shard_map/ppermute | solution.py:339
  16.5 3.3 %collective-permute-start.7 = (f32[2,32,192]{2,1,0:T(8,128)}, f32[2,32,192]{2,1,0:T(8,128)S(1)}, u32[]{:S(2)}, u32[]{:S(2)}) collective-permute-start(f32[2,32,192]{2,1,0:T(8,128)} %bitcast.6.refs_0_), channel_id=1, source_target_pairs={{0,2},{1,3},{2,0},{3,1},{4,6},{5,7},{6,4},{7,5},{8,10},{9,11},{10,... | collective-permute-start | bytes 147464 | tf_op jit(solution)/shard_map/ppermute | solution.py:304
  19.8 2.8 %collective-permute-done.7.refs_1_.refs_2_ = f32[2,32,192]{2,1,0:T(8,128)S(1)} collective-permute-done((f32[2,32,192]{2,1,0:T(8,128)}, f32[2,32,192]{2,1,0:T(8,128)S(1)}, u32[]{:S(2)}, u32[]{:S(2)}) %collective-permute-start.7) | collective-permute-done | bytes 49184 | tf_op jit(solution)/shard_map/ppermute | solution.py:304
  26.0 2.4 %collective-permute-done.2.refs_0_.refs_6_ = bf16[128,2176]{1,0:T(8,128)(2,1)S(1)} collective-permute-done((bf16[128,2176]{1,0:T(8,128)(2,1)S(1)}, bf16[128,2176]{1,0:T(8,128)(2,1)S(1)}, u32[]{:S(2)}, u32[]{:S(2)}) %collective-permute-start.2) | collective-permute-done | bytes 557088 | tf_op jit(solution)/shard_map/ppermute | solution.py:339
  31.3 3.4 %collective-permute-done.11.refs_2_.refs_3_ = f32[2,32,192]{2,1,0:T(8,128)S(1)} collective-permute-done((f32[2,32,192]{2,1,0:T(8,128)}, f32[2,32,192]{2,1,0:T(8,128)S(1)}, u32[]{:S(2)}, u32[]{:S(2)}) %collective-permute-start.11) | collective-permute-done | bytes 49184 | tf_op jit(solution)/shard_map/ppermute | solution.py:304
  37.2 3.5 %collective-permute-done.3.refs_0_.refs_10_ = bf16[128,2176]{1,0:T(8,128)(2,1)S(1)} collective-permute-done((bf16[128,2176]{1,0:T(8,128)(2,1)S(1)}, bf16[128,2176]{1,0:T(8,128)(2,1)S(1)}, u32[]{:S(2)}, u32[]{:S(2)}) %collective-permute-start.3) | collective-permute-done | bytes 557088 | tf_op jit(solution)/shard_map/ppermute | solution.py:339
  44.4 5.1 %shard_map.92 = (f32[8,32,256]{2,1,0:T(8,128)S(1)}, bf16[512,2048]{1,0:T(8,128)(2,1)S(1)}, f32[96,128]{1,0:T(8,128)S(1)}) custom-call(s32[4]{0:T(128)S(1)} %pad_add_fusion.meta_ref, bf16[128,2176]{1,0:T(8,128)(2,1)S(1)} %copy-done.3, bf16[128,2176]{1,0:T(8,128)(2,1)} %collective-permute-done.5.refs_1_, bf16[128,2176]{1,0:T(8,128)(2,1)S(1)} %shard_map.87.refs_2_, ...), custom_call_target="tpu_custom_call" | custom-call | flops 1610612736 | bytes 3221225 | tf_op jit(solution)/shard_map/pallas_call | solution.py:45
  49.7 2.4 %shard_map.93 = (f32[8,32,256]{2,1,0:T(8,128)S(1)}, f32[64,128]{1,0:T(8,128)S(1)}) custom-call(s32[4]{0:T(128)S(1)} %pad_add_fusion.meta_ref, bf16[128,2176]{1,0:T(8,128)(2,1)S(1)} %collective-permute-done.2.refs_0_.refs_6_, bf16[128,2176]{1,0:T(8,128)(2,1)S(1)} %shard_map.91.refs_1_.refs_7_, bf16[128,2176]{1,0:T(8,128)(2,1)S(1)} %collective-permute-done.12.refs_2_.refs_8_, ...), custom_call_target="tpu_custom_call" | custom-call | flops 1073741824 | bytes 2147483 | tf_op jit(solution)/shard_map/pallas_call | solution.py:45
  52.9 2.4 %shard_map.96 = (f32[8,32,256]{2,1,0:T(8,128)S(1)}, f32[64,128]{1,0:T(8,128)S(1)}) custom-call(s32[4]{0:T(128)S(1)} %pad_add_fusion.meta_ref, bf16[128,2176]{1,0:T(8,128)(2,1)S(1)} %collective-permute-done.3.refs_0_.refs_10_, bf16[128,2176]{1,0:T(8,128)(2,1)S(1)} %collective-permute-done.18.refs_1_.refs_11_, ...), custom_call_target="tpu_custom_call" | custom-call | flops 1073741824 | bytes 2147483 | tf_op jit(solution)/shard_map/pallas_call | solution.py:45
  55.3 2.1 %shard_map.97 = (f32[2,32,256]{2,1,0:T(8,128)S(1)}, f32[2,32,256]{2,1,0:T(8,128)S(1)}, f32[2,32,256]{2,1,0:T(8,128)S(1)}, f32[2,32,256]{2,1,0:T(8,128)S(1)}, f32[32,128]{1,0:T(8,128)S(1)}) custom-call(s32[4]{0:T(128)S(1)} %pad_add_fusion.meta_ref, bf16[128,2176]{1,0:T(8,128)(2,1)S(1)} %shard_map.95.refs_0_.refs_14_, ...), custom_call_target="tpu_custom_call" | custom-call | flops 536870912 | bytes 1073741 | tf_op jit(solution)/shard_map/pallas_call | solution.py:45
  60.2 2.2 %collective-permute-done.21.refs_1_ = f32[2,32,256]{2,1,0:T(8,128)S(1)} collective-permute-done((f32[2,32,256]{2,1,0:T(8,128)S(1)}, f32[2,32,256]{2,1,0:T(8,128)S(1)}, u32[]{:S(2)}, u32[]{:S(2)}) %collective-permute-start.21) | collective-permute-done | bytes 65568 | tf_op jit(solution)/shard_map/ppermute | solution.py:301
  62.3 2.5 %collective-permute-done.22.refs_2_ = f32[2,32,256]{2,1,0:T(8,128)S(1)} collective-permute-done((f32[2,32,256]{2,1,0:T(8,128)S(1)}, f32[2,32,256]{2,1,0:T(8,128)S(1)}, u32[]{:S(2)}, u32[]{:S(2)}) %collective-permute-start.22) | collective-permute-done | bytes 65568 | tf_op jit(solution)/shard_map/ppermute | solution.py:301
  68.7 2.7 %collective-permute-start.25 = (bf16[2,32,768]{2,1,0:T(8,128)(2,1)S(1)}, bf16[2,32,768]{2,1,0:T(8,128)(2,1)S(1)}, u32[]{:S(2)}, u32[]{:S(2)}) collective-permute-start(bf16[2,32,768]{2,1,0:T(8,128)(2,1)S(1)} %shard_map.98.refs_0_), channel_id=1, source_target_pairs={{0,2},{1,3},{2,0},{3,1},{4,6},{5,7},{6,4},{7,5},{8,10},{9,11},{10,... | collective-permute-start | bytes 294920 | tf_op jit(solution)/shard_map/ppermute | solution.py:304
  76.1 5.4 %shard_map.99 = (f32[2,32,768]{2,1,0:T(8,128)S(1)}, f32[2,32,256]{2,1,0:T(8,128)S(1)}, f32[2,32,256]{2,1,0:T(8,128)S(1)}, f32[2,32,256]{2,1,0:T(8,128)S(1)}, f32[2,32,256]{2,1,0:T(8,128)S(1)}) custom-call(s32[4]{0:T(128)S(1)} %pad_add_fusion.meta_ref, bf16[2,32,768]{2,1,0:T(8,128)(2,1)S(1)} %shard_map.98.refs_0_, ...), custom_call_target="tpu_custom_call" | custom-call | tf_op jit(solution)/shard_map/pallas_call | solution.py:45
  81.5 2.2 %collective-permute-start.28 = (f32[2,32,256]{2,1,0:T(8,128)S(1)}, f32[2,32,256]{2,1,0:T(8,128)S(1)}, u32[]{:S(2)}, u32[]{:S(2)}) collective-permute-start(f32[2,32,256]{2,1,0:T(8,128)S(1)} %get-tuple-element.46), channel_id=1, source_target_pairs={{0,16},{4,20},{8,24},{12,28},{16,0},{20,4},{24,8},{28,12},{32,48},... | collective-permute-start | bytes 196616 | tf_op jit(solution)/shard_map/ppermute | solution.py:301
  85.5 2.0 %shard_map.100 = (f32[2,32,192]{2,1,0:T(8,128)}, f32[2,32,512]{2,1,0:T(8,128)S(1)}) custom-call(s32[4]{0:T(128)S(1)} %pad_add_fusion.meta_ref, f32[2,32,768]{2,1,0:T(8,128)S(1)} %get-tuple-element.41.basis_ref, f32[2,32,768]{2,1,0:T(8,128)S(1)} %get-tuple-element.42.left_ref, f32[2,32,512]{2,1,0:T(8,128)S(1)} %copy-done.4), custom_call_target="tpu_custom_call" | custom-call | tf_op jit(solution)/shard_map/pallas_call | solution.py:45
  88.5 8.4 %shard_map.101 = (f32[2,32,2048]{2,1,0:T(8,128)S(1)}, bf16[2,32,2048]{2,1,0:T(8,128)(2,1)S(1)}, bf16[2,32,2048]{2,1,0:T(8,128)(2,1)S(1)}, bf16[2,32,2048]{2,1,0:T(8,128)(2,1)S(1)}) custom-call(bf16[128,2176]{1,0:T(8,128)(2,1)S(1)} %copy-done.3, bf16[128,2176]{1,0:T(8,128)(2,1)} %collective-permute-done.5.refs_1_, bf16[128,2176]{1,0:T(8,128)(2,1)S(1)} %shard_map.87.refs_2_, ...), custom_call_target="tpu_custom_call" | custom-call | flops 4294967296 | bytes 8589934 | tf_op jit(solution)/shard_map/pallas_call | solution.py:45
  97.0 2.7 %collective-permute-start.30 = (bf16[2,32,2048]{2,1,0:T(8,128)(2,1)S(1)}, bf16[2,32,2048]{2,1,0:T(8,128)(2,1)S(1)}, u32[]{:S(2)}, u32[]{:S(2)}) collective-permute-start(bf16[2,32,2048]{2,1,0:T(8,128)(2,1)S(1)} %get-tuple-element.53), channel_id=1, source_target_pairs={{0,8},{4,12},{8,16},{12,20},{16,24},{20,28},{24,0},{28,4},{32,40},... | collective-permute-start | bytes 786440 | tf_op jit(solution)/shard_map/ppermute | solution.py:301
  100.7 7.6 %collective-permute-done.30 = bf16[2,32,2048]{2,1,0:T(8,128)(2,1)S(1)} collective-permute-done((bf16[2,32,2048]{2,1,0:T(8,128)(2,1)S(1)}, bf16[2,32,2048]{2,1,0:T(8,128)(2,1)S(1)}, u32[]{:S(2)}, u32[]{:S(2)}) %collective-permute-start.30) | collective-permute-done | bytes 262176 | tf_op jit(solution)/shard_map/ppermute | solution.py:301
  109.3 2.5 %collective-permute-done.32 = bf16[2,32,2048]{2,1,0:T(8,128)(2,1)S(1)} collective-permute-done((bf16[2,32,2048]{2,1,0:T(8,128)(2,1)S(1)}, bf16[2,32,2048]{2,1,0:T(8,128)(2,1)S(1)}, u32[]{:S(2)}, u32[]{:S(2)}) %collective-permute-start.32) | collective-permute-done | bytes 262176 | tf_op jit(solution)/shard_map/ppermute | solution.py:301
  112.4 3.5 %collective-permute-start.34 = (bf16[2,32,512]{2,1,0:T(8,128)(2,1)S(1)}, bf16[2,32,512]{2,1,0:T(8,128)(2,1)S(1)}, u32[]{:S(2)}, u32[]{:S(2)}) collective-permute-start(bf16[2,32,512]{2,1,0:T(8,128)(2,1)S(1)} %get-tuple-element.58), channel_id=1, source_target_pairs={{0,2},{1,3},{2,0},{3,1},{4,6},{5,7},{6,4},{7,5},{8,10},{9,11},{10,... | collective-permute-start | bytes 196616 | tf_op jit(solution)/shard_map/ppermute | solution.py:304
  (78 shorter events, 41.3 us)
Async XLA Ops:
  2.7 13.7 %collective-permute-start = (bf16[128,2176]{1,0:T(8,128)(2,1)}, bf16[128,2176]{1,0:T(8,128)(2,1)S(1)}, u32[]{:S(2)}, u32[]{:S(2)}) collective-permute-start(bf16[128,2176]{1,0:T(8,128)(2,1)} %shard_map.86.refs_0_), channel_id=1, source_target_pairs={{0,32},{4,228},{8,40},{12,236},{16,48},{20,244},{24,56},{28,252},{... | collective-permute-start | bytes 1671176 | tf_op jit(solution)/shard_map/ppermute | solution.py:339
  5.0 18.9 %collective-permute-start.6 = (bf16[128,2176]{1,0:T(8,128)(2,1)}, bf16[128,2176]{1,0:T(8,128)(2,1)S(1)}, u32[]{:S(2)}, u32[]{:S(2)}) collective-permute-start(bf16[128,2176]{1,0:T(8,128)(2,1)} %collective-permute-done.5.refs_1_), channel_id=1, source_target_pairs={{0,32},{4,228},{8,40},{12,236},{16,48},{20,244},{24,56},{28,252},{... | collective-permute-start | bytes 1671176 | tf_op jit(solution)/shard_map/ppermute | solution.py:339
  9.6 14.5 %collective-permute-start.10 = (bf16[2,64,2048]{2,1,0:T(8,128)(2,1)S(1)}, bf16[2,64,2048]{2,1,0:T(8,128)(2,1)}, u32[]{:S(2)}, u32[]{:S(2)}) collective-permute-start(bf16[2,64,2048]{2,1,0:T(8,128)(2,1)S(1)} %shard_map.89.refs_6_), channel_id=1, source_target_pairs={{0,8},{4,12},{8,16},{12,20},{16,24},{20,28},{24,0},{28,4},{32,40},... | collective-permute-start | bytes 1572872 | tf_op jit(solution)/shard_map/ppermute | solution.py:301
  10.2 14.0 %collective-permute-start.9 = (bf16[2,64,2048]{2,1,0:T(8,128)(2,1)S(1)}, bf16[2,64,2048]{2,1,0:T(8,128)(2,1)}, u32[]{:S(2)}, u32[]{:S(2)}) collective-permute-start(bf16[2,64,2048]{2,1,0:T(8,128)(2,1)S(1)} %shard_map.89.refs_6_), channel_id=1, source_target_pairs={{0,24},{4,28},{8,0},{12,4},{16,8},{20,12},{24,16},{28,20},{32,56},... | collective-permute-start | bytes 1572872 | tf_op jit(solution)/shard_map/ppermute | solution.py:301
  16.4 11.9 %collective-permute-start.2 = (bf16[128,2176]{1,0:T(8,128)(2,1)S(1)}, bf16[128,2176]{1,0:T(8,128)(2,1)S(1)}, u32[]{:S(2)}, u32[]{:S(2)}) collective-permute-start(bf16[128,2176]{1,0:T(8,128)(2,1)S(1)} %shard_map.87.refs_2_), channel_id=1, source_target_pairs={{0,32},{4,228},{8,40},{12,236},{16,48},{20,244},{24,56},{28,252},{... | collective-permute-start | bytes 1671176 | tf_op jit(solution)/shard_map/ppermute | solution.py:339
  22.6 14.6 %collective-permute-start.14 = (bf16[128,2176]{1,0:T(8,128)(2,1)S(1)}, bf16[128,2176]{1,0:T(8,128)(2,1)S(1)}, u32[]{:S(2)}, u32[]{:S(2)}) collective-permute-start(bf16[128,2176]{1,0:T(8,128)(2,1)S(1)} %shard_map.87.refs_2_), channel_id=1, source_target_pairs={{0,4},{4,0},{8,12},{12,8},{16,20},{20,16},{24,28},{28,24},{32,36},... | collective-permute-start | bytes 1671176 | tf_op jit(solution)/shard_map/ppermute | solution.py:301
  24.0 10.9 %collective-permute-start.8 = (bf16[128,2176]{1,0:T(8,128)(2,1)S(1)}, bf16[128,2176]{1,0:T(8,128)(2,1)S(1)}, u32[]{:S(2)}, u32[]{:S(2)}) collective-permute-start(bf16[128,2176]{1,0:T(8,128)(2,1)S(1)} %shard_map.88.refs_3_), channel_id=1, source_target_pairs={{0,32},{4,228},{8,40},{12,236},{16,48},{20,244},{24,56},{28,252},{... | collective-permute-start | bytes 1671176 | tf_op jit(solution)/shard_map/ppermute | solution.py:339
  25.4 11.0 %collective-permute-start.16 = (bf16[2,64,2048]{2,1,0:T(8,128)(2,1)S(1)}, bf16[2,64,2048]{2,1,0:T(8,128)(2,1)S(1)}, u32[]{:S(2)}, u32[]{:S(2)}) collective-permute-start(bf16[2,64,2048]{2,1,0:T(8,128)(2,1)S(1)} %get-tuple-element.30), channel_id=1, source_target_pairs={{0,24},{4,12},{8,0},{12,20},{16,8},{20,28},{24,16},{28,4},{32,56},... | collective-permute-start | bytes 1572872 | tf_op jit(solution)/shard_map/ppermute | solution.py:339
  28.3 12.5 %collective-permute-start.3 = (bf16[128,2176]{1,0:T(8,128)(2,1)S(1)}, bf16[128,2176]{1,0:T(8,128)(2,1)S(1)}, u32[]{:S(2)}, u32[]{:S(2)}) collective-permute-start(bf16[128,2176]{1,0:T(8,128)(2,1)S(1)} %collective-permute-done.2.refs_0_.refs_6_), channel_id=1, source_target_pairs={{0,32},{4,228},{8,40},{12,236},{16,48},{20,244},{24,56},{28,252},{... | collective-permute-start | bytes 1671176 | tf_op jit(solution)/shard_map/ppermute | solution.py:339
  34.7 7.9 %collective-permute-start.15 = (bf16[128,2176]{1,0:T(8,128)(2,1)S(1)}, bf16[128,2176]{1,0:T(8,128)(2,1)S(1)}, u32[]{:S(2)}, u32[]{:S(2)}) collective-permute-start(bf16[128,2176]{1,0:T(8,128)(2,1)S(1)} %shard_map.88.refs_3_), channel_id=1, source_target_pairs={{0,4},{4,0},{8,12},{12,8},{16,20},{20,16},{24,28},{28,24},{32,36},... | collective-permute-start | bytes 1671176 | tf_op jit(solution)/shard_map/ppermute | solution.py:301
  35.0 14.6 %collective-permute-start.18 = (bf16[128,2176]{1,0:T(8,128)(2,1)S(1)}, bf16[128,2176]{1,0:T(8,128)(2,1)S(1)}, u32[]{:S(2)}, u32[]{:S(2)}) collective-permute-start(bf16[128,2176]{1,0:T(8,128)(2,1)S(1)} %shard_map.91.refs_1_.refs_7_), channel_id=1, source_target_pairs={{0,32},{4,228},{8,40},{12,236},{16,48},{20,244},{24,56},{28,252},{... | collective-permute-start | bytes 1671176 | tf_op jit(solution)/shard_map/ppermute | solution.py:339
  36.5 13.2 %collective-permute-start.12 = (bf16[128,2176]{1,0:T(8,128)(2,1)S(1)}, bf16[128,2176]{1,0:T(8,128)(2,1)S(1)}, u32[]{:S(2)}, u32[]{:S(2)}) collective-permute-start(bf16[128,2176]{1,0:T(8,128)(2,1)S(1)} %collective-permute-done.2.refs_0_.refs_6_), channel_id=1, source_target_pairs={{0,4},{4,0},{8,12},{12,8},{16,20},{20,16},{24,28},{28,24},{32,36},... | collective-permute-start | bytes 1671176 | tf_op jit(solution)/shard_map/ppermute | solution.py:301
  37.1 12.5 %collective-permute-start.13 = (bf16[128,2176]{1,0:T(8,128)(2,1)S(1)}, bf16[128,2176]{1,0:T(8,128)(2,1)S(1)}, u32[]{:S(2)}, u32[]{:S(2)}) collective-permute-start(bf16[128,2176]{1,0:T(8,128)(2,1)S(1)} %shard_map.91.refs_1_.refs_7_), channel_id=1, source_target_pairs={{0,4},{4,0},{8,12},{12,8},{16,20},{20,16},{24,28},{28,24},{32,36},... | collective-permute-start | bytes 1671176 | tf_op jit(solution)/shard_map/ppermute | solution.py:301
  40.8 11.9 %collective-permute-start.4 = (bf16[128,2176]{1,0:T(8,128)(2,1)S(1)}, bf16[128,2176]{1,0:T(8,128)(2,1)S(1)}, u32[]{:S(2)}, u32[]{:S(2)}) collective-permute-start(bf16[128,2176]{1,0:T(8,128)(2,1)S(1)} %collective-permute-done.3.refs_0_.refs_10_), channel_id=1, source_target_pairs={{0,32},{4,228},{8,40},{12,236},{16,48},{20,244},{24,56},{28,252},{... | collective-permute-start | bytes 1671176 | tf_op jit(solution)/shard_map/ppermute | solution.py:339
  42.6 10.2 %collective-permute-start.19 = (bf16[128,2176]{1,0:T(8,128)(2,1)S(1)}, bf16[128,2176]{1,0:T(8,128)(2,1)S(1)}, u32[]{:S(2)}, u32[]{:S(2)}) collective-permute-start(bf16[128,2176]{1,0:T(8,128)(2,1)S(1)} %collective-permute-done.3.refs_0_.refs_10_), channel_id=1, source_target_pairs={{0,4},{4,0},{8,12},{12,8},{16,20},{20,16},{24,28},{28,24},{32,36},... | collective-permute-start | bytes 1671176 | tf_op jit(solution)/shard_map/ppermute | solution.py:301
  58.7 6.1 %collective-permute-start.22 = (f32[2,32,256]{2,1,0:T(8,128)S(1)}, f32[2,32,256]{2,1,0:T(8,128)S(1)}, u32[]{:S(2)}, u32[]{:S(2)}) collective-permute-start(f32[2,32,256]{2,1,0:T(8,128)S(1)} %get-tuple-element.39), channel_id=1, source_target_pairs={{0,16},{4,20},{8,24},{12,28},{16,0},{20,4},{24,8},{28,12},{32,48},... | collective-permute-start | bytes 196616 | tf_op jit(solution)/shard_map/ppermute | solution.py:301
  67.0 7.0 %collective-permute-start.24 = (bf16[2,32,768]{2,1,0:T(8,128)(2,1)S(1)}, bf16[2,32,768]{2,1,0:T(8,128)(2,1)S(1)}, u32[]{:S(2)}, u32[]{:S(2)}) collective-permute-start(bf16[2,32,768]{2,1,0:T(8,128)(2,1)S(1)} %shard_map.98.refs_0_), channel_id=1, source_target_pairs={{0,1},{1,2},{2,3},{3,0},{4,5},{5,6},{6,7},{7,4},{8,9},{9,10},{10,1... | collective-permute-start | bytes 294920 | tf_op jit(solution)/shard_map/ppermute | solution.py:304
  68.7 6.6 %collective-permute-start.25 = (bf16[2,32,768]{2,1,0:T(8,128)(2,1)S(1)}, bf16[2,32,768]{2,1,0:T(8,128)(2,1)S(1)}, u32[]{:S(2)}, u32[]{:S(2)}) collective-permute-start(bf16[2,32,768]{2,1,0:T(8,128)(2,1)S(1)} %shard_map.98.refs_0_), channel_id=1, source_target_pairs={{0,2},{1,3},{2,0},{3,1},{4,6},{5,7},{6,4},{7,5},{8,10},{9,11},{10,... | collective-permute-start | bytes 294920 | tf_op jit(solution)/shard_map/ppermute | solution.py:304
  81.4 6.2 %collective-permute-start.27 = (f32[2,32,256]{2,1,0:T(8,128)S(1)}, f32[2,32,256]{2,1,0:T(8,128)S(1)}, u32[]{:S(2)}, u32[]{:S(2)}) collective-permute-start(f32[2,32,256]{2,1,0:T(8,128)S(1)} %get-tuple-element.45), channel_id=1, source_target_pairs={{0,24},{4,28},{8,0},{12,4},{16,8},{20,12},{24,16},{28,20},{32,56},... | collective-permute-start | bytes 196616 | tf_op jit(solution)/shard_map/ppermute | solution.py:301
  81.5 6.2 %collective-permute-start.28 = (f32[2,32,256]{2,1,0:T(8,128)S(1)}, f32[2,32,256]{2,1,0:T(8,128)S(1)}, u32[]{:S(2)}, u32[]{:S(2)}) collective-permute-start(f32[2,32,256]{2,1,0:T(8,128)S(1)} %get-tuple-element.46), channel_id=1, source_target_pairs={{0,16},{4,20},{8,24},{12,28},{16,0},{20,4},{24,8},{28,12},{32,48},... | collective-permute-start | bytes 196616 | tf_op jit(solution)/shard_map/ppermute | solution.py:301
  97.0 11.3 %collective-permute-start.30 = (bf16[2,32,2048]{2,1,0:T(8,128)(2,1)S(1)}, bf16[2,32,2048]{2,1,0:T(8,128)(2,1)S(1)}, u32[]{:S(2)}, u32[]{:S(2)}) collective-permute-start(bf16[2,32,2048]{2,1,0:T(8,128)(2,1)S(1)} %get-tuple-element.53), channel_id=1, source_target_pairs={{0,8},{4,12},{8,16},{12,20},{16,24},{20,28},{24,0},{28,4},{32,40},... | collective-permute-start | bytes 786440 | tf_op jit(solution)/shard_map/ppermute | solution.py:301
  99.7 9.6 %collective-permute-start.31 = (bf16[2,32,2048]{2,1,0:T(8,128)(2,1)S(1)}, bf16[2,32,2048]{2,1,0:T(8,128)(2,1)S(1)}, u32[]{:S(2)}, u32[]{:S(2)}) collective-permute-start(bf16[2,32,2048]{2,1,0:T(8,128)(2,1)S(1)} %get-tuple-element.54), channel_id=1, source_target_pairs={{0,16},{4,20},{8,24},{12,28},{16,0},{20,4},{24,8},{28,12},{32,48},... | collective-permute-start | bytes 786440 | tf_op jit(solution)/shard_map/ppermute | solution.py:301
  100.4 11.4 %collective-permute-start.32 = (bf16[2,32,2048]{2,1,0:T(8,128)(2,1)S(1)}, bf16[2,32,2048]{2,1,0:T(8,128)(2,1)S(1)}, u32[]{:S(2)}, u32[]{:S(2)}) collective-permute-start(bf16[2,32,2048]{2,1,0:T(8,128)(2,1)S(1)} %get-tuple-element.55), channel_id=1, source_target_pairs={{0,24},{4,28},{8,0},{12,4},{16,8},{20,12},{24,16},{28,20},{32,56},... | collective-permute-start | bytes 786440 | tf_op jit(solution)/shard_map/ppermute | solution.py:301
  112.4 6.5 %collective-permute-start.34 = (bf16[2,32,512]{2,1,0:T(8,128)(2,1)S(1)}, bf16[2,32,512]{2,1,0:T(8,128)(2,1)S(1)}, u32[]{:S(2)}, u32[]{:S(2)}) collective-permute-start(bf16[2,32,512]{2,1,0:T(8,128)(2,1)S(1)} %get-tuple-element.58), channel_id=1, source_target_pairs={{0,2},{1,3},{2,0},{3,1},{4,6},{5,7},{6,4},{7,5},{8,10},{9,11},{10,... | collective-permute-start | bytes 196616 | tf_op jit(solution)/shard_map/ppermute | solution.py:304
  (17 other events, 184.0 us)
